TPU v7x, 32 devices: a whole 2x2x4 slice. The times are simulated.
32 devices in a mesh: lat: 4 (over y, core), lon: 8 (over z, x).
Axes of the slice: x: 2, y: 2, z: 4, core: 2. Of those that a mesh axis runs over, the one named last changes fastest.
Arguments:
- features: bfloat16 [64, 64, 1024], P(None, 'lat', 'lon'), may hold values from -6 to 6
- labels: int32 [64, 1024], P('lat', 'lon'), may hold values from 0 to 5
- tile_regions: int32 [4, 8, 6], P('lat', 'lon'), may hold values from 0 to 895, as said below
- bank_slot: int32 [896], replicated, may hold values from 0 to 895, as said below
- kernel_bank: bfloat16 [896, 32, 512], P('lon'), may hold values from -0.25 to 0.25
- in_factor: bfloat16 [32, 64], replicated, may hold values from -0.75 to 0.75
- tap_factor: bfloat16 [16, 25], replicated, may hold values from -1.25 to 1.25
- out_factor: bfloat16 [64, 32], replicated, may hold values from -1 to 1
- out_bias: float32 [64], replicated, may hold values from -4 to 4
Outputs:
- mixed: bfloat16 [64, 64, 1024], P(None, 'lat', 'lon')
Inputs may be any that keep to these rules, and one draw needn't show every extreme that they name: `tile_regions`: each tile lists 6 distinct regions: exactly 2 held by the bank device of its own lon index, 2 by that of the next lon index and 2 by that of the previous one (lon indices wrap); within one latitude band the tiles ask each bank device for exactly 4 distinct regions in all. A permutation: region r is bank row bank_slot[r], held by the lon device bank_slot[r] // 112.
All inputs are finite; a program needn't handle non-finite values.
Results may differ from a plain program's by a relative error of at most 0.0056.
Values may be sent and summed in bfloat16 or wider, within the bound.
No kernel may reach another device: no remote copies, remote signals or barrier semaphores. Data moves between devices by JAX's collectives and lax.ppermute only.
A program may use at most 64 MiB of HBM per device.

v0:
```python
import functools

import jax
import jax.numpy as jnp
from jax import lax
from jax.experimental import pallas as pl
from jax.experimental.pallas import tpu as pltpu
from jax.sharding import PartitionSpec as P

KS = 5
REACH = KS // 2
PER_OWNER = 2
LANES = 128
EDGE = 2 * REACH
GROUP = 8
STEP = 2
OUT_COPIES = 4
IN_COPIES = 4
BANK_COPIES = 8
F32 = jnp.float32
BF16 = jnp.bfloat16
VMEM = pl.BlockSpec(memory_space=pltpu.VMEM)
SMEM = pl.BlockSpec(memory_space=pltpu.SMEM)
HBM = pl.BlockSpec(memory_space=pltpu.HBM)
PARAMS = pltpu.CompilerParams(vmem_limit_bytes=24 * 1024 * 1024)


def swap_pairs(count, wrap):
    first = [(i, i ^ 1) for i in range(count)]
    second = [] if wrap else [(0, 0), (count - 1, count - 1)]
    for i in range(1, count if wrap else count - 1, 2):
        second += [(i, (i + 1) % count), ((i + 1) % count, i)]
    return first, second


def in_hbm(array):
    return pltpu.with_memory_space_constraint(array, pltpu.HBM)


def lane_index(shape):
    return lax.broadcasted_iota(jnp.int32, shape, 1)


def start_copies(pairs, sems):
    copies = [pltpu.make_async_copy(source, target, sems.at[i]) for i, (source, target) in enumerate(pairs)]
    for copy in copies:
        copy.start()
    return copies


def in_parts(source, target, count):
    share = target.shape[0] // count
    return tuple((source.at[pl.ds(i * share, share)], target.at[pl.ds(i * share, share)]) for i in range(count))


def find_rows(list_ref, slot_ref, lon_count, held):
    me = lax.axis_index("lon")
    owners = (me, lax.rem(me + lon_count - 1, lon_count), lax.rem(me + 1, lon_count))
    counts = [jnp.int32(0)] * 3
    places = [[jnp.int32(0)] * PER_OWNER for _ in range(3)]
    rows = [[jnp.int32(0)] * PER_OWNER for _ in range(3)]
    for i in range(list_ref.shape[2]):
        slot = slot_ref[list_ref[0, 0, i]]
        for group, owner in enumerate(owners):
            local = slot - owner * held
            hit = (local >= 0) & (local < held)
            for nth in range(PER_OWNER):
                take = hit & (counts[group] == nth)
                places[group][nth] = jnp.where(take, i, places[group][nth])
                rows[group][nth] = jnp.where(take, local, rows[group][nth])
            counts[group] = counts[group] + hit.astype(jnp.int32)
    return places, rows


def reduce_kernel(
    lon_count,
    held,
    list_hbm,
    slot_hbm,
    feat_hbm,
    in_hbm,
    red_ref,
    pay_a_ref,
    pay_b_ref,
    list_ref,
    slot_ref,
    feat_ref,
    in_ref,
    rows_ref,
    sems,
):
    channels, lat_len, lon_len = feat_ref.shape
    rank = in_ref.shape[0]
    pairs = in_parts(feat_hbm, feat_ref, IN_COPIES)
    pairs += ((slot_hbm, slot_ref), (list_hbm, list_ref), (in_hbm, in_ref))
    for copy in start_copies(pairs, sems):
        copy.wait()
    rows_ref[...] = feat_ref[...].astype(F32).reshape(channels * lat_len, lon_len)
    cells = jnp.concatenate(
        [rows_ref[pl.ds(p, channels, stride=lat_len), :].astype(BF16) for p in range(lat_len)], axis=1
    )
    reduced = jnp.dot(in_ref[...], cells, preferred_element_type=F32)
    red_ref[...] = reduced.astype(BF16)
    _, rows = find_rows(list_ref, slot_ref, lon_count, held)
    even = (lax.axis_index("lon") % 2) == 0
    lane = lane_index((rank, LANES))
    pack = jnp.zeros((rank, LANES), F32)
    for p in range(lat_len):
        turned = pltpu.roll(reduced[:, p * lon_len : (p + 1) * lon_len], EDGE * p + REACH, 1)
        pack = jnp.where(lane // EDGE == p, turned, pack)
    for out_ref, wanted in ((pay_a_ref, even), (pay_b_ref, jnp.logical_not(even))):
        load = pack
        for nth in range(PER_OWNER):
            row = jnp.where(wanted, rows[2][nth], rows[1][nth]).astype(F32)
            load = jnp.where(lane == EDGE * lat_len + nth, row, load)
        out_ref[...] = load.astype(BF16)


def prepare_kernel(
    lon_count,
    lat_len,
    red_hbm,
    list_hbm,
    slot_hbm,
    bank_hbm,
    labels_hbm,
    tap_hbm,
    out_factor_hbm,
    bias_hbm,
    bank_ref,
    own_ref,
    position_ref,
    weights_ref,
    mixer_ref,
    offset_ref,
    list_ref,
    slot_ref,
    labels_ref,
    tap_ref,
    out_factor_ref,
    bias_ref,
    sems,
):
    held = bank_hbm.shape[0]
    small = (
        (list_hbm, list_ref),
        (slot_hbm, slot_ref),
        (labels_hbm, labels_ref),
        (tap_hbm, tap_ref),
        (out_factor_hbm, out_factor_ref),
        (bias_hbm, bias_ref),
    )
    copies = start_copies(small + in_parts(bank_hbm, bank_ref, BANK_COPIES), sems)
    for copy in copies[: len(small)]:
        copy.wait()
    places, rows = find_rows(list_ref, slot_ref, lon_count, held)
    even = (lax.axis_index("lon") % 2) == 0
    order = list(places[0])
    order += [jnp.where(even, places[2][nth], places[1][nth]) for nth in range(PER_OWNER)]
    order += [jnp.where(even, places[1][nth], places[2][nth]) for nth in range(PER_OWNER)]
    labels = labels_ref[...]
    position = jnp.zeros(labels.shape, jnp.int32)
    for index, place in enumerate(order):
        position = jnp.where(labels == place, index, position)
    position_ref[...] = position

    rank, out_channels = out_factor_ref.shape
    half = rank // 2
    tap_rank, taps = tap_ref.shape
    shape = (tap_rank * half, taps * half)
    spread = (
        lax.broadcasted_iota(jnp.int32, (shape[0], tap_rank), 0) // half == lane_index((shape[0], tap_rank))
    ).astype(BF16)
    repeat = (
        lax.broadcasted_iota(jnp.int32, (taps, shape[1]), 0) == lane_index((taps, shape[1])) // half
    ).astype(BF16)
    tall = jnp.dot(spread, tap_ref[...], preferred_element_type=F32).astype(BF16)
    wide = jnp.dot(tall, repeat, preferred_element_type=F32)
    same = lax.broadcasted_iota(jnp.int32, shape, 0) % half == lane_index(shape) % half
    weights_ref[...] = jnp.where(same, wide, 0.0).astype(BF16)

    shape = (out_channels * GROUP, rank * GROUP)
    spread = (
        lax.broadcasted_iota(jnp.int32, (shape[0], out_channels), 0) // GROUP
        == lane_index((shape[0], out_channels))
    ).astype(BF16)
    repeat = (
        lax.broadcasted_iota(jnp.int32, (rank, shape[1]), 0) == lane_index((rank, shape[1])) % rank
    ).astype(BF16)
    tall = lax.dot_general(
        spread, out_factor_ref[...], (((1,), (1,)), ((), ())), preferred_element_type=F32
    ).astype(BF16)
    wide = jnp.dot(tall, repeat, preferred_element_type=F32)
    same = lax.broadcasted_iota(jnp.int32, shape, 0) % GROUP == lane_index(shape) // rank
    mixer_ref[...] = jnp.where(same, wide, 0.0).astype(BF16)

    shape = (out_channels * GROUP, out_channels)
    mine = lax.broadcasted_iota(jnp.int32, shape, 0) // GROUP == lane_index(shape)
    offset = jnp.sum(jnp.where(mine, bias_ref[...], 0.0), axis=1, keepdims=True)
    offset_ref[...] = jnp.broadcast_to(offset, offset_ref.shape)
    for copy in copies[len(small) :]:
        copy.wait()
    for nth in range(PER_OWNER):
        own_ref[nth] = bank_ref[rows[0][nth]]


def pick_kernel(lat_len, got_b_ref, got_a_ref, bank_ref, core_b_ref, core_a_ref, edge_ref):
    lane = lane_index((1, LANES))
    for got_ref, core_ref in ((got_b_ref, core_b_ref), (got_a_ref, core_a_ref)):
        head = got_ref[...].astype(F32)[0:1, :]
        for nth in range(PER_OWNER):
            row = jnp.sum(jnp.where(lane == EDGE * lat_len + nth, head, 0.0)).astype(jnp.int32)
            core_ref[nth] = bank_ref[row]
    even = (lax.axis_index("lon") % 2) == 0
    from_prev = lane_index(got_a_ref.shape) % EDGE < REACH
    got_a = got_a_ref[...].astype(F32)
    got_b = got_b_ref[...].astype(F32)
    edge_ref[...] = jnp.where(from_prev == even, got_b, got_a).astype(BF16)


def rows_kernel(lat_len, red_ref, edge_ref, row_a_ref, row_b_ref):
    lon_len = red_ref.shape[1] // lat_len
    even = (lax.axis_index("lat") % 2) == 0
    head = red_ref[:, : REACH * lon_len].astype(F32)
    tail = red_ref[:, (lat_len - REACH) * lon_len :].astype(F32)
    row_a_ref[:, : REACH * lon_len] = jnp.where(even, tail, head).astype(BF16)
    row_b_ref[:, : REACH * lon_len] = jnp.where(even, head, tail).astype(BF16)
    row_a_ref[:, REACH * lon_len :] = edge_ref[...]
    row_b_ref[:, REACH * lon_len :] = edge_ref[...]


def shifted_columns(row, edges, place):
    lane = lane_index(row.shape)
    lon_len = row.shape[1]
    edges = pltpu.roll(edges, (LANES - REACH - EDGE * place) % LANES, 1)
    moved = []
    for col_off in range(KS):
        shift = REACH - col_off
        if shift > 0:
            piece = pltpu.roll(jnp.where(lane >= lon_len - shift, edges, row), shift, 1)
        elif shift < 0:
            piece = pltpu.roll(jnp.where(lane < -shift, edges, row), lon_len + shift, 1)
        else:
            piece = row
        moved.append(piece.astype(BF16))
    return moved


def stack_row(stack_ref, p, moved, slots, lon_len):
    half = moved[0].shape[0] // 2
    for col_off, piece in enumerate(moved):
        for row_off in range(KS):
            slot = slots.get(p + REACH - row_off)
            if slot is not None:
                k = row_off * KS + col_off
                for h in range(2):
                    stack_ref[h, k * half : (k + 1) * half, slot * lon_len : (slot + 1) * lon_len] = piece[
                        h * half : (h + 1) * half
                    ]


def apply_taps(rank, weights_ref, stack_ref, tapped_ref, lon_len):
    half = rank // 2
    tap_rank = tapped_ref.shape[0] // rank
    width = STEP * lon_len
    for start in range(0, tapped_ref.shape[1], width):
        span = slice(start, start + width)
        parts = [
            jnp.dot(weights_ref[...], stack_ref[h, :, span], preferred_element_type=F32)
            .astype(BF16)
            .reshape(tap_rank, 1, half, width)
            for h in range(2)
        ]
        tapped_ref[:, span] = jnp.concatenate(parts, axis=1).reshape(tap_rank * rank, width)


def inner_kernel(lat_len, red_ref, edge_ref, weights_ref, tapped_ref, stack_ref):
    rank = red_ref.shape[0]
    lon_len = red_ref.shape[1] // lat_len
    slots = {p: p - REACH for p in range(REACH, lat_len - REACH)}
    edges = edge_ref[...].astype(F32)
    for p in range(lat_len):
        row = red_ref[:, p * lon_len : (p + 1) * lon_len].astype(F32)
        stack_row(stack_ref, p, shifted_columns(row, edges, p), slots, lon_len)
    apply_taps(rank, weights_ref, stack_ref, tapped_ref, lon_len)


def border_kernel(
    lat_len, lat_count, red_ref, edge_ref, row_a_ref, row_b_ref, weights_ref, tapped_ref, stack_ref
):
    rank = red_ref.shape[0]
    lon_len = red_ref.shape[1] // lat_len
    lat = lax.axis_index("lat")
    even = (lat % 2) == 0
    row_a = row_a_ref[...].astype(F32)
    row_b = row_b_ref[...].astype(F32)
    above = jnp.where(lat == 0, 0.0, jnp.where(even, row_b, row_a))
    below = jnp.where(lat == lat_count - 1, 0.0, jnp.where(even, row_a, row_b))
    slots = {p: p for p in range(REACH)}
    slots.update({lat_len - REACH + p: REACH + p for p in range(REACH)})
    edges = edge_ref[...].astype(F32)
    sources = []
    for p in range(REACH):
        sources.append((p - REACH, above[:, p * lon_len : (p + 1) * lon_len], above, lat_len - REACH + p))
        sources.append((lat_len + p, below[:, p * lon_len : (p + 1) * lon_len], below, p))
    for p in [*range(2 * REACH), *range(lat_len - 2 * REACH, lat_len)]:
        sources.append((p, red_ref[:, p * lon_len : (p + 1) * lon_len].astype(F32), None, p))
    for p, row, holder, place in sources:
        side = edges if holder is None else holder[:, REACH * lon_len :]
        stack_row(stack_ref, p, shifted_columns(row, side, place), slots, lon_len)
    apply_taps(rank, weights_ref, stack_ref, tapped_ref, lon_len)


def mix_kernel(
    inner_ref,
    border_ref,
    core_b_ref,
    core_a_ref,
    own_ref,
    position_ref,
    mixer_ref,
    offset_ref,
    out_hbm,
    stage_ref,
    sems,
):
    lat_len, lon_len = position_ref.shape
    rank = own_ref.shape[1]
    cores = jnp.concatenate(
        [ref[...].reshape(PER_OWNER * rank, -1) for ref in (own_ref, core_a_ref, core_b_ref)], axis=0
    )
    pieces = []
    for start in range(0, lat_len, STEP):
        if start < REACH:
            ref, first = border_ref, start
        elif start < lat_len - REACH:
            ref, first = inner_ref, start - REACH
        else:
            ref, first = border_ref, start - (lat_len - 2 * REACH)
        every = jnp.dot(cores, ref[:, first * lon_len : (first + STEP) * lon_len], preferred_element_type=F32)
        position = jnp.concatenate([position_ref[start + r : start + r + 1, :] for r in range(STEP)], axis=1)
        hidden = jnp.zeros((rank, STEP * lon_len), F32)
        for index in range(3 * PER_OWNER):
            hidden = jnp.where(position == index, every[index * rank : (index + 1) * rank], hidden)
        hidden = hidden.astype(BF16)
        pieces += [hidden[:, r * lon_len : (r + 1) * lon_len] for r in range(STEP)]
    groups = [jnp.concatenate(pieces[g : g + GROUP], axis=0) for g in range(0, lat_len, GROUP)]
    channels = stage_ref.shape[0]
    share = channels // OUT_COPIES
    copies = []
    for part in range(OUT_COPIES):
        span = slice(part * share * GROUP, (part + 1) * share * GROUP)
        blocks = []
        for hidden in groups:
            output = jnp.dot(mixer_ref[span, :], hidden, preferred_element_type=F32) + offset_ref[span, :]
            mixed = output / (1.0 + jnp.exp(-output))
            blocks.append(mixed.reshape(share, GROUP, lon_len))
        held = slice(part * share, (part + 1) * share)
        stage_ref[held] = jnp.concatenate(blocks, axis=1).astype(BF16)
        copy = pltpu.make_async_copy(stage_ref.at[held], out_hbm.at[held], sems.at[part])
        copy.start()
        copies.append(copy)
    for copy in copies:
        copy.wait()


def on_device(
    features, labels, tile_regions, bank_slot, kernel_bank, in_factor, tap_factor, out_factor, out_bias
):
    channels, lat_len, lon_len = features.shape
    rank = in_factor.shape[0]
    held, core_rows, core_cols = kernel_bank.shape
    tap_rank, taps = tap_factor.shape
    out_channels = out_factor.shape[0]
    cells = lat_len * lon_len
    lon_count, lat_count = lax.axis_size("lon"), lax.axis_size("lat")
    lon_first, lon_second = swap_pairs(lon_count, True)
    lat_first, lat_second = swap_pairs(lat_count, False)
    edge_shape = jax.ShapeDtypeStruct((rank, LANES), BF16)
    reduced, pay_a, pay_b = pl.pallas_call(
        functools.partial(reduce_kernel, lon_count, held),
        out_shape=(jax.ShapeDtypeStruct((rank, cells), BF16), edge_shape, edge_shape),
        in_specs=[HBM] * 4,
        out_specs=(VMEM,) * 3,
        scratch_shapes=[
            pltpu.SMEM(tile_regions.shape, jnp.int32),
            pltpu.SMEM(bank_slot.shape, jnp.int32),
            pltpu.VMEM(features.shape, BF16),
            pltpu.VMEM(in_factor.shape, BF16),
            pltpu.VMEM((channels * lat_len, lon_len), F32),
            pltpu.SemaphoreType.DMA((IN_COPIES + 3,)),
        ],
        compiler_params=PARAMS,
    )(*(in_hbm(x) for x in (tile_regions, bank_slot, features, in_factor)))
    got_b = lax.ppermute(pay_b, "lon", lon_second)
    got_a = lax.ppermute(pay_a, "lon", lon_first)
    core_shape = jax.ShapeDtypeStruct((PER_OWNER, core_rows, core_cols), BF16)
    bank, own, position, weights, mixer, offset = pl.pallas_call(
        functools.partial(prepare_kernel, lon_count, lat_len),
        out_shape=(
            jax.ShapeDtypeStruct(kernel_bank.shape, BF16),
            core_shape,
            jax.ShapeDtypeStruct(labels.shape, jnp.int32),
            jax.ShapeDtypeStruct((tap_rank * rank // 2, taps * rank // 2), BF16),
            jax.ShapeDtypeStruct((out_channels * GROUP, rank * GROUP), BF16),
            jax.ShapeDtypeStruct((out_channels * GROUP, lon_len), F32),
        ),
        in_specs=[HBM] * 8,
        out_specs=(VMEM,) * 6,
        scratch_shapes=[
            pltpu.SMEM(tile_regions.shape, jnp.int32),
            pltpu.SMEM(bank_slot.shape, jnp.int32),
            pltpu.VMEM(labels.shape, jnp.int32),
            pltpu.VMEM(tap_factor.shape, BF16),
            pltpu.VMEM(out_factor.shape[::-1], BF16),
            pltpu.VMEM((1, out_channels), F32),
            pltpu.SemaphoreType.DMA((6 + BANK_COPIES,)),
        ],
        compiler_params=PARAMS,
        cost_estimate=pl.CostEstimate(flops=10**6, bytes_accessed=kernel_bank.size * 4, transcendentals=0),
    )(
        reduced,
        *(
            in_hbm(x)
            for x in (
                tile_regions,
                bank_slot,
                kernel_bank,
                labels,
                tap_factor,
                out_factor.T,
                out_bias.reshape(1, -1),
            )
        ),
    )
    row_shape = jax.ShapeDtypeStruct((rank, REACH * lon_len + LANES), BF16)
    core_b, core_a, edges = pl.pallas_call(
        functools.partial(pick_kernel, lat_len),
        out_shape=(core_shape, core_shape, edge_shape),
        in_specs=[VMEM] * 3,
        out_specs=(VMEM,) * 3,
        compiler_params=PARAMS,
    )(got_b, got_a, bank)
    core_b = lax.ppermute(core_b, "lon", lon_second)
    core_a = lax.ppermute(core_a, "lon", lon_first)
    row_a, row_b = pl.pallas_call(
        functools.partial(rows_kernel, lat_len),
        out_shape=(row_shape, row_shape),
        in_specs=[VMEM] * 2,
        out_specs=(VMEM,) * 2,
        compiler_params=PARAMS,
    )(reduced, edges)
    row_a = lax.ppermute(row_a, "lat", lat_first)
    row_b = lax.ppermute(row_b, "lat", lat_second)
    border_cells = 2 * REACH * lon_len
    inner = pl.pallas_call(
        functools.partial(inner_kernel, lat_len),
        out_shape=jax.ShapeDtypeStruct((tap_rank * rank, cells - border_cells), BF16),
        in_specs=[VMEM] * 3,
        out_specs=VMEM,
        scratch_shapes=[pltpu.VMEM((2, taps * rank // 2, cells - border_cells), BF16)],
        compiler_params=PARAMS,
    )(reduced, edges, weights)
    border = pl.pallas_call(
        functools.partial(border_kernel, lat_len, lat_count),
        out_shape=jax.ShapeDtypeStruct((tap_rank * rank, border_cells), BF16),
        in_specs=[VMEM] * 5,
        out_specs=VMEM,
        scratch_shapes=[pltpu.VMEM((2, taps * rank // 2, border_cells), BF16)],
        compiler_params=PARAMS,
    )(reduced, edges, row_a, row_b, weights)
    out_shape = (out_channels, lat_len, lon_len)
    return pl.pallas_call(
        mix_kernel,
        out_shape=jax.ShapeDtypeStruct(out_shape, BF16),
        in_specs=[VMEM] * 8,
        out_specs=HBM,
        scratch_shapes=[pltpu.VMEM(out_shape, BF16), pltpu.SemaphoreType.DMA((OUT_COPIES,))],
        compiler_params=PARAMS,
    )(inner, border, core_b, core_a, own, position, mixer, offset)


def solution(mesh):
    placed = (
        P(None, "lat", "lon"),
        P("lat", "lon"),
        P("lat", "lon", None),
        P(),
        P("lon", None, None),
        P(),
        P(),
        P(),
        P(),
    )
    return jax.shard_map(
        on_device, mesh=mesh, in_specs=placed, out_specs=P(None, "lat", "lon"), check_vma=False
    )
```

profile of v0, /device:TPU:1, one launch (start us, length us, event | category | flops | bytes accessed | tf_op | source)
XLA Modules:
  0.0 21.6 jit_solution(16981183573151629254)
XLA Ops:
  0.0 1.4 %shard_map.91 = (bf16[32,2048]{1,0:T(8,128)(2,1)S(1)}, bf16[32,128]{1,0:T(8,128)(2,1)S(1)}, bf16[32,128]{1,0:T(8,128)(2,1)S(1)}) custom-call(s32[1,1,6]{2,1,0:T(1,128)} %list_hbm.3, s32[896]{0:T(1024)} %slot_hbm.3, bf16[64,16,128]{2,1,0:T(8,128)(2,1)} %feat_hbm.1, bf16[32,64]{1,0:T(8,128)(2,1)} %in_hbm.1), custom_call_target="tpu_custom_call" | custom-call | tf_op jit(solution)/shard_map/pallas_call | solution.py:380
  1.4 5.1 %collective-permute-start = (bf16[32,128]{1,0:T(8,128)(2,1)S(1)}, bf16[32,128]{1,0:T(8,128)(2,1)S(1)}, u32[]{:S(2)}, u32[]{:S(2)}) collective-permute-start(bf16[32,128]{1,0:T(8,128)(2,1)S(1)} %get-tuple-element.20), channel_id=1, source_target_pairs={{1,2},{2,1},{3,4},{4,3},{5,6},{6,5},{7,0},{0,7},{9,10},{10,9},{11,... | collective-permute-start | bytes 24584 | tf_op jit(solution)/shard_map/ppermute | solution.py:395
  6.5 0.0 collective-permute-start.1
  6.6 2.2 %shard_map.92 = (bf16[112,32,512]{2,1,0:T(8,128)(2,1)S(1)}, bf16[2,32,512]{2,1,0:T(8,128)(2,1)S(1)}, s32[16,128]{1,0:T(8,128)S(1)}, bf16[256,400]{1,0:T(8,128)(2...) custom-call(bf16[32,2048]{1,0:T(8,128)(2,1)S(1)} %get-tuple-element.19.red_hbm.red_ref, ...), custom_call_target="tpu_custom_call" | custom-call | flops 1000000 | bytes 7340032 | tf_op jit(solution)/shard_map/pallas_call | solution.py:398
  8.7 0.0 collective-permute-done.got_b_ref
  8.7 0.3 %collective-permute-done.1.got_a_ref = bf16[32,128]{1,0:T(8,128)(2,1)S(1)} collective-permute-done((bf16[32,128]{1,0:T(8,128)(2,1)S(1)}, bf16[32,128]{1,0:T(8,128)(2,1)S(1)}, u32[]{:S(2)}, u32[]{:S(2)}) %collective-permute-start.1) | collective-permute-done | bytes 8224 | tf_op jit(solution)/shard_map/ppermute | solution.py:396
  9.1 0.1 shard_map.93
  9.2 2.8 %collective-permute-start.4 = (bf16[2,32,512]{2,1,0:T(8,128)(2,1)S(1)}, bf16[2,32,512]{2,1,0:T(8,128)(2,1)S(1)}, u32[]{:S(2)}, u32[]{:S(2)}) collective-permute-start(bf16[2,32,512]{2,1,0:T(8,128)(2,1)S(1)} %get-tuple-element.27), channel_id=1, source_target_pairs={{1,2},{2,1},{3,4},{4,3},{5,6},{6,5},{7,0},{0,7},{9,10},{10,9},{11,... | collective-permute-start | bytes 196616 | tf_op jit(solution)/shard_map/ppermute | solution.py:444
  12.0 0.0 collective-permute-start.5
  12.0 2.2 %collective-permute-start.2 = (bf16[32,384]{1,0:T(8,128)(2,1)S(1)}, bf16[32,384]{1,0:T(8,128)(2,1)S(1)}, u32[]{:S(2)}, u32[]{:S(2)}) collective-permute-start(bf16[32,384]{1,0:T(8,128)(2,1)S(1)} %get-tuple-element.25), channel_id=1, source_target_pairs={{0,8},{8,0},{16,24},{24,16},{1,9},{9,1},{17,25},{25,17},{2,10},{10... | collective-permute-start | bytes 73736 | tf_op jit(solution)/shard_map/ppermute | solution.py:453
  14.1 3.0 %collective-permute-start.3 = (bf16[32,384]{1,0:T(8,128)(2,1)S(1)}, bf16[32,384]{1,0:T(8,128)(2,1)S(1)}, u32[]{:S(2)}, u32[]{:S(2)}) collective-permute-start(bf16[32,384]{1,0:T(8,128)(2,1)S(1)} %get-tuple-element.26), channel_id=1, source_target_pairs={{0,0},{24,24},{8,16},{16,8},{1,1},{25,25},{9,17},{17,9},{2,2},{26,... | collective-permute-start | bytes 73736 | tf_op jit(solution)/shard_map/ppermute | solution.py:454
  17.2 1.4 %shard_map.94.inner_ref = bf16[512,1536]{1,0:T(8,128)(2,1)S(1)} custom-call(bf16[32,2048]{1,0:T(8,128)(2,1)S(1)} %get-tuple-element.19.red_hbm.red_ref, bf16[32,128]{1,0:T(8,128)(2,1)S(1)} %get-tuple-element.23.edge_ref, bf16[256,400]{1,0:T(8,128)(2,1)S(1)} %get-tuple-element.24.weights_ref), custom_call_target="tpu_custom_call" | custom-call | tf_op jit(solution)/shard_map/pallas_call | solution.py:456
  18.6 0.0 collective-permute-done.2.row_a_ref
  18.7 0.6 %collective-permute-done.3.row_b_ref = bf16[32,384]{1,0:T(8,128)(2,1)S(1)} collective-permute-done((bf16[32,384]{1,0:T(8,128)(2,1)S(1)}, bf16[32,384]{1,0:T(8,128)(2,1)S(1)}, u32[]{:S(2)}, u32[]{:S(2)}) %collective-permute-start.3) | collective-permute-done | bytes 24608 | tf_op jit(solution)/shard_map/ppermute | solution.py:454
  19.3 0.7 %shard_map.96.border_ref = bf16[512,512]{1,0:T(8,128)(2,1)S(1)} custom-call(bf16[32,2048]{1,0:T(8,128)(2,1)S(1)} %get-tuple-element.19.red_hbm.red_ref, bf16[32,128]{1,0:T(8,128)(2,1)S(1)} %get-tuple-element.23.edge_ref, bf16[32,384]{1,0:T(8,128)(2,1)S(1)} %collective-permute-done.2.row_a_ref, bf16[32,384]{1,0:T(8,128)(2,1)S(1)} %collective-permute-done.3.row_b_ref, ...), custom_call_target="tpu_custom_call" | custom-call | tf_op jit(solution)/shard_map/pallas_call | solution.py:464
  20.0 0.0 collective-permute-done.4.core_b_ref
  20.0 0.0 collective-permute-done.5.core_a_ref
  20.1 1.5 %shard_map.97 = bf16[64,16,128]{2,1,0:T(8,128)(2,1)} custom-call(bf16[512,1536]{1,0:T(8,128)(2,1)S(1)} %shard_map.94.inner_ref, bf16[512,512]{1,0:T(8,128)(2,1)S(1)} %shard_map.96.border_ref, bf16[2,32,512]{2,1,0:T(8,128)(2,1)S(1)} %collective-permute-done.4.core_b_ref, bf16[2,32,512]{2,1,0:T(8,128)(2,1)S(1)} %collective-permute-done.5.core_a_ref, ...), custom_call_target="tpu_custom_call" | custom-call | tf_op jit(solution)/shard_map/pallas_call | solution.py:473
  (1 shorter events, 0.0 us)
Async XLA Ops:
  1.4 7.3 %collective-permute-start = (bf16[32,128]{1,0:T(8,128)(2,1)S(1)}, bf16[32,128]{1,0:T(8,128)(2,1)S(1)}, u32[]{:S(2)}, u32[]{:S(2)}) collective-permute-start(bf16[32,128]{1,0:T(8,128)(2,1)S(1)} %get-tuple-element.20), channel_id=1, source_target_pairs={{1,2},{2,1},{3,4},{4,3},{5,6},{6,5},{7,0},{0,7},{9,10},{10,9},{11,... | collective-permute-start | bytes 24584 | tf_op jit(solution)/shard_map/ppermute | solution.py:395
  6.5 2.5 %collective-permute-start.1 = (bf16[32,128]{1,0:T(8,128)(2,1)S(1)}, bf16[32,128]{1,0:T(8,128)(2,1)S(1)}, u32[]{:S(2)}, u32[]{:S(2)}) collective-permute-start(bf16[32,128]{1,0:T(8,128)(2,1)S(1)} %get-tuple-element.21), channel_id=1, source_target_pairs={{0,1},{1,0},{2,3},{3,2},{4,5},{5,4},{6,7},{7,6},{8,9},{9,8},{10,11... | collective-permute-start | bytes 24584 | tf_op jit(solution)/shard_map/ppermute | solution.py:396
  9.2 10.8 %collective-permute-start.4 = (bf16[2,32,512]{2,1,0:T(8,128)(2,1)S(1)}, bf16[2,32,512]{2,1,0:T(8,128)(2,1)S(1)}, u32[]{:S(2)}, u32[]{:S(2)}) collective-permute-start(bf16[2,32,512]{2,1,0:T(8,128)(2,1)S(1)} %get-tuple-element.27), channel_id=1, source_target_pairs={{1,2},{2,1},{3,4},{4,3},{5,6},{6,5},{7,0},{0,7},{9,10},{10,9},{11,... | collective-permute-start | bytes 196616 | tf_op jit(solution)/shard_map/ppermute | solution.py:444
  12.0 8.1 %collective-permute-start.5 = (bf16[2,32,512]{2,1,0:T(8,128)(2,1)S(1)}, bf16[2,32,512]{2,1,0:T(8,128)(2,1)S(1)}, u32[]{:S(2)}, u32[]{:S(2)}) collective-permute-start(bf16[2,32,512]{2,1,0:T(8,128)(2,1)S(1)} %get-tuple-element.28), channel_id=1, source_target_pairs={{0,1},{1,0},{2,3},{3,2},{4,5},{5,4},{6,7},{7,6},{8,9},{9,8},{10,11... | collective-permute-start | bytes 196616 | tf_op jit(solution)/shard_map/ppermute | solution.py:445
  12.0 6.7 %collective-permute-start.2 = (bf16[32,384]{1,0:T(8,128)(2,1)S(1)}, bf16[32,384]{1,0:T(8,128)(2,1)S(1)}, u32[]{:S(2)}, u32[]{:S(2)}) collective-permute-start(bf16[32,384]{1,0:T(8,128)(2,1)S(1)} %get-tuple-element.25), channel_id=1, source_target_pairs={{0,8},{8,0},{16,24},{24,16},{1,9},{9,1},{17,25},{25,17},{2,10},{10... | collective-permute-start | bytes 73736 | tf_op jit(solution)/shard_map/ppermute | solution.py:453
  14.1 5.1 %collective-permute-start.3 = (bf16[32,384]{1,0:T(8,128)(2,1)S(1)}, bf16[32,384]{1,0:T(8,128)(2,1)S(1)}, u32[]{:S(2)}, u32[]{:S(2)}) collective-permute-start(bf16[32,384]{1,0:T(8,128)(2,1)S(1)} %get-tuple-element.26), channel_id=1, source_target_pairs={{0,0},{24,24},{8,16},{16,8},{1,1},{25,25},{9,17},{17,9},{2,2},{26,... | collective-permute-start | bytes 73736 | tf_op jit(solution)/shard_map/ppermute | solution.py:454
where the time goes:
time: 21.8 us; the launch traced here: 21.6 us
  starting transfers between devices  13.1 us (60%)
  Pallas kernels  7.45 us (34%)
  waiting for transfers between devices  0.93 us (4%)
    ppermute x1, starting transfers between devices, on_device(): got_b = lax.ppermute(pay_b, 'lon', lon_second)  5.14 us
    ppermute x1, starting transfers between devices, on_device(): row_b = lax.ppermute(row_b, 'lat', lat_second)  3.05 us
    ppermute x1, starting transfers between devices, on_device(): core_b = lax.ppermute(core_b, 'lon', lon_second)  2.77 us
    pallas_call x1, Pallas kernels, on_device(): pl.pallas_call(functools.partial(prepare_kernel, lon_count, lat_len), out...  2.18 us
    ppermute x1, starting transfers between devices, on_device(): row_a = lax.ppermute(row_a, 'lat', lat_first)  2.17 us
    pallas_call x1, Pallas kernels, on_device(): pl.pallas_call(mix_kernel, out_shape=jax.ShapeDtypeStruct(out_shape, BF16...  1.55 us
    pallas_call x1, Pallas kernels, on_device(): pl.pallas_call(functools.partial(inner_kernel, lat_len), out_shape=jax.Sh...  1.44 us
    pallas_call x1, Pallas kernels, on_device(): pl.pallas_call(functools.partial(reduce_kernel, lon_count, held), out_sha...  1.4 us
  transfers between devices with their start and end apart: 6, of which 2 were waited for; matrix products, arithmetic and copies ran while one was open for 0% of the time, Pallas kernels for 20%

commit v1 on v0

--- a/solution.py
+++ b/solution.py
@@ -25,11 +25,9 @@
 PARAMS = pltpu.CompilerParams(vmem_limit_bytes=24 * 1024 * 1024)
 
 
-def swap_pairs(count, wrap):
+def swap_pairs(count):
     first = [(i, i ^ 1) for i in range(count)]
-    second = [] if wrap else [(0, 0), (count - 1, count - 1)]
-    for i in range(1, count if wrap else count - 1, 2):
-        second += [(i, (i + 1) % count), ((i + 1) % count, i)]
+    second = [(i, (i + 1 if i % 2 else i - 1) % count) for i in range(count)]
     return first, second
 
 
@@ -374,8 +372,8 @@
     out_channels = out_factor.shape[0]
     cells = lat_len * lon_len
     lon_count, lat_count = lax.axis_size("lon"), lax.axis_size("lat")
-    lon_first, lon_second = swap_pairs(lon_count, True)
-    lat_first, lat_second = swap_pairs(lat_count, False)
+    lon_first, lon_second = swap_pairs(lon_count)
+    lat_first, lat_second = swap_pairs(lat_count)
     edge_shape = jax.ShapeDtypeStruct((rank, LANES), BF16)
     reduced, pay_a, pay_b = pl.pallas_call(
         functools.partial(reduce_kernel, lon_count, held),

time: 21.8 us -> 20.7 us (0.950)
  the two profiles are of different devices: /device:TPU:1 before, /device:TPU:0 now
where the time goes in v1:
time: 20.7 us; the launch traced here: 20.5 us
  starting transfers between devices  10.5 us (51%)
  Pallas kernels  7.45 us (36%)
  waiting for transfers between devices  2.47 us (12%)
    ppermute x1, starting transfers between devices, on_device(): got_b = lax.ppermute(pay_b, 'lon', lon_second)  6.04 us
    ppermute x1, starting transfers between devices, on_device(): core_b = lax.ppermute(core_b, 'lon', lon_second)  2.77 us
    pallas_call x1, Pallas kernels, on_device(): pl.pallas_call(functools.partial(prepare_kernel, lon_count, lat_len), out...  2.18 us
    ppermute x1, starting transfers between devices, on_device(): row_b = lax.ppermute(row_b, 'lat', lat_second)  1.63 us
    pallas_call x1, Pallas kernels, on_device(): pl.pallas_call(mix_kernel, out_shape=jax.ShapeDtypeStruct(out_shape, BF16...  1.54 us
    ppermute x1, waiting for transfers between devices, on_device(): got_a = lax.ppermute(pay_a, 'lon', lon_first)  1.45 us
    pallas_call x1, Pallas kernels, on_device(): pl.pallas_call(functools.partial(inner_kernel, lat_len), out_shape=jax.Sh...  1.44 us
    pallas_call x1, Pallas kernels, on_device(): pl.pallas_call(functools.partial(reduce_kernel, lon_count, held), out_sha...  1.4 us
  transfers between devices with their start and end apart: 6, of which 4 were waited for; matrix products, arithmetic and copies ran while one was open for 0% of the time, Pallas kernels for 21%

profile of v1, /device:TPU:0, one launch (start us, length us, event | category | flops | bytes accessed | tf_op | source)
XLA Modules:
  0.0 20.5 jit_solution(14254757157964142104)
XLA Ops:
  0.0 1.4 %shard_map.91 = (bf16[32,2048]{1,0:T(8,128)(2,1)S(1)}, bf16[32,128]{1,0:T(8,128)(2,1)S(1)}, bf16[32,128]{1,0:T(8,128)(2,1)S(1)}) custom-call(s32[1,1,6]{2,1,0:T(1,128)} %list_hbm.3, s32[896]{0:T(1024)} %slot_hbm.3, bf16[64,16,128]{2,1,0:T(8,128)(2,1)} %feat_hbm.1, bf16[32,64]{1,0:T(8,128)(2,1)} %in_hbm.1), custom_call_target="tpu_custom_call" | custom-call | tf_op jit(solution)/shard_map/pallas_call | solution.py:378
  1.4 6.0 %collective-permute-start = (bf16[32,128]{1,0:T(8,128)(2,1)S(1)}, bf16[32,128]{1,0:T(8,128)(2,1)S(1)}, u32[]{:S(2)}, u32[]{:S(2)}) collective-permute-start(bf16[32,128]{1,0:T(8,128)(2,1)S(1)} %get-tuple-element.20), channel_id=1, source_target_pairs={{0,7},{1,2},{2,1},{3,4},{4,3},{5,6},{6,5},{7,0},{8,15},{9,10},{10,... | collective-permute-start | bytes 24584 | tf_op jit(solution)/shard_map/ppermute | solution.py:393
  7.4 0.0 collective-permute-start.1
  7.5 2.2 %shard_map.92 = (bf16[112,32,512]{2,1,0:T(8,128)(2,1)S(1)}, bf16[2,32,512]{2,1,0:T(8,128)(2,1)S(1)}, s32[16,128]{1,0:T(8,128)S(1)}, bf16[256,400]{1,0:T(8,128)(2...) custom-call(bf16[32,2048]{1,0:T(8,128)(2,1)S(1)} %get-tuple-element.19.red_hbm.red_ref, ...), custom_call_target="tpu_custom_call" | custom-call | flops 1000000 | bytes 7340032 | tf_op jit(solution)/shard_map/pallas_call | solution.py:396
  9.6 0.0 collective-permute-done.got_b_ref
  9.6 1.5 %collective-permute-done.1.got_a_ref = bf16[32,128]{1,0:T(8,128)(2,1)S(1)} collective-permute-done((bf16[32,128]{1,0:T(8,128)(2,1)S(1)}, bf16[32,128]{1,0:T(8,128)(2,1)S(1)}, u32[]{:S(2)}, u32[]{:S(2)}) %collective-permute-start.1) | collective-permute-done | bytes 8224 | tf_op jit(solution)/shard_map/ppermute | solution.py:394
  11.1 0.1 shard_map.93
  11.2 2.8 %collective-permute-start.4 = (bf16[2,32,512]{2,1,0:T(8,128)(2,1)S(1)}, bf16[2,32,512]{2,1,0:T(8,128)(2,1)S(1)}, u32[]{:S(2)}, u32[]{:S(2)}) collective-permute-start(bf16[2,32,512]{2,1,0:T(8,128)(2,1)S(1)} %get-tuple-element.27), channel_id=1, source_target_pairs={{0,7},{1,2},{2,1},{3,4},{4,3},{5,6},{6,5},{7,0},{8,15},{9,10},{10,... | collective-permute-start | bytes 196616 | tf_op jit(solution)/shard_map/ppermute | solution.py:442
  14.0 0.0 collective-permute-start.5
  14.0 0.1 collective-permute-start.2
  14.1 1.6 %collective-permute-start.3 = (bf16[32,384]{1,0:T(8,128)(2,1)S(1)}, bf16[32,384]{1,0:T(8,128)(2,1)S(1)}, u32[]{:S(2)}, u32[]{:S(2)}) collective-permute-start(bf16[32,384]{1,0:T(8,128)(2,1)S(1)} %get-tuple-element.26), channel_id=1, source_target_pairs={{0,24},{8,16},{16,8},{24,0},{1,25},{9,17},{17,9},{25,1},{2,26},{10... | collective-permute-start | bytes 73736 | tf_op jit(solution)/shard_map/ppermute | solution.py:452
  15.7 1.4 %shard_map.94.inner_ref = bf16[512,1536]{1,0:T(8,128)(2,1)S(1)} custom-call(bf16[32,2048]{1,0:T(8,128)(2,1)S(1)} %get-tuple-element.19.red_hbm.red_ref, bf16[32,128]{1,0:T(8,128)(2,1)S(1)} %get-tuple-element.23.edge_ref, bf16[256,400]{1,0:T(8,128)(2,1)S(1)} %get-tuple-element.24.weights_ref), custom_call_target="tpu_custom_call" | custom-call | tf_op jit(solution)/shard_map/pallas_call | solution.py:454
  17.2 0.0 collective-permute-done.2.row_a_ref
  17.2 0.2 %collective-permute-done.3.row_b_ref = bf16[32,384]{1,0:T(8,128)(2,1)S(1)} collective-permute-done((bf16[32,384]{1,0:T(8,128)(2,1)S(1)}, bf16[32,384]{1,0:T(8,128)(2,1)S(1)}, u32[]{:S(2)}, u32[]{:S(2)}) %collective-permute-start.3) | collective-permute-done | bytes 24608 | tf_op jit(solution)/shard_map/ppermute | solution.py:452
  17.4 0.7 %shard_map.96.border_ref = bf16[512,512]{1,0:T(8,128)(2,1)S(1)} custom-call(bf16[32,2048]{1,0:T(8,128)(2,1)S(1)} %get-tuple-element.19.red_hbm.red_ref, bf16[32,128]{1,0:T(8,128)(2,1)S(1)} %get-tuple-element.23.edge_ref, bf16[32,384]{1,0:T(8,128)(2,1)S(1)} %collective-permute-done.2.row_a_ref, bf16[32,384]{1,0:T(8,128)(2,1)S(1)} %collective-permute-done.3.row_b_ref, ...), custom_call_target="tpu_custom_call" | custom-call | tf_op jit(solution)/shard_map/pallas_call | solution.py:462
  18.2 0.2 collective-permute-done.4.core_b_ref
  18.3 0.6 %collective-permute-done.5.core_a_ref = bf16[2,32,512]{2,1,0:T(8,128)(2,1)S(1)} collective-permute-done((bf16[2,32,512]{2,1,0:T(8,128)(2,1)S(1)}, bf16[2,32,512]{2,1,0:T(8,128)(2,1)S(1)}, u32[]{:S(2)}, u32[]{:S(2)}) %collective-permute-start.5) | collective-permute-done | bytes 65568 | tf_op jit(solution)/shard_map/ppermute | solution.py:443
  19.0 1.5 %shard_map.97 = bf16[64,16,128]{2,1,0:T(8,128)(2,1)} custom-call(bf16[512,1536]{1,0:T(8,128)(2,1)S(1)} %shard_map.94.inner_ref, bf16[512,512]{1,0:T(8,128)(2,1)S(1)} %shard_map.96.border_ref, bf16[2,32,512]{2,1,0:T(8,128)(2,1)S(1)} %collective-permute-done.4.core_b_ref, bf16[2,32,512]{2,1,0:T(8,128)(2,1)S(1)} %collective-permute-done.5.core_a_ref, ...), custom_call_target="tpu_custom_call" | custom-call | tf_op jit(solution)/shard_map/pallas_call | solution.py:471
  (1 shorter events, 0.0 us)
Async XLA Ops:
  1.4 8.2 %collective-permute-start = (bf16[32,128]{1,0:T(8,128)(2,1)S(1)}, bf16[32,128]{1,0:T(8,128)(2,1)S(1)}, u32[]{:S(2)}, u32[]{:S(2)}) collective-permute-start(bf16[32,128]{1,0:T(8,128)(2,1)S(1)} %get-tuple-element.20), channel_id=1, source_target_pairs={{0,7},{1,2},{2,1},{3,4},{4,3},{5,6},{6,5},{7,0},{8,15},{9,10},{10,... | collective-permute-start | bytes 24584 | tf_op jit(solution)/shard_map/ppermute | solution.py:393
  7.4 3.7 %collective-permute-start.1 = (bf16[32,128]{1,0:T(8,128)(2,1)S(1)}, bf16[32,128]{1,0:T(8,128)(2,1)S(1)}, u32[]{:S(2)}, u32[]{:S(2)}) collective-permute-start(bf16[32,128]{1,0:T(8,128)(2,1)S(1)} %get-tuple-element.21), channel_id=1, source_target_pairs={{0,1},{1,0},{2,3},{3,2},{4,5},{5,4},{6,7},{7,6},{8,9},{9,8},{10,11... | collective-permute-start | bytes 24584 | tf_op jit(solution)/shard_map/ppermute | solution.py:394
  11.2 7.1 %collective-permute-start.4 = (bf16[2,32,512]{2,1,0:T(8,128)(2,1)S(1)}, bf16[2,32,512]{2,1,0:T(8,128)(2,1)S(1)}, u32[]{:S(2)}, u32[]{:S(2)}) collective-permute-start(bf16[2,32,512]{2,1,0:T(8,128)(2,1)S(1)} %get-tuple-element.27), channel_id=1, source_target_pairs={{0,7},{1,2},{2,1},{3,4},{4,3},{5,6},{6,5},{7,0},{8,15},{9,10},{10,... | collective-permute-start | bytes 196616 | tf_op jit(solution)/shard_map/ppermute | solution.py:442
  14.0 5.0 %collective-permute-start.5 = (bf16[2,32,512]{2,1,0:T(8,128)(2,1)S(1)}, bf16[2,32,512]{2,1,0:T(8,128)(2,1)S(1)}, u32[]{:S(2)}, u32[]{:S(2)}) collective-permute-start(bf16[2,32,512]{2,1,0:T(8,128)(2,1)S(1)} %get-tuple-element.28), channel_id=1, source_target_pairs={{0,1},{1,0},{2,3},{3,2},{4,5},{5,4},{6,7},{7,6},{8,9},{9,8},{10,11... | collective-permute-start | bytes 196616 | tf_op jit(solution)/shard_map/ppermute | solution.py:443
  14.0 3.2 %collective-permute-start.2 = (bf16[32,384]{1,0:T(8,128)(2,1)S(1)}, bf16[32,384]{1,0:T(8,128)(2,1)S(1)}, u32[]{:S(2)}, u32[]{:S(2)}) collective-permute-start(bf16[32,384]{1,0:T(8,128)(2,1)S(1)} %get-tuple-element.25), channel_id=1, source_target_pairs={{0,8},{8,0},{16,24},{24,16},{1,9},{9,1},{17,25},{25,17},{2,10},{10... | collective-permute-start | bytes 73736 | tf_op jit(solution)/shard_map/ppermute | solution.py:451
  14.1 3.3 %collective-permute-start.3 = (bf16[32,384]{1,0:T(8,128)(2,1)S(1)}, bf16[32,384]{1,0:T(8,128)(2,1)S(1)}, u32[]{:S(2)}, u32[]{:S(2)}) collective-permute-start(bf16[32,384]{1,0:T(8,128)(2,1)S(1)} %get-tuple-element.26), channel_id=1, source_target_pairs={{0,24},{8,16},{16,8},{24,0},{1,25},{9,17},{17,9},{25,1},{2,26},{10... | collective-permute-start | bytes 73736 | tf_op jit(solution)/shard_map/ppermute | solution.py:452

commit v2 on v1

--- a/solution.py
+++ b/solution.py
@@ -70,21 +70,20 @@
     return places, rows
 
 
-def reduce_kernel(
+def edge_kernel(
     lon_count,
     held,
     list_hbm,
     slot_hbm,
     feat_hbm,
     in_hbm,
-    red_ref,
     pay_a_ref,
     pay_b_ref,
     list_ref,
     slot_ref,
     feat_ref,
     in_ref,
-    rows_ref,
+    turned_ref,
     sems,
 ):
     channels, lat_len, lon_len = feat_ref.shape
@@ -93,21 +92,24 @@
     pairs += ((slot_hbm, slot_ref), (list_hbm, list_ref), (in_hbm, in_ref))
     for copy in start_copies(pairs, sems):
         copy.wait()
-    rows_ref[...] = feat_ref[...].astype(F32).reshape(channels * lat_len, lon_len)
-    cells = jnp.concatenate(
-        [rows_ref[pl.ds(p, channels, stride=lat_len), :].astype(BF16) for p in range(lat_len)], axis=1
-    )
-    reduced = jnp.dot(in_ref[...], cells, preferred_element_type=F32)
-    red_ref[...] = reduced.astype(BF16)
+    lane = lane_index((lat_len, LANES))
+    batch = LANES // EDGE
+    for first in range(0, channels, batch):
+        packed = jnp.zeros((lat_len, LANES), F32)
+        for c in range(batch):
+            moved = pltpu.roll(feat_ref[first + c].astype(F32), (EDGE * c + REACH) % LANES, 1)
+            packed = jnp.where(lane // EDGE == c, moved, packed)
+        turned_ref[first * EDGE : (first + batch) * EDGE, :] = jnp.transpose(packed)
+    columns = jnp.concatenate(
+        [turned_ref[pl.ds(j, channels, stride=EDGE), :].astype(BF16) for j in range(EDGE)], axis=1
+    )
+    edges = jnp.dot(in_ref[...], columns, preferred_element_type=F32)
+    edges = jnp.concatenate([edges, jnp.zeros((rank, LANES - EDGE * lat_len), F32)], axis=1)
     _, rows = find_rows(list_ref, slot_ref, lon_count, held)
     even = (lax.axis_index("lon") % 2) == 0
     lane = lane_index((rank, LANES))
-    pack = jnp.zeros((rank, LANES), F32)
-    for p in range(lat_len):
-        turned = pltpu.roll(reduced[:, p * lon_len : (p + 1) * lon_len], EDGE * p + REACH, 1)
-        pack = jnp.where(lane // EDGE == p, turned, pack)
     for out_ref, wanted in ((pay_a_ref, even), (pay_b_ref, jnp.logical_not(even))):
-        load = pack
+        load = edges
         for nth in range(PER_OWNER):
             row = jnp.where(wanted, rows[2][nth], rows[1][nth]).astype(F32)
             load = jnp.where(lane == EDGE * lat_len + nth, row, load)
@@ -117,14 +119,17 @@
 def prepare_kernel(
     lon_count,
     lat_len,
-    red_hbm,
+    pay_hbm,
     list_hbm,
     slot_hbm,
+    feat_hbm,
+    in_hbm,
     bank_hbm,
     labels_hbm,
     tap_hbm,
     out_factor_hbm,
     bias_hbm,
+    red_ref,
     bank_ref,
     own_ref,
     position_ref,
@@ -137,6 +142,9 @@
     tap_ref,
     out_factor_ref,
     bias_ref,
+    feat_ref,
+    in_ref,
+    rows_ref,
     sems,
 ):
     held = bank_hbm.shape[0]
@@ -147,10 +155,18 @@
         (tap_hbm, tap_ref),
         (out_factor_hbm, out_factor_ref),
         (bias_hbm, bias_ref),
+        (in_hbm, in_ref),
+        (feat_hbm, feat_ref),
     )
     copies = start_copies(small + in_parts(bank_hbm, bank_ref, BANK_COPIES), sems)
     for copy in copies[: len(small)]:
         copy.wait()
+    channels, lon_len = feat_ref.shape[0], feat_ref.shape[2]
+    rows_ref[...] = feat_ref[...].astype(F32).reshape(channels * lat_len, lon_len)
+    cells = jnp.concatenate(
+        [rows_ref[pl.ds(p, channels, stride=lat_len), :].astype(BF16) for p in range(lat_len)], axis=1
+    )
+    red_ref[...] = jnp.dot(in_ref[...], cells, preferred_element_type=F32).astype(BF16)
     places, rows = find_rows(list_ref, slot_ref, lon_count, held)
     even = (lax.axis_index("lon") % 2) == 0
     order = list(places[0])
@@ -202,29 +218,32 @@
         own_ref[nth] = bank_ref[rows[0][nth]]
 
 
-def pick_kernel(lat_len, got_b_ref, got_a_ref, bank_ref, core_b_ref, core_a_ref, edge_ref):
+def pick_kernel(lat_len, got_b_ref, got_a_ref, bank_ref, core_b_ref, core_a_ref):
     lane = lane_index((1, LANES))
     for got_ref, core_ref in ((got_b_ref, core_b_ref), (got_a_ref, core_a_ref)):
         head = got_ref[...].astype(F32)[0:1, :]
         for nth in range(PER_OWNER):
             row = jnp.sum(jnp.where(lane == EDGE * lat_len + nth, head, 0.0)).astype(jnp.int32)
             core_ref[nth] = bank_ref[row]
+
+
+def rows_kernel(lat_len, got_b_ref, got_a_ref, core_ref, red_ref, edge_ref, row_a_ref, row_b_ref):
+    lon_len = red_ref.shape[1] // lat_len
     even = (lax.axis_index("lon") % 2) == 0
-    from_prev = lane_index(got_a_ref.shape) % EDGE < REACH
-    got_a = got_a_ref[...].astype(F32)
-    got_b = got_b_ref[...].astype(F32)
-    edge_ref[...] = jnp.where(from_prev == even, got_b, got_a).astype(BF16)
-
-
-def rows_kernel(lat_len, red_ref, edge_ref, row_a_ref, row_b_ref):
-    lon_len = red_ref.shape[1] // lat_len
+    from_prev = lane_index(got_a_ref.shape) < REACH * lat_len
+    got = jnp.where(from_prev == even, got_b_ref[...].astype(F32), got_a_ref[...].astype(F32)).astype(BF16)
+    source = lax.broadcasted_iota(jnp.int32, (LANES, LANES), 0)
+    target = lane_index((LANES, LANES))
+    order = (source == (target % EDGE) * lat_len + target // EDGE) & (target < EDGE * lat_len)
+    edges = jnp.dot(got, order.astype(BF16), preferred_element_type=F32).astype(BF16)
+    edge_ref[...] = edges
     even = (lax.axis_index("lat") % 2) == 0
     head = red_ref[:, : REACH * lon_len].astype(F32)
     tail = red_ref[:, (lat_len - REACH) * lon_len :].astype(F32)
     row_a_ref[:, : REACH * lon_len] = jnp.where(even, tail, head).astype(BF16)
     row_b_ref[:, : REACH * lon_len] = jnp.where(even, head, tail).astype(BF16)
-    row_a_ref[:, REACH * lon_len :] = edge_ref[...]
-    row_b_ref[:, REACH * lon_len :] = edge_ref[...]
+    row_a_ref[:, REACH * lon_len :] = edges
+    row_b_ref[:, REACH * lon_len :] = edges
 
 
 def shifted_columns(row, edges, place):
@@ -257,56 +276,74 @@
                     ]
 
 
-def apply_taps(rank, weights_ref, stack_ref, tapped_ref, lon_len):
+def apply_taps(rank, weights_ref, stacked, tapped_ref, lon_len):
     half = rank // 2
     tap_rank = tapped_ref.shape[0] // rank
     width = STEP * lon_len
     for start in range(0, tapped_ref.shape[1], width):
-        span = slice(start, start + width)
         parts = [
-            jnp.dot(weights_ref[...], stack_ref[h, :, span], preferred_element_type=F32)
+            jnp.dot(weights_ref[...], stacked(h, start, width), preferred_element_type=F32)
             .astype(BF16)
             .reshape(tap_rank, 1, half, width)
             for h in range(2)
         ]
-        tapped_ref[:, span] = jnp.concatenate(parts, axis=1).reshape(tap_rank * rank, width)
-
-
-def inner_kernel(lat_len, red_ref, edge_ref, weights_ref, tapped_ref, stack_ref):
+        tapped_ref[:, start : start + width] = jnp.concatenate(parts, axis=1).reshape(tap_rank * rank, width)
+
+
+def border_slots(lat_len):
+    slots = {p: p for p in range(REACH)}
+    slots.update({lat_len - REACH + p: REACH + p for p in range(REACH)})
+    return slots
+
+
+def inner_kernel(lat_len, red_ref, edge_ref, weights_ref, tapped_ref, halo_stack_ref, stack_ref):
     rank = red_ref.shape[0]
     lon_len = red_ref.shape[1] // lat_len
     slots = {p: p - REACH for p in range(REACH, lat_len - REACH)}
     edges = edge_ref[...].astype(F32)
     for p in range(lat_len):
         row = red_ref[:, p * lon_len : (p + 1) * lon_len].astype(F32)
-        stack_row(stack_ref, p, shifted_columns(row, edges, p), slots, lon_len)
-    apply_taps(rank, weights_ref, stack_ref, tapped_ref, lon_len)
-
-
-def border_kernel(
-    lat_len, lat_count, red_ref, edge_ref, row_a_ref, row_b_ref, weights_ref, tapped_ref, stack_ref
-):
-    rank = red_ref.shape[0]
-    lon_len = red_ref.shape[1] // lat_len
+        moved = shifted_columns(row, edges, p)
+        stack_row(stack_ref, p, moved, slots, lon_len)
+        stack_row(halo_stack_ref, p, moved, border_slots(lat_len), lon_len)
+    apply_taps(rank, weights_ref, lambda h, start, width: stack_ref[h, :, start : start + width], tapped_ref, lon_len)
+
+
+def border_kernel(lat_len, lat_count, row_a_ref, row_b_ref, weights_ref, own_stack_ref, tapped_ref, stack_ref):
+    rank = row_a_ref.shape[0]
+    lon_len = (row_a_ref.shape[1] - LANES) // REACH
     lat = lax.axis_index("lat")
     even = (lat % 2) == 0
     row_a = row_a_ref[...].astype(F32)
     row_b = row_b_ref[...].astype(F32)
     above = jnp.where(lat == 0, 0.0, jnp.where(even, row_b, row_a))
     below = jnp.where(lat == lat_count - 1, 0.0, jnp.where(even, row_a, row_b))
-    slots = {p: p for p in range(REACH)}
-    slots.update({lat_len - REACH + p: REACH + p for p in range(REACH)})
-    edges = edge_ref[...].astype(F32)
-    sources = []
-    for p in range(REACH):
-        sources.append((p - REACH, above[:, p * lon_len : (p + 1) * lon_len], above, lat_len - REACH + p))
-        sources.append((lat_len + p, below[:, p * lon_len : (p + 1) * lon_len], below, p))
-    for p in [*range(2 * REACH), *range(lat_len - 2 * REACH, lat_len)]:
-        sources.append((p, red_ref[:, p * lon_len : (p + 1) * lon_len].astype(F32), None, p))
-    for p, row, holder, place in sources:
-        side = edges if holder is None else holder[:, REACH * lon_len :]
-        stack_row(stack_ref, p, shifted_columns(row, side, place), slots, lon_len)
-    apply_taps(rank, weights_ref, stack_ref, tapped_ref, lon_len)
+    slots = border_slots(lat_len)
+    for i in range(REACH):
+        for p, holder, place in ((i - REACH, above, lat_len - REACH + i), (lat_len + i, below, i)):
+            row = holder[:, i * lon_len : (i + 1) * lon_len]
+            moved = shifted_columns(row, holder[:, REACH * lon_len :], place)
+            stack_row(stack_ref, p, moved, slots, lon_len)
+    block = KS * rank // 2
+    in_halo = {
+        (slot, row_off)
+        for p, slot in slots.items()
+        for row_off in range(KS)
+        if not 0 <= p + row_off - REACH < lat_len
+    }
+
+    def stacked(h, start, width):
+        columns = []
+        for slot in range(start // lon_len, (start + width) // lon_len):
+            span = slice(slot * lon_len, (slot + 1) * lon_len)
+            pieces = []
+            for row_off in range(KS):
+                ref = stack_ref if (slot, row_off) in in_halo else own_stack_ref
+                pieces.append(ref[h, row_off * block : (row_off + 1) * block, span])
+            columns.append(jnp.concatenate(pieces, axis=0))
+        return jnp.concatenate(columns, axis=1)
+
+    apply_taps(rank, weights_ref, stacked, tapped_ref, lon_len)
 
 
 def mix_kernel(
@@ -351,7 +388,7 @@
         blocks = []
         for hidden in groups:
             output = jnp.dot(mixer_ref[span, :], hidden, preferred_element_type=F32) + offset_ref[span, :]
-            mixed = output / (1.0 + jnp.exp(-output))
+            mixed = 0.5 * output * (1.0 + jnp.tanh(0.5 * output))
             blocks.append(mixed.reshape(share, GROUP, lon_len))
         held = slice(part * share, (part + 1) * share)
         stage_ref[held] = jnp.concatenate(blocks, axis=1).astype(BF16)
@@ -375,17 +412,17 @@
     lon_first, lon_second = swap_pairs(lon_count)
     lat_first, lat_second = swap_pairs(lat_count)
     edge_shape = jax.ShapeDtypeStruct((rank, LANES), BF16)
-    reduced, pay_a, pay_b = pl.pallas_call(
-        functools.partial(reduce_kernel, lon_count, held),
-        out_shape=(jax.ShapeDtypeStruct((rank, cells), BF16), edge_shape, edge_shape),
+    pay_a, pay_b = pl.pallas_call(
+        functools.partial(edge_kernel, lon_count, held),
+        out_shape=(edge_shape, edge_shape),
         in_specs=[HBM] * 4,
-        out_specs=(VMEM,) * 3,
+        out_specs=(VMEM,) * 2,
         scratch_shapes=[
             pltpu.SMEM(tile_regions.shape, jnp.int32),
             pltpu.SMEM(bank_slot.shape, jnp.int32),
             pltpu.VMEM(features.shape, BF16),
             pltpu.VMEM(in_factor.shape, BF16),
-            pltpu.VMEM((channels * lat_len, lon_len), F32),
+            pltpu.VMEM((channels * EDGE, lat_len), F32),
             pltpu.SemaphoreType.DMA((IN_COPIES + 3,)),
         ],
         compiler_params=PARAMS,
@@ -393,9 +430,10 @@
     got_b = lax.ppermute(pay_b, "lon", lon_second)
     got_a = lax.ppermute(pay_a, "lon", lon_first)
     core_shape = jax.ShapeDtypeStruct((PER_OWNER, core_rows, core_cols), BF16)
-    bank, own, position, weights, mixer, offset = pl.pallas_call(
+    reduced, bank, own, position, weights, mixer, offset = pl.pallas_call(
         functools.partial(prepare_kernel, lon_count, lat_len),
         out_shape=(
+            jax.ShapeDtypeStruct((rank, cells), BF16),
             jax.ShapeDtypeStruct(kernel_bank.shape, BF16),
             core_shape,
             jax.ShapeDtypeStruct(labels.shape, jnp.int32),
@@ -403,8 +441,8 @@
             jax.ShapeDtypeStruct((out_channels * GROUP, rank * GROUP), BF16),
             jax.ShapeDtypeStruct((out_channels * GROUP, lon_len), F32),
         ),
-        in_specs=[HBM] * 8,
-        out_specs=(VMEM,) * 6,
+        in_specs=[HBM] * 10,
+        out_specs=(VMEM,) * 7,
         scratch_shapes=[
             pltpu.SMEM(tile_regions.shape, jnp.int32),
             pltpu.SMEM(bank_slot.shape, jnp.int32),
@@ -412,17 +450,22 @@
             pltpu.VMEM(tap_factor.shape, BF16),
             pltpu.VMEM(out_factor.shape[::-1], BF16),
             pltpu.VMEM((1, out_channels), F32),
-            pltpu.SemaphoreType.DMA((6 + BANK_COPIES,)),
+            pltpu.VMEM(features.shape, BF16),
+            pltpu.VMEM(in_factor.shape, BF16),
+            pltpu.VMEM((channels * lat_len, lon_len), F32),
+            pltpu.SemaphoreType.DMA((8 + BANK_COPIES,)),
         ],
         compiler_params=PARAMS,
         cost_estimate=pl.CostEstimate(flops=10**6, bytes_accessed=kernel_bank.size * 4, transcendentals=0),
     )(
-        reduced,
+        pay_a,
         *(
             in_hbm(x)
             for x in (
                 tile_regions,
                 bank_slot,
+                features,
+                in_factor,
                 kernel_bank,
                 labels,
                 tap_factor,
@@ -432,41 +475,43 @@
         ),
     )
     row_shape = jax.ShapeDtypeStruct((rank, REACH * lon_len + LANES), BF16)
-    core_b, core_a, edges = pl.pallas_call(
+    core_b, core_a = pl.pallas_call(
         functools.partial(pick_kernel, lat_len),
-        out_shape=(core_shape, core_shape, edge_shape),
+        out_shape=(core_shape, core_shape),
         in_specs=[VMEM] * 3,
+        out_specs=(VMEM,) * 2,
+        compiler_params=PARAMS,
+    )(got_b, got_a, bank)
+    edges, row_a, row_b = pl.pallas_call(
+        functools.partial(rows_kernel, lat_len),
+        out_shape=(edge_shape, row_shape, row_shape),
+        in_specs=[VMEM, VMEM, HBM, VMEM],
         out_specs=(VMEM,) * 3,
         compiler_params=PARAMS,
-    )(got_b, got_a, bank)
+    )(got_b, got_a, core_a, reduced)
     core_b = lax.ppermute(core_b, "lon", lon_second)
     core_a = lax.ppermute(core_a, "lon", lon_first)
-    row_a, row_b = pl.pallas_call(
-        functools.partial(rows_kernel, lat_len),
-        out_shape=(row_shape, row_shape),
-        in_specs=[VMEM] * 2,
-        out_specs=(VMEM,) * 2,
-        compiler_params=PARAMS,
-    )(reduced, edges)
     row_a = lax.ppermute(row_a, "lat", lat_first)
     row_b = lax.ppermute(row_b, "lat", lat_second)
     border_cells = 2 * REACH * lon_len
-    inner = pl.pallas_call(
+    stack_rows = taps * rank // 2
+    halo_stack_shape = jax.ShapeDtypeStruct((2, stack_rows, border_cells), BF16)
+    inner, halo_stack = pl.pallas_call(
         functools.partial(inner_kernel, lat_len),
-        out_shape=jax.ShapeDtypeStruct((tap_rank * rank, cells - border_cells), BF16),
+        out_shape=(jax.ShapeDtypeStruct((tap_rank * rank, cells - border_cells), BF16), halo_stack_shape),
         in_specs=[VMEM] * 3,
-        out_specs=VMEM,
-        scratch_shapes=[pltpu.VMEM((2, taps * rank // 2, cells - border_cells), BF16)],
+        out_specs=(VMEM,) * 2,
+        scratch_shapes=[pltpu.VMEM((2, stack_rows, cells - border_cells), BF16)],
         compiler_params=PARAMS,
     )(reduced, edges, weights)
     border = pl.pallas_call(
         functools.partial(border_kernel, lat_len, lat_count),
         out_shape=jax.ShapeDtypeStruct((tap_rank * rank, border_cells), BF16),
-        in_specs=[VMEM] * 5,
+        in_specs=[VMEM] * 4,
         out_specs=VMEM,
-        scratch_shapes=[pltpu.VMEM((2, taps * rank // 2, border_cells), BF16)],
-        compiler_params=PARAMS,
-    )(reduced, edges, row_a, row_b, weights)
+        scratch_shapes=[pltpu.VMEM(halo_stack_shape.shape, BF16)],
+        compiler_params=PARAMS,
+    )(row_a, row_b, weights, halo_stack)
     out_shape = (out_channels, lat_len, lon_len)
     return pl.pallas_call(
         mix_kernel,

time: 20.7 us -> 20.7 us (level)
    pallas_call x3, Pallas kernels: 2.85 us -> 3.06 us  [the longest x1 1.46 us: on_device(): pl.pallas_call(functools.partial(inner_kernel, lat_len), out_shape=(jax.S...]
  transfers between devices with their start and end apart: 6 -> 6, of which waited for: 4 -> 4; matrix products, arithmetic and copies ran while one was open for 0% -> 0% of each run, Pallas kernels for 21% -> 22%
where the time goes in v2:
time: 20.7 us; the launch traced here: 20.6 us
  starting transfers between devices  10.4 us (50%)
  Pallas kernels  7.62 us (37%)
  waiting for transfers between devices  2.43 us (12%)
    ppermute x1, starting transfers between devices, on_device(): got_b = lax.ppermute(pay_b, 'lon', lon_second)  6.04 us
    ppermute x1, starting transfers between devices, on_device(): core_b = lax.ppermute(core_b, 'lon', lon_second)  2.77 us
    pallas_call x1, Pallas kernels, on_device(): pl.pallas_call(functools.partial(prepare_kernel, lon_count, lat_len), out...  2.29 us
    ppermute x1, starting transfers between devices, on_device(): row_b = lax.ppermute(row_b, 'lat', lat_second)  1.63 us
    pallas_call x1, Pallas kernels, on_device(): pl.pallas_call(mix_kernel, out_shape=jax.ShapeDtypeStruct(out_shape, BF16...  1.53 us
    pallas_call x1, Pallas kernels, on_device(): pl.pallas_call(functools.partial(inner_kernel, lat_len), out_shape=(jax.S...  1.46 us
    pallas_call x1, Pallas kernels, on_device(): pl.pallas_call(functools.partial(edge_kernel, lon_count, held), out_shape...  1.46 us
    ppermute x1, waiting for transfers between devices, on_device(): got_a = lax.ppermute(pay_a, 'lon', lon_first)  1.34 us
  transfers between devices with their start and end apart: 6, of which 4 were waited for; matrix products, arithmetic and copies ran while one was open for 0% of the time, Pallas kernels for 22%

profile of v2, /device:TPU:0, one launch (start us, length us, event | category | flops | bytes accessed | tf_op | source)
XLA Modules:
  0.0 20.6 jit_solution(18404880429138230558)
XLA Ops:
  0.0 1.5 %shard_map.91 = (bf16[32,128]{1,0:T(8,128)(2,1)S(1)}, bf16[32,128]{1,0:T(8,128)(2,1)S(1)}) custom-call(s32[1,1,6]{2,1,0:T(1,128)} %list_hbm.3, s32[896]{0:T(1024)} %slot_hbm.3, bf16[64,16,128]{2,1,0:T(8,128)(2,1)} %feat_hbm.3, bf16[32,64]{1,0:T(8,128)(2,1)} %in_hbm.3), custom_call_target="tpu_custom_call" | custom-call | tf_op jit(solution)/shard_map/pallas_call | solution.py:415
  1.5 6.0 %collective-permute-start = (bf16[32,128]{1,0:T(8,128)(2,1)S(1)}, bf16[32,128]{1,0:T(8,128)(2,1)S(1)}, u32[]{:S(2)}, u32[]{:S(2)}) collective-permute-start(bf16[32,128]{1,0:T(8,128)(2,1)S(1)} %get-tuple-element.23), channel_id=1, source_target_pairs={{0,7},{1,2},{2,1},{3,4},{4,3},{5,6},{6,5},{7,0},{8,15},{9,10},{10,... | collective-permute-start | bytes 24584 | tf_op jit(solution)/shard_map/ppermute | solution.py:430
  7.5 0.0 collective-permute-start.1
  7.5 2.3 %shard_map.92 = (bf16[32,2048]{1,0:T(8,128)(2,1)S(1)}, bf16[112,32,512]{2,1,0:T(8,128)(2,1)S(1)}, bf16[2,32,512]{2,1,0:T(8,128)(2,1)S(1)}, s32[16,128]{1,0:T(8,1...) custom-call(bf16[32,128]{1,0:T(8,128)(2,1)S(1)} %get-tuple-element.21.pay_hbm, ...), custom_call_target="tpu_custom_call" | custom-call | flops 1000000 | bytes 7340032 | tf_op jit(solution)/shard_map/pallas_call | solution.py:433
  9.8 0.0 collective-permute-done.got_b_ref
  9.8 1.3 %collective-permute-done.1.got_a_ref = bf16[32,128]{1,0:T(8,128)(2,1)S(1)} collective-permute-done((bf16[32,128]{1,0:T(8,128)(2,1)S(1)}, bf16[32,128]{1,0:T(8,128)(2,1)S(1)}, u32[]{:S(2)}, u32[]{:S(2)}) %collective-permute-start.1) | collective-permute-done | bytes 8224 | tf_op jit(solution)/shard_map/ppermute | solution.py:431
  11.2 0.1 shard_map.93
  11.3 2.8 %collective-permute-start.4 = (bf16[2,32,512]{2,1,0:T(8,128)(2,1)S(1)}, bf16[2,32,512]{2,1,0:T(8,128)(2,1)S(1)}, u32[]{:S(2)}, u32[]{:S(2)}) collective-permute-start(bf16[2,32,512]{2,1,0:T(8,128)(2,1)S(1)} %get-tuple-element.32), channel_id=1, source_target_pairs={{0,7},{1,2},{2,1},{3,4},{4,3},{5,6},{6,5},{7,0},{8,15},{9,10},{10,... | collective-permute-start | bytes 196616 | tf_op jit(solution)/shard_map/ppermute | solution.py:492
  14.1 0.0 collective-permute-start.5
  14.1 0.1 shard_map.94
  14.2 0.0 collective-permute-start.2
  14.2 1.6 %collective-permute-start.3 = (bf16[32,384]{1,0:T(8,128)(2,1)S(1)}, bf16[32,384]{1,0:T(8,128)(2,1)S(1)}, u32[]{:S(2)}, u32[]{:S(2)}) collective-permute-start(bf16[32,384]{1,0:T(8,128)(2,1)S(1)} %get-tuple-element.30), channel_id=1, source_target_pairs={{0,24},{8,16},{16,8},{24,0},{1,25},{9,17},{17,9},{25,1},{2,26},{10... | collective-permute-start | bytes 73736 | tf_op jit(solution)/shard_map/ppermute | solution.py:495
  15.9 1.5 %shard_map.95 = (bf16[512,1536]{1,0:T(8,128)(2,1)S(1)}, bf16[2,400,512]{2,1,0:T(8,128)(2,1)S(1)}) custom-call(bf16[32,2048]{1,0:T(8,128)(2,1)S(1)} %get-tuple-element.22.red_ref, bf16[32,128]{1,0:T(8,128)(2,1)S(1)} %get-tuple-element.26.edge_ref, bf16[256,400]{1,0:T(8,128)(2,1)S(1)} %get-tuple-element.27.weights_ref), custom_call_target="tpu_custom_call" | custom-call | tf_op jit(solution)/shard_map/pallas_call | solution.py:499
  17.3 0.0 collective-permute-done.2.row_a_ref
  17.3 0.2 collective-permute-done.3.row_b_ref
  17.5 0.6 %shard_map.96.border_ref = bf16[512,512]{1,0:T(8,128)(2,1)S(1)} custom-call(bf16[32,384]{1,0:T(8,128)(2,1)S(1)} %collective-permute-done.2.row_a_ref, bf16[32,384]{1,0:T(8,128)(2,1)S(1)} %collective-permute-done.3.row_b_ref, bf16[256,400]{1,0:T(8,128)(2,1)S(1)} %get-tuple-element.27.weights_ref, bf16[2,400,512]{2,1,0:T(8,128)(2,1)S(1)} %get-tuple-element.31.own_stack_ref), custom_call_target="tpu_custom_call" | custom-call | tf_op jit(solution)/shard_map/pallas_call | solution.py:507
  18.1 0.3 %collective-permute-done.4.core_b_ref = bf16[2,32,512]{2,1,0:T(8,128)(2,1)S(1)} collective-permute-done((bf16[2,32,512]{2,1,0:T(8,128)(2,1)S(1)}, bf16[2,32,512]{2,1,0:T(8,128)(2,1)S(1)}, u32[]{:S(2)}, u32[]{:S(2)}) %collective-permute-start.4) | collective-permute-done | bytes 65568 | tf_op jit(solution)/shard_map/ppermute | solution.py:492
  18.4 0.6 %collective-permute-done.5.core_a_ref = bf16[2,32,512]{2,1,0:T(8,128)(2,1)S(1)} collective-permute-done((bf16[2,32,512]{2,1,0:T(8,128)(2,1)S(1)}, bf16[2,32,512]{2,1,0:T(8,128)(2,1)S(1)}, u32[]{:S(2)}, u32[]{:S(2)}) %collective-permute-start.5) | collective-permute-done | bytes 65568 | tf_op jit(solution)/shard_map/ppermute | solution.py:493
  19.0 1.5 %shard_map.97 = bf16[64,16,128]{2,1,0:T(8,128)(2,1)} custom-call(bf16[512,1536]{1,0:T(8,128)(2,1)S(1)} %get-tuple-element.28.inner_ref, bf16[512,512]{1,0:T(8,128)(2,1)S(1)} %shard_map.96.border_ref, bf16[2,32,512]{2,1,0:T(8,128)(2,1)S(1)} %collective-permute-done.4.core_b_ref, bf16[2,32,512]{2,1,0:T(8,128)(2,1)S(1)} %collective-permute-done.5.core_a_ref, ...), custom_call_target="tpu_custom_call" | custom-call | tf_op jit(solution)/shard_map/pallas_call | solution.py:516
Async XLA Ops:
  1.5 8.3 %collective-permute-start = (bf16[32,128]{1,0:T(8,128)(2,1)S(1)}, bf16[32,128]{1,0:T(8,128)(2,1)S(1)}, u32[]{:S(2)}, u32[]{:S(2)}) collective-permute-start(bf16[32,128]{1,0:T(8,128)(2,1)S(1)} %get-tuple-element.23), channel_id=1, source_target_pairs={{0,7},{1,2},{2,1},{3,4},{4,3},{5,6},{6,5},{7,0},{8,15},{9,10},{10,... | collective-permute-start | bytes 24584 | tf_op jit(solution)/shard_map/ppermute | solution.py:430
  7.5 3.7 %collective-permute-start.1 = (bf16[32,128]{1,0:T(8,128)(2,1)S(1)}, bf16[32,128]{1,0:T(8,128)(2,1)S(1)}, u32[]{:S(2)}, u32[]{:S(2)}) collective-permute-start(bf16[32,128]{1,0:T(8,128)(2,1)S(1)} %get-tuple-element.21.pay_hbm), channel_id=1, source_target_pairs={{0,1},{1,0},{2,3},{3,2},{4,5},{5,4},{6,7},{7,6},{8,9},{9,8},{10,11... | collective-permute-start | bytes 24584 | tf_op jit(solution)/shard_map/ppermute | solution.py:431
  11.3 7.1 %collective-permute-start.4 = (bf16[2,32,512]{2,1,0:T(8,128)(2,1)S(1)}, bf16[2,32,512]{2,1,0:T(8,128)(2,1)S(1)}, u32[]{:S(2)}, u32[]{:S(2)}) collective-permute-start(bf16[2,32,512]{2,1,0:T(8,128)(2,1)S(1)} %get-tuple-element.32), channel_id=1, source_target_pairs={{0,7},{1,2},{2,1},{3,4},{4,3},{5,6},{6,5},{7,0},{8,15},{9,10},{10,... | collective-permute-start | bytes 196616 | tf_op jit(solution)/shard_map/ppermute | solution.py:492
  14.1 5.0 %collective-permute-start.5 = (bf16[2,32,512]{2,1,0:T(8,128)(2,1)S(1)}, bf16[2,32,512]{2,1,0:T(8,128)(2,1)S(1)}, u32[]{:S(2)}, u32[]{:S(2)}) collective-permute-start(bf16[2,32,512]{2,1,0:T(8,128)(2,1)S(1)} %get-tuple-element.25.core_ref), channel_id=1, source_target_pairs={{0,1},{1,0},{2,3},{3,2},{4,5},{5,4},{6,7},{7,6},{8,9},{9,8},{10,11... | collective-permute-start | bytes 196616 | tf_op jit(solution)/shard_map/ppermute | solution.py:493
  14.2 3.1 %collective-permute-start.2 = (bf16[32,384]{1,0:T(8,128)(2,1)S(1)}, bf16[32,384]{1,0:T(8,128)(2,1)S(1)}, u32[]{:S(2)}, u32[]{:S(2)}) collective-permute-start(bf16[32,384]{1,0:T(8,128)(2,1)S(1)} %get-tuple-element.29), channel_id=1, source_target_pairs={{0,8},{8,0},{16,24},{24,16},{1,9},{9,1},{17,25},{25,17},{2,10},{10... | collective-permute-start | bytes 73736 | tf_op jit(solution)/shard_map/ppermute | solution.py:494
  14.2 3.3 %collective-permute-start.3 = (bf16[32,384]{1,0:T(8,128)(2,1)S(1)}, bf16[32,384]{1,0:T(8,128)(2,1)S(1)}, u32[]{:S(2)}, u32[]{:S(2)}) collective-permute-start(bf16[32,384]{1,0:T(8,128)(2,1)S(1)} %get-tuple-element.30), channel_id=1, source_target_pairs={{0,24},{8,16},{16,8},{24,0},{1,25},{9,17},{17,9},{25,1},{2,26},{10... | collective-permute-start | bytes 73736 | tf_op jit(solution)/shard_map/ppermute | solution.py:495

commit v3 on v2

--- a/solution.py
+++ b/solution.py
@@ -15,7 +15,6 @@
 GROUP = 8
 STEP = 2
 OUT_COPIES = 4
-IN_COPIES = 4
 BANK_COPIES = 8
 F32 = jnp.float32
 BF16 = jnp.bfloat16
@@ -88,31 +87,36 @@
 ):
     channels, lat_len, lon_len = feat_ref.shape
     rank = in_ref.shape[0]
-    pairs = in_parts(feat_hbm, feat_ref, IN_COPIES)
-    pairs += ((slot_hbm, slot_ref), (list_hbm, list_ref), (in_hbm, in_ref))
-    for copy in start_copies(pairs, sems):
+    batch = LANES // EDGE
+    parts = channels // batch
+    pairs = ((slot_hbm, slot_ref), (list_hbm, list_ref)) + in_parts(feat_hbm, feat_ref, parts) + ((in_hbm, in_ref),)
+    copies = start_copies(pairs, sems)
+    for copy in copies[:2]:
         copy.wait()
+    _, rows = find_rows(list_ref, slot_ref, lon_count, held)
+    even = (lax.axis_index("lon") % 2) == 0
+    asked = []
+    for wanted in (even, jnp.logical_not(even)):
+        asked.append([jnp.where(wanted, rows[2][nth], rows[1][nth]).astype(F32) for nth in range(PER_OWNER)])
     lane = lane_index((lat_len, LANES))
-    batch = LANES // EDGE
-    for first in range(0, channels, batch):
+    for part in range(parts):
+        copies[2 + part].wait()
         packed = jnp.zeros((lat_len, LANES), F32)
         for c in range(batch):
-            moved = pltpu.roll(feat_ref[first + c].astype(F32), (EDGE * c + REACH) % LANES, 1)
+            moved = pltpu.roll(feat_ref[part * batch + c].astype(F32), (EDGE * c + REACH) % LANES, 1)
             packed = jnp.where(lane // EDGE == c, moved, packed)
-        turned_ref[first * EDGE : (first + batch) * EDGE, :] = jnp.transpose(packed)
+        turned_ref[part * LANES : (part + 1) * LANES, :] = jnp.transpose(packed)
     columns = jnp.concatenate(
         [turned_ref[pl.ds(j, channels, stride=EDGE), :].astype(BF16) for j in range(EDGE)], axis=1
     )
+    copies[2 + parts].wait()
     edges = jnp.dot(in_ref[...], columns, preferred_element_type=F32)
     edges = jnp.concatenate([edges, jnp.zeros((rank, LANES - EDGE * lat_len), F32)], axis=1)
-    _, rows = find_rows(list_ref, slot_ref, lon_count, held)
-    even = (lax.axis_index("lon") % 2) == 0
     lane = lane_index((rank, LANES))
-    for out_ref, wanted in ((pay_a_ref, even), (pay_b_ref, jnp.logical_not(even))):
+    for out_ref, ask in ((pay_a_ref, asked[0]), (pay_b_ref, asked[1])):
         load = edges
         for nth in range(PER_OWNER):
-            row = jnp.where(wanted, rows[2][nth], rows[1][nth]).astype(F32)
-            load = jnp.where(lane == EDGE * lat_len + nth, row, load)
+            load = jnp.where(lane == EDGE * lat_len + nth, ask[nth], load)
         out_ref[...] = load.astype(BF16)
 
 
@@ -276,7 +280,7 @@
                     ]
 
 
-def apply_taps(rank, weights_ref, stacked, tapped_ref, lon_len):
+def apply_taps(rank, weights_ref, stacked, tapped_ref, lon_len, then=None):
     half = rank // 2
     tap_rank = tapped_ref.shape[0] // rank
     width = STEP * lon_len
@@ -287,7 +291,18 @@
             .reshape(tap_rank, 1, half, width)
             for h in range(2)
         ]
-        tapped_ref[:, start : start + width] = jnp.concatenate(parts, axis=1).reshape(tap_rank * rank, width)
+        tapped = jnp.concatenate(parts, axis=1).reshape(tap_rank * rank, width)
+        tapped_ref[:, start : start + width] = tapped
+        if then is not None:
+            then(start, width, tapped)
+
+
+def pick_cores(cores, first, hidden, tapped, position):
+    rank = hidden.shape[0]
+    every = jnp.dot(cores, tapped, preferred_element_type=F32)
+    for index in range(cores.shape[0] // rank):
+        hidden = jnp.where(position == first + index, every[index * rank : (index + 1) * rank], hidden)
+    return hidden
 
 
 def border_slots(lat_len):
@@ -296,8 +311,28 @@
     return slots
 
 
-def inner_kernel(lat_len, red_ref, edge_ref, weights_ref, tapped_ref, halo_stack_ref, stack_ref):
+def flat_cores(*refs):
+    return jnp.concatenate([ref[...].reshape(-1, ref.shape[2]) for ref in refs], axis=0)
+
+
+def row_positions(position_ref, start):
+    return jnp.concatenate([position_ref[start + r : start + r + 1, :] for r in range(STEP)], axis=1)
+
+
+def inner_kernel(
+    lat_len,
+    red_ref,
+    edge_ref,
+    weights_ref,
+    own_ref,
+    position_ref,
+    tapped_ref,
+    halo_stack_ref,
+    hidden_ref,
+    stack_ref,
+):
     rank = red_ref.shape[0]
+    own = flat_cores(own_ref)
     lon_len = red_ref.shape[1] // lat_len
     slots = {p: p - REACH for p in range(REACH, lat_len - REACH)}
     edges = edge_ref[...].astype(F32)
@@ -306,10 +341,19 @@
         moved = shifted_columns(row, edges, p)
         stack_row(stack_ref, p, moved, slots, lon_len)
         stack_row(halo_stack_ref, p, moved, border_slots(lat_len), lon_len)
-    apply_taps(rank, weights_ref, lambda h, start, width: stack_ref[h, :, start : start + width], tapped_ref, lon_len)
-
-
-def border_kernel(lat_len, lat_count, row_a_ref, row_b_ref, weights_ref, own_stack_ref, tapped_ref, stack_ref):
+
+    def stacked(h, start, width):
+        return stack_ref[h, :, start : start + width]
+
+    def add_own(start, width, tapped):
+        position = row_positions(position_ref, start // lon_len + REACH)
+        hidden = jnp.zeros((rank, width), F32)
+        hidden_ref[:, start : start + width] = pick_cores(own, 0, hidden, tapped, position)
+
+    apply_taps(rank, weights_ref, stacked, tapped_ref, lon_len, add_own)
+
+
+def border_kernel(lat_len, lat_count, row_b_ref, row_a_ref, weights_ref, own_stack_ref, tapped_ref, stack_ref):
     rank = row_a_ref.shape[0]
     lon_len = (row_a_ref.shape[1] - LANES) // REACH
     lat = lax.axis_index("lat")
@@ -352,6 +396,7 @@
     core_b_ref,
     core_a_ref,
     own_ref,
+    hidden_ref,
     position_ref,
     mixer_ref,
     offset_ref,
@@ -361,22 +406,19 @@
 ):
     lat_len, lon_len = position_ref.shape
     rank = own_ref.shape[1]
-    cores = jnp.concatenate(
-        [ref[...].reshape(PER_OWNER * rank, -1) for ref in (own_ref, core_a_ref, core_b_ref)], axis=0
-    )
+    some = flat_cores(core_a_ref, core_b_ref)
+    every = flat_cores(own_ref, core_a_ref, core_b_ref)
     pieces = []
     for start in range(0, lat_len, STEP):
-        if start < REACH:
-            ref, first = border_ref, start
-        elif start < lat_len - REACH:
-            ref, first = inner_ref, start - REACH
+        position = row_positions(position_ref, start)
+        if REACH <= start < lat_len - REACH:
+            span = slice((start - REACH) * lon_len, (start - REACH + STEP) * lon_len)
+            hidden = pick_cores(some, PER_OWNER, hidden_ref[:, span], inner_ref[:, span], position)
         else:
-            ref, first = border_ref, start - (lat_len - 2 * REACH)
-        every = jnp.dot(cores, ref[:, first * lon_len : (first + STEP) * lon_len], preferred_element_type=F32)
-        position = jnp.concatenate([position_ref[start + r : start + r + 1, :] for r in range(STEP)], axis=1)
-        hidden = jnp.zeros((rank, STEP * lon_len), F32)
-        for index in range(3 * PER_OWNER):
-            hidden = jnp.where(position == index, every[index * rank : (index + 1) * rank], hidden)
+            first = start if start < REACH else start - (lat_len - 2 * REACH)
+            span = slice(first * lon_len, (first + STEP) * lon_len)
+            hidden = jnp.zeros((rank, STEP * lon_len), F32)
+            hidden = pick_cores(every, 0, hidden, border_ref[:, span], position)
         hidden = hidden.astype(BF16)
         pieces += [hidden[:, r * lon_len : (r + 1) * lon_len] for r in range(STEP)]
     groups = [jnp.concatenate(pieces[g : g + GROUP], axis=0) for g in range(0, lat_len, GROUP)]
@@ -423,7 +465,7 @@
             pltpu.VMEM(features.shape, BF16),
             pltpu.VMEM(in_factor.shape, BF16),
             pltpu.VMEM((channels * EDGE, lat_len), F32),
-            pltpu.SemaphoreType.DMA((IN_COPIES + 3,)),
+            pltpu.SemaphoreType.DMA((channels * EDGE // LANES + 3,)),
         ],
         compiler_params=PARAMS,
     )(*(in_hbm(x) for x in (tile_regions, bank_slot, features, in_factor)))
@@ -496,14 +538,18 @@
     border_cells = 2 * REACH * lon_len
     stack_rows = taps * rank // 2
     halo_stack_shape = jax.ShapeDtypeStruct((2, stack_rows, border_cells), BF16)
-    inner, halo_stack = pl.pallas_call(
+    inner, halo_stack, hidden = pl.pallas_call(
         functools.partial(inner_kernel, lat_len),
-        out_shape=(jax.ShapeDtypeStruct((tap_rank * rank, cells - border_cells), BF16), halo_stack_shape),
-        in_specs=[VMEM] * 3,
-        out_specs=(VMEM,) * 2,
+        out_shape=(
+            jax.ShapeDtypeStruct((tap_rank * rank, cells - border_cells), BF16),
+            halo_stack_shape,
+            jax.ShapeDtypeStruct((rank, cells - border_cells), F32),
+        ),
+        in_specs=[VMEM] * 5,
+        out_specs=(VMEM,) * 3,
         scratch_shapes=[pltpu.VMEM((2, stack_rows, cells - border_cells), BF16)],
         compiler_params=PARAMS,
-    )(reduced, edges, weights)
+    )(reduced, edges, weights, own, position)
     border = pl.pallas_call(
         functools.partial(border_kernel, lat_len, lat_count),
         out_shape=jax.ShapeDtypeStruct((tap_rank * rank, border_cells), BF16),
@@ -511,16 +557,16 @@
         out_specs=VMEM,
         scratch_shapes=[pltpu.VMEM(halo_stack_shape.shape, BF16)],
         compiler_params=PARAMS,
-    )(row_a, row_b, weights, halo_stack)
+    )(row_b, row_a, weights, halo_stack)
     out_shape = (out_channels, lat_len, lon_len)
     return pl.pallas_call(
         mix_kernel,
         out_shape=jax.ShapeDtypeStruct(out_shape, BF16),
-        in_specs=[VMEM] * 8,
+        in_specs=[VMEM] * 9,
         out_specs=HBM,
         scratch_shapes=[pltpu.VMEM(out_shape, BF16), pltpu.SemaphoreType.DMA((OUT_COPIES,))],
         compiler_params=PARAMS,
-    )(inner, border, core_b, core_a, own, position, mixer, offset)
+    )(inner, border, core_b, core_a, own, hidden, position, mixer, offset)
 
 
 def solution(mesh):

time: 20.7 us -> 20.8 us (level)
  Pallas kernels: 7.62 us -> 8.37 us
  waiting for transfers between devices: 2.43 us -> 1.7 us
    ppermute x1, starting transfers between devices: 0.01 us -> 1.63 us  [on_device(): row_a = lax.ppermute(row_a, 'lat', lat_first)]
    ppermute x1, starting transfers between devices: 1.63 us -> 0.01 us  [on_device(): row_b = lax.ppermute(row_b, 'lat', lat_second)]
    pallas_call x1, Pallas kernels: 1.46 us -> 2.17 us  [on_device(): pl.pallas_call(functools.partial(inner_kernel, lat_len), out_shape=(jax.S...]
    ppermute x1, waiting for transfers between devices: 0.29 us -> 0.01 us  [on_device(): core_b = lax.ppermute(core_b, 'lon', lon_second)]
    ppermute x1, waiting for transfers between devices: 0.63 us -> 0.35 us  [on_device(): core_a = lax.ppermute(core_a, 'lon', lon_first)]
  transfers between devices with their start and end apart: 6 -> 6, of which waited for: 4 -> 2; matrix products, arithmetic and copies ran while one was open for 0% -> 0% of each run, Pallas kernels for 22% -> 25%
where the time goes in v3:
time: 20.8 us; the launch traced here: 20.6 us
  starting transfers between devices  10.4 us (50%)
  Pallas kernels  8.37 us (40%)
  waiting for transfers between devices  1.7 us (8%)
    ppermute x1, starting transfers between devices, on_device(): got_b = lax.ppermute(pay_b, 'lon', lon_second)  6.04 us
    ppermute x1, starting transfers between devices, on_device(): core_b = lax.ppermute(core_b, 'lon', lon_second)  2.77 us
    pallas_call x1, Pallas kernels, on_device(): pl.pallas_call(functools.partial(prepare_kernel, lon_count, lat_len), out...  2.29 us
    pallas_call x1, Pallas kernels, on_device(): pl.pallas_call(functools.partial(inner_kernel, lat_len), out_shape=(jax.S...  2.17 us
    ppermute x1, starting transfers between devices, on_device(): row_a = lax.ppermute(row_a, 'lat', lat_first)  1.63 us
    pallas_call x1, Pallas kernels, on_device(): pl.pallas_call(functools.partial(edge_kernel, lon_count, held), out_shape...  1.57 us
    pallas_call x1, Pallas kernels, on_device(): pl.pallas_call(mix_kernel, out_shape=jax.ShapeDtypeStruct(out_shape, BF16...  1.46 us
    ppermute x1, waiting for transfers between devices, on_device(): got_a = lax.ppermute(pay_a, 'lon', lon_first)  1.34 us
  transfers between devices with their start and end apart: 6, of which 2 were waited for; matrix products, arithmetic and copies ran while one was open for 0% of the time, Pallas kernels for 25%

profile of v3, /device:TPU:0, one launch (start us, length us, event | category | flops | bytes accessed | tf_op | source)
XLA Modules:
  0.0 20.6 jit_solution(7268714627502870108)
XLA Ops:
  0.0 1.6 %shard_map.91 = (bf16[32,128]{1,0:T(8,128)(2,1)S(1)}, bf16[32,128]{1,0:T(8,128)(2,1)S(1)}) custom-call(s32[1,1,6]{2,1,0:T(1,128)} %list_hbm.3, s32[896]{0:T(1024)} %slot_hbm.3, bf16[64,16,128]{2,1,0:T(8,128)(2,1)} %feat_hbm.3, bf16[32,64]{1,0:T(8,128)(2,1)} %in_hbm.3), custom_call_target="tpu_custom_call" | custom-call | tf_op jit(solution)/shard_map/pallas_call | solution.py:457
  1.6 6.0 %collective-permute-start = (bf16[32,128]{1,0:T(8,128)(2,1)S(1)}, bf16[32,128]{1,0:T(8,128)(2,1)S(1)}, u32[]{:S(2)}, u32[]{:S(2)}) collective-permute-start(bf16[32,128]{1,0:T(8,128)(2,1)S(1)} %get-tuple-element.24), channel_id=1, source_target_pairs={{0,7},{1,2},{2,1},{3,4},{4,3},{5,6},{6,5},{7,0},{8,15},{9,10},{10,... | collective-permute-start | bytes 24584 | tf_op jit(solution)/shard_map/ppermute | solution.py:472
  7.6 0.0 collective-permute-start.1
  7.6 2.3 %shard_map.92 = (bf16[32,2048]{1,0:T(8,128)(2,1)S(1)}, bf16[112,32,512]{2,1,0:T(8,128)(2,1)S(1)}, bf16[2,32,512]{2,1,0:T(8,128)(2,1)S(1)}, s32[16,128]{1,0:T(8,1...) custom-call(bf16[32,128]{1,0:T(8,128)(2,1)S(1)} %get-tuple-element.22.pay_hbm, ...), custom_call_target="tpu_custom_call" | custom-call | flops 1000000 | bytes 7340032 | tf_op jit(solution)/shard_map/pallas_call | solution.py:475
  9.9 0.0 collective-permute-done.got_b_ref
  9.9 1.3 %collective-permute-done.1.got_a_ref = bf16[32,128]{1,0:T(8,128)(2,1)S(1)} collective-permute-done((bf16[32,128]{1,0:T(8,128)(2,1)S(1)}, bf16[32,128]{1,0:T(8,128)(2,1)S(1)}, u32[]{:S(2)}, u32[]{:S(2)}) %collective-permute-start.1) | collective-permute-done | bytes 8224 | tf_op jit(solution)/shard_map/ppermute | solution.py:473
  11.3 0.1 shard_map.93
  11.4 2.8 %collective-permute-start.4 = (bf16[2,32,512]{2,1,0:T(8,128)(2,1)S(1)}, bf16[2,32,512]{2,1,0:T(8,128)(2,1)S(1)}, u32[]{:S(2)}, u32[]{:S(2)}) collective-permute-start(bf16[2,32,512]{2,1,0:T(8,128)(2,1)S(1)} %get-tuple-element.35), channel_id=1, source_target_pairs={{0,7},{1,2},{2,1},{3,4},{4,3},{5,6},{6,5},{7,0},{8,15},{9,10},{10,... | collective-permute-start | bytes 196616 | tf_op jit(solution)/shard_map/ppermute | solution.py:534
  14.2 0.0 collective-permute-start.5
  14.2 0.1 shard_map.94
  14.3 0.0 collective-permute-start.2
  14.3 1.6 %collective-permute-start.3 = (bf16[32,384]{1,0:T(8,128)(2,1)S(1)}, bf16[32,384]{1,0:T(8,128)(2,1)S(1)}, u32[]{:S(2)}, u32[]{:S(2)}) collective-permute-start(bf16[32,384]{1,0:T(8,128)(2,1)S(1)} %get-tuple-element.33), channel_id=1, source_target_pairs={{0,8},{8,0},{16,24},{24,16},{1,9},{9,1},{17,25},{25,17},{2,10},{10... | collective-permute-start | bytes 73736 | tf_op jit(solution)/shard_map/ppermute | solution.py:536
  16.0 2.2 %shard_map.95 = (bf16[512,1536]{1,0:T(8,128)(2,1)S(1)}, bf16[2,400,512]{2,1,0:T(8,128)(2,1)S(1)}, f32[32,1536]{1,0:T(8,128)S(1)}) custom-call(bf16[32,2048]{1,0:T(8,128)(2,1)S(1)} %get-tuple-element.23.red_ref, bf16[32,128]{1,0:T(8,128)(2,1)S(1)} %get-tuple-element.27.edge_ref, bf16[256,400]{1,0:T(8,128)(2,1)S(1)} %get-tuple-element.28.weights_ref, ...), custom_call_target="tpu_custom_call" | custom-call | tf_op jit(solution)/shard_map/pallas_call | solution.py:541
  18.1 0.0 collective-permute-done.2.row_b_ref
  18.1 0.0 collective-permute-done.3.row_a_ref
  18.2 0.6 %shard_map.96.border_ref = bf16[512,512]{1,0:T(8,128)(2,1)S(1)} custom-call(bf16[32,384]{1,0:T(8,128)(2,1)S(1)} %collective-permute-done.2.row_b_ref, bf16[32,384]{1,0:T(8,128)(2,1)S(1)} %collective-permute-done.3.row_a_ref, bf16[256,400]{1,0:T(8,128)(2,1)S(1)} %get-tuple-element.28.weights_ref, bf16[2,400,512]{2,1,0:T(8,128)(2,1)S(1)} %get-tuple-element.34.own_stack_ref), custom_call_target="tpu_custom_call" | custom-call | tf_op jit(solution)/shard_map/pallas_call | solution.py:553
  18.8 0.0 collective-permute-done.4.core_b_ref
  18.8 0.4 %collective-permute-done.5.core_a_ref = bf16[2,32,512]{2,1,0:T(8,128)(2,1)S(1)} collective-permute-done((bf16[2,32,512]{2,1,0:T(8,128)(2,1)S(1)}, bf16[2,32,512]{2,1,0:T(8,128)(2,1)S(1)}, u32[]{:S(2)}, u32[]{:S(2)}) %collective-permute-start.5) | collective-permute-done | bytes 65568 | tf_op jit(solution)/shard_map/ppermute | solution.py:535
  19.1 1.5 %shard_map.97 = bf16[64,16,128]{2,1,0:T(8,128)(2,1)} custom-call(bf16[512,1536]{1,0:T(8,128)(2,1)S(1)} %get-tuple-element.31.inner_ref, bf16[512,512]{1,0:T(8,128)(2,1)S(1)} %shard_map.96.border_ref, bf16[2,32,512]{2,1,0:T(8,128)(2,1)S(1)} %collective-permute-done.4.core_b_ref, bf16[2,32,512]{2,1,0:T(8,128)(2,1)S(1)} %collective-permute-done.5.core_a_ref, ...), custom_call_target="tpu_custom_call" | custom-call | tf_op jit(solution)/shard_map/pallas_call | solution.py:562
Async XLA Ops:
  1.6 8.3 %collective-permute-start = (bf16[32,128]{1,0:T(8,128)(2,1)S(1)}, bf16[32,128]{1,0:T(8,128)(2,1)S(1)}, u32[]{:S(2)}, u32[]{:S(2)}) collective-permute-start(bf16[32,128]{1,0:T(8,128)(2,1)S(1)} %get-tuple-element.24), channel_id=1, source_target_pairs={{0,7},{1,2},{2,1},{3,4},{4,3},{5,6},{6,5},{7,0},{8,15},{9,10},{10,... | collective-permute-start | bytes 24584 | tf_op jit(solution)/shard_map/ppermute | solution.py:472
  7.6 3.7 %collective-permute-start.1 = (bf16[32,128]{1,0:T(8,128)(2,1)S(1)}, bf16[32,128]{1,0:T(8,128)(2,1)S(1)}, u32[]{:S(2)}, u32[]{:S(2)}) collective-permute-start(bf16[32,128]{1,0:T(8,128)(2,1)S(1)} %get-tuple-element.22.pay_hbm), channel_id=1, source_target_pairs={{0,1},{1,0},{2,3},{3,2},{4,5},{5,4},{6,7},{7,6},{8,9},{9,8},{10,11... | collective-permute-start | bytes 24584 | tf_op jit(solution)/shard_map/ppermute | solution.py:473
  11.4 7.4 %collective-permute-start.4 = (bf16[2,32,512]{2,1,0:T(8,128)(2,1)S(1)}, bf16[2,32,512]{2,1,0:T(8,128)(2,1)S(1)}, u32[]{:S(2)}, u32[]{:S(2)}) collective-permute-start(bf16[2,32,512]{2,1,0:T(8,128)(2,1)S(1)} %get-tuple-element.35), channel_id=1, source_target_pairs={{0,7},{1,2},{2,1},{3,4},{4,3},{5,6},{6,5},{7,0},{8,15},{9,10},{10,... | collective-permute-start | bytes 196616 | tf_op jit(solution)/shard_map/ppermute | solution.py:534
  14.2 5.0 %collective-permute-start.5 = (bf16[2,32,512]{2,1,0:T(8,128)(2,1)S(1)}, bf16[2,32,512]{2,1,0:T(8,128)(2,1)S(1)}, u32[]{:S(2)}, u32[]{:S(2)}) collective-permute-start(bf16[2,32,512]{2,1,0:T(8,128)(2,1)S(1)} %get-tuple-element.26.core_ref), channel_id=1, source_target_pairs={{0,1},{1,0},{2,3},{3,2},{4,5},{5,4},{6,7},{7,6},{8,9},{9,8},{10,11... | collective-permute-start | bytes 196616 | tf_op jit(solution)/shard_map/ppermute | solution.py:535
  14.3 3.8 %collective-permute-start.2 = (bf16[32,384]{1,0:T(8,128)(2,1)S(1)}, bf16[32,384]{1,0:T(8,128)(2,1)S(1)}, u32[]{:S(2)}, u32[]{:S(2)}) collective-permute-start(bf16[32,384]{1,0:T(8,128)(2,1)S(1)} %get-tuple-element.32), channel_id=1, source_target_pairs={{0,24},{8,16},{16,8},{24,0},{1,25},{9,17},{17,9},{25,1},{2,26},{10... | collective-permute-start | bytes 73736 | tf_op jit(solution)/shard_map/ppermute | solution.py:537
  14.3 3.8 %collective-permute-start.3 = (bf16[32,384]{1,0:T(8,128)(2,1)S(1)}, bf16[32,384]{1,0:T(8,128)(2,1)S(1)}, u32[]{:S(2)}, u32[]{:S(2)}) collective-permute-start(bf16[32,384]{1,0:T(8,128)(2,1)S(1)} %get-tuple-element.33), channel_id=1, source_target_pairs={{0,8},{8,0},{16,24},{24,16},{1,9},{9,1},{17,25},{25,17},{2,10},{10... | collective-permute-start | bytes 73736 | tf_op jit(solution)/shard_map/ppermute | solution.py:536

commit v4 on v2

--- a/solution.py
+++ b/solution.py
@@ -13,7 +13,7 @@
 LANES = 128
 EDGE = 2 * REACH
 GROUP = 8
-STEP = 2
+STEP = 4
 OUT_COPIES = 4
 IN_COPIES = 4
 BANK_COPIES = 8
@@ -309,7 +309,7 @@
     apply_taps(rank, weights_ref, lambda h, start, width: stack_ref[h, :, start : start + width], tapped_ref, lon_len)
 
 
-def border_kernel(lat_len, lat_count, row_a_ref, row_b_ref, weights_ref, own_stack_ref, tapped_ref, stack_ref):
+def border_kernel(lat_len, lat_count, row_b_ref, row_a_ref, weights_ref, own_stack_ref, tapped_ref, stack_ref):
     rank = row_a_ref.shape[0]
     lon_len = (row_a_ref.shape[1] - LANES) // REACH
     lat = lax.axis_index("lat")
@@ -364,21 +364,21 @@
     cores = jnp.concatenate(
         [ref[...].reshape(PER_OWNER * rank, -1) for ref in (own_ref, core_a_ref, core_b_ref)], axis=0
     )
-    pieces = []
-    for start in range(0, lat_len, STEP):
-        if start < REACH:
-            ref, first = border_ref, start
-        elif start < lat_len - REACH:
-            ref, first = inner_ref, start - REACH
-        else:
-            ref, first = border_ref, start - (lat_len - 2 * REACH)
-        every = jnp.dot(cores, ref[:, first * lon_len : (first + STEP) * lon_len], preferred_element_type=F32)
-        position = jnp.concatenate([position_ref[start + r : start + r + 1, :] for r in range(STEP)], axis=1)
-        hidden = jnp.zeros((rank, STEP * lon_len), F32)
+    chunks = [(border_ref, 0, [*range(REACH), *range(lat_len - REACH, lat_len)])]
+    for start in range(REACH, lat_len - REACH, STEP):
+        chunks.append((inner_ref, start - REACH, [*range(start, start + STEP)]))
+    by_row = {}
+    for ref, first, rows in chunks:
+        width = len(rows) * lon_len
+        every = jnp.dot(cores, ref[:, first * lon_len : first * lon_len + width], preferred_element_type=F32)
+        position = jnp.concatenate([position_ref[r : r + 1, :] for r in rows], axis=1)
+        hidden = jnp.zeros((rank, width), F32)
         for index in range(3 * PER_OWNER):
             hidden = jnp.where(position == index, every[index * rank : (index + 1) * rank], hidden)
         hidden = hidden.astype(BF16)
-        pieces += [hidden[:, r * lon_len : (r + 1) * lon_len] for r in range(STEP)]
+        for i, r in enumerate(rows):
+            by_row[r] = hidden[:, i * lon_len : (i + 1) * lon_len]
+    pieces = [by_row[r] for r in range(lat_len)]
     groups = [jnp.concatenate(pieces[g : g + GROUP], axis=0) for g in range(0, lat_len, GROUP)]
     channels = stage_ref.shape[0]
     share = channels // OUT_COPIES
@@ -511,7 +511,7 @@
         out_specs=VMEM,
         scratch_shapes=[pltpu.VMEM(halo_stack_shape.shape, BF16)],
         compiler_params=PARAMS,
-    )(row_a, row_b, weights, halo_stack)
+    )(row_b, row_a, weights, halo_stack)
     out_shape = (out_channels, lat_len, lon_len)
     return pl.pallas_call(
         mix_kernel,

time: 20.7 us -> 20.7 us (level)
    ppermute x1, starting transfers between devices: 0.01 us -> 1.63 us  [on_device(): row_a = lax.ppermute(row_a, 'lat', lat_first)]
    ppermute x1, starting transfers between devices: 1.63 us -> 0.01 us  [on_device(): row_b = lax.ppermute(row_b, 'lat', lat_second)]
where the time goes in v4:
time: 20.7 us; the launch traced here: 20.6 us
  starting transfers between devices  10.4 us (50%)
  Pallas kernels  7.66 us (37%)
  waiting for transfers between devices  2.41 us (12%)
    ppermute x1, starting transfers between devices, on_device(): got_b = lax.ppermute(pay_b, 'lon', lon_second)  6.04 us
    ppermute x1, starting transfers between devices, on_device(): core_b = lax.ppermute(core_b, 'lon', lon_second)  2.77 us
    pallas_call x1, Pallas kernels, on_device(): pl.pallas_call(functools.partial(prepare_kernel, lon_count, lat_len), out...  2.29 us
    ppermute x1, starting transfers between devices, on_device(): row_a = lax.ppermute(row_a, 'lat', lat_first)  1.63 us
    pallas_call x1, Pallas kernels, on_device(): pl.pallas_call(mix_kernel, out_shape=jax.ShapeDtypeStruct(out_shape, BF16...  1.54 us
    pallas_call x1, Pallas kernels, on_device(): pl.pallas_call(functools.partial(inner_kernel, lat_len), out_shape=(jax.S...  1.47 us
    pallas_call x1, Pallas kernels, on_device(): pl.pallas_call(functools.partial(edge_kernel, lon_count, held), out_shape...  1.46 us
    ppermute x1, waiting for transfers between devices, on_device(): got_a = lax.ppermute(pay_a, 'lon', lon_first)  1.34 us
  transfers between devices with their start and end apart: 6, of which 4 were waited for; matrix products, arithmetic and copies ran while one was open for 0% of the time, Pallas kernels for 22%

profile of v4, /device:TPU:0, one launch (start us, length us, event | category | flops | bytes accessed | tf_op | source)
XLA Modules:
  0.0 20.6 jit_solution(16800638223809555104)
XLA Ops:
  0.0 1.5 %shard_map.91 = (bf16[32,128]{1,0:T(8,128)(2,1)S(1)}, bf16[32,128]{1,0:T(8,128)(2,1)S(1)}) custom-call(s32[1,1,6]{2,1,0:T(1,128)} %list_hbm.3, s32[896]{0:T(1024)} %slot_hbm.3, bf16[64,16,128]{2,1,0:T(8,128)(2,1)} %feat_hbm.3, bf16[32,64]{1,0:T(8,128)(2,1)} %in_hbm.3), custom_call_target="tpu_custom_call" | custom-call | tf_op jit(solution)/shard_map/pallas_call | solution.py:415
  1.5 6.0 %collective-permute-start = (bf16[32,128]{1,0:T(8,128)(2,1)S(1)}, bf16[32,128]{1,0:T(8,128)(2,1)S(1)}, u32[]{:S(2)}, u32[]{:S(2)}) collective-permute-start(bf16[32,128]{1,0:T(8,128)(2,1)S(1)} %get-tuple-element.23), channel_id=1, source_target_pairs={{0,7},{1,2},{2,1},{3,4},{4,3},{5,6},{6,5},{7,0},{8,15},{9,10},{10,... | collective-permute-start | bytes 24584 | tf_op jit(solution)/shard_map/ppermute | solution.py:430
  7.5 0.0 collective-permute-start.1
  7.5 2.3 %shard_map.92 = (bf16[32,2048]{1,0:T(8,128)(2,1)S(1)}, bf16[112,32,512]{2,1,0:T(8,128)(2,1)S(1)}, bf16[2,32,512]{2,1,0:T(8,128)(2,1)S(1)}, s32[16,128]{1,0:T(8,1...) custom-call(bf16[32,128]{1,0:T(8,128)(2,1)S(1)} %get-tuple-element.21.pay_hbm, ...), custom_call_target="tpu_custom_call" | custom-call | flops 1000000 | bytes 7340032 | tf_op jit(solution)/shard_map/pallas_call | solution.py:433
  9.8 0.0 collective-permute-done.got_b_ref
  9.8 1.3 %collective-permute-done.1.got_a_ref = bf16[32,128]{1,0:T(8,128)(2,1)S(1)} collective-permute-done((bf16[32,128]{1,0:T(8,128)(2,1)S(1)}, bf16[32,128]{1,0:T(8,128)(2,1)S(1)}, u32[]{:S(2)}, u32[]{:S(2)}) %collective-permute-start.1) | collective-permute-done | bytes 8224 | tf_op jit(solution)/shard_map/ppermute | solution.py:431
  11.2 0.1 shard_map.93
  11.3 2.8 %collective-permute-start.4 = (bf16[2,32,512]{2,1,0:T(8,128)(2,1)S(1)}, bf16[2,32,512]{2,1,0:T(8,128)(2,1)S(1)}, u32[]{:S(2)}, u32[]{:S(2)}) collective-permute-start(bf16[2,32,512]{2,1,0:T(8,128)(2,1)S(1)} %get-tuple-element.32), channel_id=1, source_target_pairs={{0,7},{1,2},{2,1},{3,4},{4,3},{5,6},{6,5},{7,0},{8,15},{9,10},{10,... | collective-permute-start | bytes 196616 | tf_op jit(solution)/shard_map/ppermute | solution.py:492
  14.1 0.0 collective-permute-start.5
  14.1 0.1 shard_map.94
  14.2 0.0 collective-permute-start.2
  14.2 1.6 %collective-permute-start.3 = (bf16[32,384]{1,0:T(8,128)(2,1)S(1)}, bf16[32,384]{1,0:T(8,128)(2,1)S(1)}, u32[]{:S(2)}, u32[]{:S(2)}) collective-permute-start(bf16[32,384]{1,0:T(8,128)(2,1)S(1)} %get-tuple-element.30), channel_id=1, source_target_pairs={{0,8},{8,0},{16,24},{24,16},{1,9},{9,1},{17,25},{25,17},{2,10},{10... | collective-permute-start | bytes 73736 | tf_op jit(solution)/shard_map/ppermute | solution.py:494
  15.9 1.5 %shard_map.95 = (bf16[512,1536]{1,0:T(8,128)(2,1)S(1)}, bf16[2,400,512]{2,1,0:T(8,128)(2,1)S(1)}) custom-call(bf16[32,2048]{1,0:T(8,128)(2,1)S(1)} %get-tuple-element.22.red_ref, bf16[32,128]{1,0:T(8,128)(2,1)S(1)} %get-tuple-element.26.edge_ref, bf16[256,400]{1,0:T(8,128)(2,1)S(1)} %get-tuple-element.27.weights_ref), custom_call_target="tpu_custom_call" | custom-call | tf_op jit(solution)/shard_map/pallas_call | solution.py:499
  17.3 0.3 %collective-permute-done.2.row_b_ref = bf16[32,384]{1,0:T(8,128)(2,1)S(1)} collective-permute-done((bf16[32,384]{1,0:T(8,128)(2,1)S(1)}, bf16[32,384]{1,0:T(8,128)(2,1)S(1)}, u32[]{:S(2)}, u32[]{:S(2)}) %collective-permute-start.2) | collective-permute-done | bytes 24608 | tf_op jit(solution)/shard_map/ppermute | solution.py:495
  17.7 0.0 collective-permute-done.3.row_a_ref
  17.7 0.6 %shard_map.96.border_ref = bf16[512,512]{1,0:T(8,128)(2,1)S(1)} custom-call(bf16[32,384]{1,0:T(8,128)(2,1)S(1)} %collective-permute-done.2.row_b_ref, bf16[32,384]{1,0:T(8,128)(2,1)S(1)} %collective-permute-done.3.row_a_ref, bf16[256,400]{1,0:T(8,128)(2,1)S(1)} %get-tuple-element.27.weights_ref, bf16[2,400,512]{2,1,0:T(8,128)(2,1)S(1)} %get-tuple-element.31.own_stack_ref), custom_call_target="tpu_custom_call" | custom-call | tf_op jit(solution)/shard_map/pallas_call | solution.py:507
  18.3 0.1 collective-permute-done.4.core_b_ref
  18.4 0.6 %collective-permute-done.5.core_a_ref = bf16[2,32,512]{2,1,0:T(8,128)(2,1)S(1)} collective-permute-done((bf16[2,32,512]{2,1,0:T(8,128)(2,1)S(1)}, bf16[2,32,512]{2,1,0:T(8,128)(2,1)S(1)}, u32[]{:S(2)}, u32[]{:S(2)}) %collective-permute-start.5) | collective-permute-done | bytes 65568 | tf_op jit(solution)/shard_map/ppermute | solution.py:493
  19.0 1.5 %shard_map.97 = bf16[64,16,128]{2,1,0:T(8,128)(2,1)} custom-call(bf16[512,1536]{1,0:T(8,128)(2,1)S(1)} %get-tuple-element.28.inner_ref, bf16[512,512]{1,0:T(8,128)(2,1)S(1)} %shard_map.96.border_ref, bf16[2,32,512]{2,1,0:T(8,128)(2,1)S(1)} %collective-permute-done.4.core_b_ref, bf16[2,32,512]{2,1,0:T(8,128)(2,1)S(1)} %collective-permute-done.5.core_a_ref, ...), custom_call_target="tpu_custom_call" | custom-call | tf_op jit(solution)/shard_map/pallas_call | solution.py:516
Async XLA Ops:
  1.5 8.3 %collective-permute-start = (bf16[32,128]{1,0:T(8,128)(2,1)S(1)}, bf16[32,128]{1,0:T(8,128)(2,1)S(1)}, u32[]{:S(2)}, u32[]{:S(2)}) collective-permute-start(bf16[32,128]{1,0:T(8,128)(2,1)S(1)} %get-tuple-element.23), channel_id=1, source_target_pairs={{0,7},{1,2},{2,1},{3,4},{4,3},{5,6},{6,5},{7,0},{8,15},{9,10},{10,... | collective-permute-start | bytes 24584 | tf_op jit(solution)/shard_map/ppermute | solution.py:430
  7.5 3.7 %collective-permute-start.1 = (bf16[32,128]{1,0:T(8,128)(2,1)S(1)}, bf16[32,128]{1,0:T(8,128)(2,1)S(1)}, u32[]{:S(2)}, u32[]{:S(2)}) collective-permute-start(bf16[32,128]{1,0:T(8,128)(2,1)S(1)} %get-tuple-element.21.pay_hbm), channel_id=1, source_target_pairs={{0,1},{1,0},{2,3},{3,2},{4,5},{5,4},{6,7},{7,6},{8,9},{9,8},{10,11... | collective-permute-start | bytes 24584 | tf_op jit(solution)/shard_map/ppermute | solution.py:431
  11.3 7.1 %collective-permute-start.4 = (bf16[2,32,512]{2,1,0:T(8,128)(2,1)S(1)}, bf16[2,32,512]{2,1,0:T(8,128)(2,1)S(1)}, u32[]{:S(2)}, u32[]{:S(2)}) collective-permute-start(bf16[2,32,512]{2,1,0:T(8,128)(2,1)S(1)} %get-tuple-element.32), channel_id=1, source_target_pairs={{0,7},{1,2},{2,1},{3,4},{4,3},{5,6},{6,5},{7,0},{8,15},{9,10},{10,... | collective-permute-start | bytes 196616 | tf_op jit(solution)/shard_map/ppermute | solution.py:492
  14.1 5.0 %collective-permute-start.5 = (bf16[2,32,512]{2,1,0:T(8,128)(2,1)S(1)}, bf16[2,32,512]{2,1,0:T(8,128)(2,1)S(1)}, u32[]{:S(2)}, u32[]{:S(2)}) collective-permute-start(bf16[2,32,512]{2,1,0:T(8,128)(2,1)S(1)} %get-tuple-element.25.core_ref), channel_id=1, source_target_pairs={{0,1},{1,0},{2,3},{3,2},{4,5},{5,4},{6,7},{7,6},{8,9},{9,8},{10,11... | collective-permute-start | bytes 196616 | tf_op jit(solution)/shard_map/ppermute | solution.py:493
  14.2 3.4 %collective-permute-start.2 = (bf16[32,384]{1,0:T(8,128)(2,1)S(1)}, bf16[32,384]{1,0:T(8,128)(2,1)S(1)}, u32[]{:S(2)}, u32[]{:S(2)}) collective-permute-start(bf16[32,384]{1,0:T(8,128)(2,1)S(1)} %get-tuple-element.29), channel_id=1, source_target_pairs={{0,24},{8,16},{16,8},{24,0},{1,25},{9,17},{17,9},{25,1},{2,26},{10... | collective-permute-start | bytes 73736 | tf_op jit(solution)/shard_map/ppermute | solution.py:495
  14.2 3.4 %collective-permute-start.3 = (bf16[32,384]{1,0:T(8,128)(2,1)S(1)}, bf16[32,384]{1,0:T(8,128)(2,1)S(1)}, u32[]{:S(2)}, u32[]{:S(2)}) collective-permute-start(bf16[32,384]{1,0:T(8,128)(2,1)S(1)} %get-tuple-element.30), channel_id=1, source_target_pairs={{0,8},{8,0},{16,24},{24,16},{1,9},{9,1},{17,25},{25,17},{2,10},{10... | collective-permute-start | bytes 73736 | tf_op jit(solution)/shard_map/ppermute | solution.py:494

commit v5 on v4

--- a/solution.py
+++ b/solution.py
@@ -54,120 +54,41 @@
 def find_rows(list_ref, slot_ref, lon_count, held):
     me = lax.axis_index("lon")
     owners = (me, lax.rem(me + lon_count - 1, lon_count), lax.rem(me + 1, lon_count))
-    counts = [jnp.int32(0)] * 3
-    places = [[jnp.int32(0)] * PER_OWNER for _ in range(3)]
-    rows = [[jnp.int32(0)] * PER_OWNER for _ in range(3)]
-    for i in range(list_ref.shape[2]):
-        slot = slot_ref[list_ref[0, 0, i]]
-        for group, owner in enumerate(owners):
+    slots = [slot_ref[list_ref[0, 0, i]] for i in range(list_ref.shape[2])]
+    places, rows = [], []
+    for owner in owners:
+        least, greatest = jnp.int32(held), jnp.int32(-1)
+        first, last = jnp.int32(0), jnp.int32(0)
+        for i, slot in enumerate(slots):
             local = slot - owner * held
             hit = (local >= 0) & (local < held)
-            for nth in range(PER_OWNER):
-                take = hit & (counts[group] == nth)
-                places[group][nth] = jnp.where(take, i, places[group][nth])
-                rows[group][nth] = jnp.where(take, local, rows[group][nth])
-            counts[group] = counts[group] + hit.astype(jnp.int32)
+            first = jnp.where(hit & (local < least), i, first)
+            last = jnp.where(hit & (local > greatest), i, last)
+            least = jnp.where(hit, jnp.minimum(local, least), least)
+            greatest = jnp.where(hit, jnp.maximum(local, greatest), greatest)
+        places.append([first, last])
+        rows.append([jnp.minimum(least, held - 1), jnp.maximum(greatest, 0)])
     return places, rows
 
 
-def edge_kernel(
-    lon_count,
-    held,
-    list_hbm,
-    slot_hbm,
-    feat_hbm,
-    in_hbm,
-    pay_a_ref,
-    pay_b_ref,
-    list_ref,
-    slot_ref,
-    feat_ref,
-    in_ref,
-    turned_ref,
-    sems,
-):
-    channels, lat_len, lon_len = feat_ref.shape
-    rank = in_ref.shape[0]
-    pairs = in_parts(feat_hbm, feat_ref, IN_COPIES)
-    pairs += ((slot_hbm, slot_ref), (list_hbm, list_ref), (in_hbm, in_ref))
-    for copy in start_copies(pairs, sems):
+class Held:
+    names = ("bank", "own", "position", "weights", "mixer", "offset")
+    sources = ("labels", "tap", "out_factor", "bias")
+
+    def __init__(self, refs):
+        self.__dict__.update(zip(self.names, refs))
+
+
+def start_sources(sources, targets, bank_hbm, bank_ref, sems):
+    pairs = tuple(zip(sources, targets))
+    return start_copies(pairs + in_parts(bank_hbm, bank_ref, BANK_COPIES), sems)
+
+
+def build_held(lon_count, list_ref, slot_ref, targets, copies, held):
+    labels_ref, tap_ref, out_factor_ref, bias_ref = targets
+    for copy in copies[: len(targets)]:
         copy.wait()
-    lane = lane_index((lat_len, LANES))
-    batch = LANES // EDGE
-    for first in range(0, channels, batch):
-        packed = jnp.zeros((lat_len, LANES), F32)
-        for c in range(batch):
-            moved = pltpu.roll(feat_ref[first + c].astype(F32), (EDGE * c + REACH) % LANES, 1)
-            packed = jnp.where(lane // EDGE == c, moved, packed)
-        turned_ref[first * EDGE : (first + batch) * EDGE, :] = jnp.transpose(packed)
-    columns = jnp.concatenate(
-        [turned_ref[pl.ds(j, channels, stride=EDGE), :].astype(BF16) for j in range(EDGE)], axis=1
-    )
-    edges = jnp.dot(in_ref[...], columns, preferred_element_type=F32)
-    edges = jnp.concatenate([edges, jnp.zeros((rank, LANES - EDGE * lat_len), F32)], axis=1)
-    _, rows = find_rows(list_ref, slot_ref, lon_count, held)
-    even = (lax.axis_index("lon") % 2) == 0
-    lane = lane_index((rank, LANES))
-    for out_ref, wanted in ((pay_a_ref, even), (pay_b_ref, jnp.logical_not(even))):
-        load = edges
-        for nth in range(PER_OWNER):
-            row = jnp.where(wanted, rows[2][nth], rows[1][nth]).astype(F32)
-            load = jnp.where(lane == EDGE * lat_len + nth, row, load)
-        out_ref[...] = load.astype(BF16)
-
-
-def prepare_kernel(
-    lon_count,
-    lat_len,
-    pay_hbm,
-    list_hbm,
-    slot_hbm,
-    feat_hbm,
-    in_hbm,
-    bank_hbm,
-    labels_hbm,
-    tap_hbm,
-    out_factor_hbm,
-    bias_hbm,
-    red_ref,
-    bank_ref,
-    own_ref,
-    position_ref,
-    weights_ref,
-    mixer_ref,
-    offset_ref,
-    list_ref,
-    slot_ref,
-    labels_ref,
-    tap_ref,
-    out_factor_ref,
-    bias_ref,
-    feat_ref,
-    in_ref,
-    rows_ref,
-    sems,
-):
-    held = bank_hbm.shape[0]
-    small = (
-        (list_hbm, list_ref),
-        (slot_hbm, slot_ref),
-        (labels_hbm, labels_ref),
-        (tap_hbm, tap_ref),
-        (out_factor_hbm, out_factor_ref),
-        (bias_hbm, bias_ref),
-        (in_hbm, in_ref),
-        (feat_hbm, feat_ref),
-    )
-    copies = start_copies(small + in_parts(bank_hbm, bank_ref, BANK_COPIES), sems)
-    for copy in copies[: len(small)]:
-        copy.wait()
-    channels, lon_len = feat_ref.shape[0], feat_ref.shape[2]
-    rows_ref[...] = feat_ref[...].astype(F32).reshape(channels * lat_len, lon_len)
-    cells = jnp.concatenate(
-        [rows_ref[pl.ds(p, channels, stride=lat_len), :].astype(BF16) for p in range(lat_len)], axis=1
-    )
-    red_ref[...] = jnp.dot(in_ref[...], cells, preferred_element_type=F32).astype(BF16)
-    places, rows = find_rows(list_ref, slot_ref, lon_count, held)
+    places, rows = find_rows(list_ref, slot_ref, lon_count, held.bank.shape[0])
     even = (lax.axis_index("lon") % 2) == 0
     order = list(places[0])
     order += [jnp.where(even, places[2][nth], places[1][nth]) for nth in range(PER_OWNER)]
@@ -176,7 +97,7 @@
     position = jnp.zeros(labels.shape, jnp.int32)
     for index, place in enumerate(order):
         position = jnp.where(labels == place, index, position)
-    position_ref[...] = position
+    held.position[...] = position
 
     rank, out_channels = out_factor_ref.shape
     half = rank // 2
@@ -191,7 +112,7 @@
     tall = jnp.dot(spread, tap_ref[...], preferred_element_type=F32).astype(BF16)
     wide = jnp.dot(tall, repeat, preferred_element_type=F32)
     same = lax.broadcasted_iota(jnp.int32, shape, 0) % half == lane_index(shape) % half
-    weights_ref[...] = jnp.where(same, wide, 0.0).astype(BF16)
+    held.weights[...] = jnp.where(same, wide, 0.0).astype(BF16)
 
     shape = (out_channels * GROUP, rank * GROUP)
     spread = (
@@ -206,25 +127,115 @@
     ).astype(BF16)
     wide = jnp.dot(tall, repeat, preferred_element_type=F32)
     same = lax.broadcasted_iota(jnp.int32, shape, 0) % GROUP == lane_index(shape) // rank
-    mixer_ref[...] = jnp.where(same, wide, 0.0).astype(BF16)
+    held.mixer[...] = jnp.where(same, wide, 0.0).astype(BF16)
 
     shape = (out_channels * GROUP, out_channels)
     mine = lax.broadcasted_iota(jnp.int32, shape, 0) // GROUP == lane_index(shape)
     offset = jnp.sum(jnp.where(mine, bias_ref[...], 0.0), axis=1, keepdims=True)
-    offset_ref[...] = jnp.broadcast_to(offset, offset_ref.shape)
-    for copy in copies[len(small) :]:
+    held.offset[...] = jnp.broadcast_to(offset, held.offset.shape)
+    for copy in copies[len(targets) :]:
         copy.wait()
     for nth in range(PER_OWNER):
-        own_ref[nth] = bank_ref[rows[0][nth]]
-
-
-def pick_kernel(lat_len, got_b_ref, got_a_ref, bank_ref, core_b_ref, core_a_ref):
+        held.own[nth] = held.bank[rows[0][nth]]
+
+
+def edge_kernel(lon_count, *refs):
+    list_hbm, slot_hbm, feat_hbm, in_hbm, bank_hbm = refs[:5]
+    sources, (pay_a_ref, pay_b_ref), held_refs = refs[5:9], refs[9:11], refs[11:17]
+    list_ref, slot_ref, feat_ref, in_ref, turned_ref = refs[17:22]
+    targets, sems, held_sems = refs[22:26], refs[26], refs[27]
+    held = Held(held_refs)
+    channels, lat_len, lon_len = feat_ref.shape
+    rank = in_ref.shape[0]
+    early = lax.axis_index("lon") != lon_count - 1
+    pairs = in_parts(feat_hbm, feat_ref, IN_COPIES)
+    pairs += ((slot_hbm, slot_ref), (list_hbm, list_ref), (in_hbm, in_ref))
+    copies = start_copies(pairs, sems)
+
+    @pl.when(early)
+    def _():
+        start_sources(sources, targets, bank_hbm, held.bank, held_sems)
+
+    for copy in copies:
+        copy.wait()
+    lane = lane_index((lat_len, LANES))
+    batch = LANES // EDGE
+    for first in range(0, channels, batch):
+        packed = jnp.zeros((lat_len, LANES), F32)
+        for c in range(batch):
+            moved = pltpu.roll(feat_ref[first + c].astype(F32), (EDGE * c + REACH) % LANES, 1)
+            packed = jnp.where(lane // EDGE == c, moved, packed)
+        turned_ref[first * EDGE : (first + batch) * EDGE, :] = jnp.transpose(packed)
+    columns = jnp.concatenate(
+        [turned_ref[pl.ds(j, channels, stride=EDGE), :].astype(BF16) for j in range(EDGE)], axis=1
+    )
+    edges = jnp.dot(in_ref[...], columns, preferred_element_type=F32)
+    edges = jnp.concatenate([edges, jnp.zeros((rank, LANES - EDGE * lat_len), F32)], axis=1)
+    _, rows = find_rows(list_ref, slot_ref, lon_count, held.bank.shape[0])
+    even = (lax.axis_index("lon") % 2) == 0
+    lane = lane_index((rank, LANES))
+    for out_ref, wanted in ((pay_a_ref, even), (pay_b_ref, jnp.logical_not(even))):
+        load = edges
+        for nth in range(PER_OWNER):
+            row = jnp.where(wanted, rows[2][nth], rows[1][nth]).astype(F32)
+            load = jnp.where(lane == EDGE * lat_len + nth, row, load)
+        out_ref[...] = load.astype(BF16)
+
+    @pl.when(early)
+    def _():
+        pairs = tuple(zip(sources, targets)) + in_parts(bank_hbm, held.bank, BANK_COPIES)
+        waits = [pltpu.make_async_copy(source, target, held_sems.at[i]) for i, (source, target) in enumerate(pairs)]
+        build_held(lon_count, list_ref, slot_ref, targets, waits, held)
+
+
+def prepare_kernel(lon_count, lat_len, *refs):
+    list_hbm, slot_hbm, feat_hbm, in_hbm, bank_hbm = refs[:5]
+    sources, given = refs[5:9], Held((None, *refs[9:14]))
+    red_ref, held = refs[14], Held(refs[15:21])
+    list_ref, slot_ref, feat_ref, in_ref, rows_ref = refs[21:26]
+    targets, sems, held_sems = refs[26:30], refs[30], refs[31]
+    early = lax.axis_index("lon") != lon_count - 1
+    pairs = in_parts(feat_hbm, feat_ref, IN_COPIES) + ((in_hbm, in_ref),)
+    copies = start_copies(pairs, sems)
+    late_pairs = ((slot_hbm, slot_ref), (list_hbm, list_ref))
+    late_pairs += tuple(zip(sources, targets)) + in_parts(bank_hbm, held.bank, BANK_COPIES)
+
+    @pl.when(jnp.logical_not(early))
+    def _():
+        start_copies(late_pairs, held_sems)
+
+    @pl.when(early)
+    def _():
+        for name in held.names[1:]:
+            getattr(held, name)[...] = getattr(given, name)[...]
+
+    for copy in copies:
+        copy.wait()
+    channels, lon_len = feat_ref.shape[0], feat_ref.shape[2]
+    rows_ref[...] = feat_ref[...].astype(F32).reshape(channels * lat_len, lon_len)
+    cells = jnp.concatenate(
+        [rows_ref[pl.ds(p, channels, stride=lat_len), :].astype(BF16) for p in range(lat_len)], axis=1
+    )
+    red_ref[...] = jnp.dot(in_ref[...], cells, preferred_element_type=F32).astype(BF16)
+
+    @pl.when(jnp.logical_not(early))
+    def _():
+        waits = [
+            pltpu.make_async_copy(source, target, held_sems.at[i]) for i, (source, target) in enumerate(late_pairs)
+        ]
+        for copy in waits[:2]:
+            copy.wait()
+        build_held(lon_count, list_ref, slot_ref, targets, waits[2:], held)
+
+
+def pick_kernel(lon_count, lat_len, got_b_ref, got_a_ref, early_bank_ref, late_bank_ref, core_a_ref, core_b_ref):
+    early = lax.axis_index("lon") != lon_count - 1
     lane = lane_index((1, LANES))
     for got_ref, core_ref in ((got_b_ref, core_b_ref), (got_a_ref, core_a_ref)):
         head = got_ref[...].astype(F32)[0:1, :]
         for nth in range(PER_OWNER):
             row = jnp.sum(jnp.where(lane == EDGE * lat_len + nth, head, 0.0)).astype(jnp.int32)
-            core_ref[nth] = bank_ref[row]
+            core_ref[nth] = jnp.where(early, early_bank_ref[row], late_bank_ref[row])
 
 
 def rows_kernel(lat_len, got_b_ref, got_a_ref, core_ref, red_ref, edge_ref, row_a_ref, row_b_ref):
@@ -349,8 +360,8 @@
 def mix_kernel(
     inner_ref,
     border_ref,
+    core_a_ref,
     core_b_ref,
-    core_a_ref,
     own_ref,
     position_ref,
     mixer_ref,
@@ -412,83 +423,87 @@
     lon_first, lon_second = swap_pairs(lon_count)
     lat_first, lat_second = swap_pairs(lat_count)
     edge_shape = jax.ShapeDtypeStruct((rank, LANES), BF16)
-    pay_a, pay_b = pl.pallas_call(
-        functools.partial(edge_kernel, lon_count, held),
-        out_shape=(edge_shape, edge_shape),
-        in_specs=[HBM] * 4,
-        out_specs=(VMEM,) * 2,
+    core_shape = jax.ShapeDtypeStruct((PER_OWNER, core_rows, core_cols), BF16)
+    held_shapes = (
+        jax.ShapeDtypeStruct(kernel_bank.shape, BF16),
+        core_shape,
+        jax.ShapeDtypeStruct(labels.shape, jnp.int32),
+        jax.ShapeDtypeStruct((tap_rank * rank // 2, taps * rank // 2), BF16),
+        jax.ShapeDtypeStruct((out_channels * GROUP, rank * GROUP), BF16),
+        jax.ShapeDtypeStruct((out_channels * GROUP, lon_len), F32),
+    )
+    lists = [
+        pltpu.SMEM(tile_regions.shape, jnp.int32),
+        pltpu.SMEM(bank_slot.shape, jnp.int32),
+        pltpu.VMEM(features.shape, BF16),
+        pltpu.VMEM(in_factor.shape, BF16),
+    ]
+    targets = [
+        pltpu.VMEM(labels.shape, jnp.int32),
+        pltpu.VMEM(tap_factor.shape, BF16),
+        pltpu.VMEM(out_factor.shape[::-1], BF16),
+        pltpu.VMEM((1, out_channels), F32),
+    ]
+    sources = tuple(
+        in_hbm(x)
+        for x in (
+            tile_regions,
+            bank_slot,
+            features,
+            in_factor,
+            kernel_bank,
+            labels,
+            tap_factor,
+            out_factor.T,
+            out_bias.reshape(1, -1),
+        )
+    )
+    pay_a, pay_b, early_bank, *given = pl.pallas_call(
+        functools.partial(edge_kernel, lon_count),
+        out_shape=(edge_shape, edge_shape, *held_shapes),
+        in_specs=[HBM] * 9,
+        out_specs=(VMEM,) * 8,
         scratch_shapes=[
-            pltpu.SMEM(tile_regions.shape, jnp.int32),
-            pltpu.SMEM(bank_slot.shape, jnp.int32),
-            pltpu.VMEM(features.shape, BF16),
-            pltpu.VMEM(in_factor.shape, BF16),
+            *lists,
             pltpu.VMEM((channels * EDGE, lat_len), F32),
+            *targets,
             pltpu.SemaphoreType.DMA((IN_COPIES + 3,)),
+            pltpu.SemaphoreType.DMA((4 + BANK_COPIES,)),
         ],
         compiler_params=PARAMS,
-    )(*(in_hbm(x) for x in (tile_regions, bank_slot, features, in_factor)))
+    )(*sources)
     got_b = lax.ppermute(pay_b, "lon", lon_second)
     got_a = lax.ppermute(pay_a, "lon", lon_first)
-    core_shape = jax.ShapeDtypeStruct((PER_OWNER, core_rows, core_cols), BF16)
-    reduced, bank, own, position, weights, mixer, offset = pl.pallas_call(
+    reduced, late_bank, own, position, weights, mixer, offset = pl.pallas_call(
         functools.partial(prepare_kernel, lon_count, lat_len),
-        out_shape=(
-            jax.ShapeDtypeStruct((rank, cells), BF16),
-            jax.ShapeDtypeStruct(kernel_bank.shape, BF16),
-            core_shape,
-            jax.ShapeDtypeStruct(labels.shape, jnp.int32),
-            jax.ShapeDtypeStruct((tap_rank * rank // 2, taps * rank // 2), BF16),
-            jax.ShapeDtypeStruct((out_channels * GROUP, rank * GROUP), BF16),
-            jax.ShapeDtypeStruct((out_channels * GROUP, lon_len), F32),
-        ),
-        in_specs=[HBM] * 10,
+        out_shape=(jax.ShapeDtypeStruct((rank, cells), BF16), *held_shapes),
+        in_specs=[HBM] * 9 + [VMEM] * 5,
         out_specs=(VMEM,) * 7,
         scratch_shapes=[
-            pltpu.SMEM(tile_regions.shape, jnp.int32),
-            pltpu.SMEM(bank_slot.shape, jnp.int32),
-            pltpu.VMEM(labels.shape, jnp.int32),
-            pltpu.VMEM(tap_factor.shape, BF16),
-            pltpu.VMEM(out_factor.shape[::-1], BF16),
-            pltpu.VMEM((1, out_channels), F32),
-            pltpu.VMEM(features.shape, BF16),
-            pltpu.VMEM(in_factor.shape, BF16),
+            *lists,
             pltpu.VMEM((channels * lat_len, lon_len), F32),
-            pltpu.SemaphoreType.DMA((8 + BANK_COPIES,)),
+            *targets,
+            pltpu.SemaphoreType.DMA((IN_COPIES + 1,)),
+            pltpu.SemaphoreType.DMA((6 + BANK_COPIES,)),
         ],
         compiler_params=PARAMS,
         cost_estimate=pl.CostEstimate(flops=10**6, bytes_accessed=kernel_bank.size * 4, transcendentals=0),
-    )(
-        pay_a,
-        *(
-            in_hbm(x)
-            for x in (
-                tile_regions,
-                bank_slot,
-                features,
-                in_factor,
-                kernel_bank,
-                labels,
-                tap_factor,
-                out_factor.T,
-                out_bias.reshape(1, -1),
-            )
-        ),
-    )
+    )(*sources, *given)
     row_shape = jax.ShapeDtypeStruct((rank, REACH * lon_len + LANES), BF16)
-    core_b, core_a = pl.pallas_call(
-        functools.partial(pick_kernel, lat_len),
+    core_a, core_b = pl.pallas_call(
+        functools.partial(pick_kernel, lon_count, lat_len),
         out_shape=(core_shape, core_shape),
-        in_specs=[VMEM] * 3,
+        in_specs=[VMEM] * 4,
         out_specs=(VMEM,) * 2,
         compiler_params=PARAMS,
-    )(got_b, got_a, bank)
+    )(got_b, got_a, early_bank, late_bank)
     edges, row_a, row_b = pl.pallas_call(
         functools.partial(rows_kernel, lat_len),
         out_shape=(edge_shape, row_shape, row_shape),
         in_specs=[VMEM, VMEM, HBM, VMEM],
         out_specs=(VMEM,) * 3,
         compiler_params=PARAMS,
-    )(got_b, got_a, core_a, reduced)
+    )(got_b, got_a, core_b, reduced)
     core_b = lax.ppermute(core_b, "lon", lon_second)
     core_a = lax.ppermute(core_a, "lon", lon_first)
     row_a = lax.ppermute(row_a, "lat", lat_first)
@@ -520,7 +535,7 @@
         out_specs=HBM,
         scratch_shapes=[pltpu.VMEM(out_shape, BF16), pltpu.SemaphoreType.DMA((OUT_COPIES,))],
         compiler_params=PARAMS,
-    )(inner, border, core_b, core_a, own, position, mixer, offset)
+    )(inner, border, core_a, core_b, own, position, mixer, offset)
 
 
 def solution(mesh):

time: 20.7 us -> 20.9 us (level)
  Pallas kernels: 7.66 us -> 8.4 us
  starting transfers between devices: 10.4 us -> 9.67 us
    pallas_call x2, Pallas kernels: 1.59 us -> 3.21 us  [the longest x1 3.07 us: on_device(): pl.pallas_call(functools.partial(edge_kernel, lon_count), out_shape=(edge...]
    ppermute x1, starting transfers between devices: 6.04 us -> 4.54 us  [on_device(): got_b = lax.ppermute(pay_b, 'lon', lon_second)]
    pallas_call x1, Pallas kernels: 2.29 us -> 1.42 us  [on_device(): pl.pallas_call(functools.partial(prepare_kernel, lon_count, lat_len), out...]
    ppermute x1, starting transfers between devices: 2.77 us -> 3.4 us  [on_device(): core_b = lax.ppermute(core_b, 'lon', lon_second)]
    ppermute x1, waiting for transfers between devices: 0.63 us -> 0.01 us  [on_device(): core_a = lax.ppermute(core_a, 'lon', lon_first)]
    ppermute x1, waiting for transfers between devices: 1.34 us -> 1.78 us  [on_device(): got_a = lax.ppermute(pay_a, 'lon', lon_first)]
    ppermute x1, waiting for transfers between devices: 0.01 us -> 0.43 us  [on_device(): got_b = lax.ppermute(pay_b, 'lon', lon_second)]
  transfers between devices with their start and end apart: 6 -> 6, of which waited for: 4 -> 3; matrix products, arithmetic and copies ran while one was open for 0% -> 0% of each run, Pallas kernels for 22% -> 18%
where the time goes in v5:
time: 20.9 us; the launch traced here: 20.7 us
  starting transfers between devices  9.67 us (46%)
  Pallas kernels  8.4 us (40%)
  waiting for transfers between devices  2.56 us (12%)
    ppermute x1, starting transfers between devices, on_device(): got_b = lax.ppermute(pay_b, 'lon', lon_second)  4.54 us
    ppermute x1, starting transfers between devices, on_device(): core_b = lax.ppermute(core_b, 'lon', lon_second)  3.4 us
    pallas_call x1, Pallas kernels, on_device(): pl.pallas_call(functools.partial(edge_kernel, lon_count), out_shape=(edge...  3.07 us
    ppermute x1, waiting for transfers between devices, on_device(): got_a = lax.ppermute(pay_a, 'lon', lon_first)  1.78 us
    ppermute x1, starting transfers between devices, on_device(): row_a = lax.ppermute(row_a, 'lat', lat_first)  1.63 us
    pallas_call x1, Pallas kernels, on_device(): pl.pallas_call(mix_kernel, out_shape=jax.ShapeDtypeStruct(out_shape, BF16...  1.54 us
    pallas_call x1, Pallas kernels, on_device(): pl.pallas_call(functools.partial(inner_kernel, lat_len), out_shape=(jax.S...  1.46 us
    pallas_call x1, Pallas kernels, on_device(): pl.pallas_call(functools.partial(prepare_kernel, lon_count, lat_len), out...  1.42 us
  transfers between devices with their start and end apart: 6, of which 3 were waited for; matrix products, arithmetic and copies ran while one was open for 0% of the time, Pallas kernels for 18%

profile of v5, /device:TPU:0, one launch (start us, length us, event | category | flops | bytes accessed | tf_op | source)
XLA Modules:
  0.0 20.7 jit_solution(12598884661634056565)
XLA Ops:
  0.0 3.1 %shard_map.91 = (bf16[32,128]{1,0:T(8,128)(2,1)S(1)}, bf16[32,128]{1,0:T(8,128)(2,1)S(1)}, bf16[112,32,512]{2,1,0:T(8,128)(2,1)S(1)}, bf16[2,32,512]{2,1,0:T(8,1...) custom-call(s32[1,1,6]{2,1,0:T(1,128)} %refs_0_.3, ...), custom_call_target="tpu_custom_call" | custom-call | tf_op jit(solution)/shard_map/pallas_call | solution.py:461
  3.1 4.5 %collective-permute-start = (bf16[32,128]{1,0:T(8,128)(2,1)S(1)}, bf16[32,128]{1,0:T(8,128)(2,1)S(1)}, u32[]{:S(2)}, u32[]{:S(2)}) collective-permute-start(bf16[32,128]{1,0:T(8,128)(2,1)S(1)} %get-tuple-element.33), channel_id=1, source_target_pairs={{0,7},{1,2},{2,1},{3,4},{4,3},{5,6},{6,5},{7,0},{8,15},{9,10},{10,... | collective-permute-start | bytes 24584 | tf_op jit(solution)/shard_map/ppermute | solution.py:475
  7.6 0.0 collective-permute-start.1
  7.6 1.4 %shard_map.92 = (bf16[32,2048]{1,0:T(8,128)(2,1)S(1)}, bf16[112,32,512]{2,1,0:T(8,128)(2,1)S(1)}, bf16[2,32,512]{2,1,0:T(8,128)(2,1)S(1)}, s32[16,128]{1,0:T(8,1...) custom-call(s32[1,1,6]{2,1,0:T(1,128)} %refs_0_.3, s32[896]{0:T(1024)} %refs_1_.3, ...), custom_call_target="tpu_custom_call" | custom-call | flops 1000000 | bytes 7340032 | tf_op jit(solution)/shard_map/pallas_call | solution.py:477
  9.1 0.4 %collective-permute-done.got_b_ref = bf16[32,128]{1,0:T(8,128)(2,1)S(1)} collective-permute-done((bf16[32,128]{1,0:T(8,128)(2,1)S(1)}, bf16[32,128]{1,0:T(8,128)(2,1)S(1)}, u32[]{:S(2)}, u32[]{:S(2)}) %collective-permute-start) | collective-permute-done | bytes 8224 | tf_op jit(solution)/shard_map/ppermute | solution.py:475
  9.5 1.8 %collective-permute-done.1.got_a_ref = bf16[32,128]{1,0:T(8,128)(2,1)S(1)} collective-permute-done((bf16[32,128]{1,0:T(8,128)(2,1)S(1)}, bf16[32,128]{1,0:T(8,128)(2,1)S(1)}, u32[]{:S(2)}, u32[]{:S(2)}) %collective-permute-start.1) | collective-permute-done | bytes 8224 | tf_op jit(solution)/shard_map/ppermute | solution.py:476
  11.3 0.1 shard_map.93
  11.4 0.1 collective-permute-start.4
  11.5 3.4 %collective-permute-start.5 = (bf16[2,32,512]{2,1,0:T(8,128)(2,1)S(1)}, bf16[2,32,512]{2,1,0:T(8,128)(2,1)S(1)}, u32[]{:S(2)}, u32[]{:S(2)}) collective-permute-start(bf16[2,32,512]{2,1,0:T(8,128)(2,1)S(1)} %get-tuple-element.37.core_ref), channel_id=1, source_target_pairs={{0,7},{1,2},{2,1},{3,4},{4,3},{5,6},{6,5},{7,0},{8,15},{9,10},{10,... | collective-permute-start | bytes 196616 | tf_op jit(solution)/shard_map/ppermute | solution.py:507
  14.9 0.1 shard_map.94
  15.0 0.0 collective-permute-start.2
  15.0 1.6 %collective-permute-start.3 = (bf16[32,384]{1,0:T(8,128)(2,1)S(1)}, bf16[32,384]{1,0:T(8,128)(2,1)S(1)}, u32[]{:S(2)}, u32[]{:S(2)}) collective-permute-start(bf16[32,384]{1,0:T(8,128)(2,1)S(1)} %get-tuple-element.42), channel_id=1, source_target_pairs={{0,8},{8,0},{16,24},{24,16},{1,9},{9,1},{17,25},{25,17},{2,10},{10... | collective-permute-start | bytes 73736 | tf_op jit(solution)/shard_map/ppermute | solution.py:509
  16.7 1.5 %shard_map.95 = (bf16[512,1536]{1,0:T(8,128)(2,1)S(1)}, bf16[2,400,512]{2,1,0:T(8,128)(2,1)S(1)}) custom-call(bf16[32,2048]{1,0:T(8,128)(2,1)S(1)} %get-tuple-element.32.red_ref, bf16[32,128]{1,0:T(8,128)(2,1)S(1)} %get-tuple-element.38.edge_ref, bf16[256,400]{1,0:T(8,128)(2,1)S(1)} %get-tuple-element.39.weights_ref), custom_call_target="tpu_custom_call" | custom-call | tf_op jit(solution)/shard_map/pallas_call | solution.py:514
  18.1 0.3 %collective-permute-done.2.row_b_ref = bf16[32,384]{1,0:T(8,128)(2,1)S(1)} collective-permute-done((bf16[32,384]{1,0:T(8,128)(2,1)S(1)}, bf16[32,384]{1,0:T(8,128)(2,1)S(1)}, u32[]{:S(2)}, u32[]{:S(2)}) %collective-permute-start.2) | collective-permute-done | bytes 24608 | tf_op jit(solution)/shard_map/ppermute | solution.py:510
  18.5 0.0 collective-permute-done.3.row_a_ref
  18.5 0.6 %shard_map.96.border_ref = bf16[512,512]{1,0:T(8,128)(2,1)S(1)} custom-call(bf16[32,384]{1,0:T(8,128)(2,1)S(1)} %collective-permute-done.2.row_b_ref, bf16[32,384]{1,0:T(8,128)(2,1)S(1)} %collective-permute-done.3.row_a_ref, bf16[256,400]{1,0:T(8,128)(2,1)S(1)} %get-tuple-element.39.weights_ref, bf16[2,400,512]{2,1,0:T(8,128)(2,1)S(1)} %get-tuple-element.43.own_stack_ref), custom_call_target="tpu_custom_call" | custom-call | tf_op jit(solution)/shard_map/pallas_call | solution.py:522
  19.1 0.0 collective-permute-done.4.core_a_ref
  19.1 0.0 collective-permute-done.5.core_b_ref
  19.1 1.5 %shard_map.97 = bf16[64,16,128]{2,1,0:T(8,128)(2,1)} custom-call(bf16[512,1536]{1,0:T(8,128)(2,1)S(1)} %get-tuple-element.40.inner_ref, bf16[512,512]{1,0:T(8,128)(2,1)S(1)} %shard_map.96.border_ref, bf16[2,32,512]{2,1,0:T(8,128)(2,1)S(1)} %collective-permute-done.4.core_a_ref, bf16[2,32,512]{2,1,0:T(8,128)(2,1)S(1)} %collective-permute-done.5.core_b_ref, ...), custom_call_target="tpu_custom_call" | custom-call | tf_op jit(solution)/shard_map/pallas_call | solution.py:531
Async XLA Ops:
  3.1 6.4 %collective-permute-start = (bf16[32,128]{1,0:T(8,128)(2,1)S(1)}, bf16[32,128]{1,0:T(8,128)(2,1)S(1)}, u32[]{:S(2)}, u32[]{:S(2)}) collective-permute-start(bf16[32,128]{1,0:T(8,128)(2,1)S(1)} %get-tuple-element.33), channel_id=1, source_target_pairs={{0,7},{1,2},{2,1},{3,4},{4,3},{5,6},{6,5},{7,0},{8,15},{9,10},{10,... | collective-permute-start | bytes 24584 | tf_op jit(solution)/shard_map/ppermute | solution.py:475
  7.6 3.7 %collective-permute-start.1 = (bf16[32,128]{1,0:T(8,128)(2,1)S(1)}, bf16[32,128]{1,0:T(8,128)(2,1)S(1)}, u32[]{:S(2)}, u32[]{:S(2)}) collective-permute-start(bf16[32,128]{1,0:T(8,128)(2,1)S(1)} %get-tuple-element.34), channel_id=1, source_target_pairs={{0,1},{1,0},{2,3},{3,2},{4,5},{5,4},{6,7},{7,6},{8,9},{9,8},{10,11... | collective-permute-start | bytes 24584 | tf_op jit(solution)/shard_map/ppermute | solution.py:476
  11.4 7.7 %collective-permute-start.4 = (bf16[2,32,512]{2,1,0:T(8,128)(2,1)S(1)}, bf16[2,32,512]{2,1,0:T(8,128)(2,1)S(1)}, u32[]{:S(2)}, u32[]{:S(2)}) collective-permute-start(bf16[2,32,512]{2,1,0:T(8,128)(2,1)S(1)} %get-tuple-element.44), channel_id=1, source_target_pairs={{0,1},{1,0},{2,3},{3,2},{4,5},{5,4},{6,7},{7,6},{8,9},{9,8},{10,11... | collective-permute-start | bytes 196616 | tf_op jit(solution)/shard_map/ppermute | solution.py:508
  11.5 7.6 %collective-permute-start.5 = (bf16[2,32,512]{2,1,0:T(8,128)(2,1)S(1)}, bf16[2,32,512]{2,1,0:T(8,128)(2,1)S(1)}, u32[]{:S(2)}, u32[]{:S(2)}) collective-permute-start(bf16[2,32,512]{2,1,0:T(8,128)(2,1)S(1)} %get-tuple-element.37.core_ref), channel_id=1, source_target_pairs={{0,7},{1,2},{2,1},{3,4},{4,3},{5,6},{6,5},{7,0},{8,15},{9,10},{10,... | collective-permute-start | bytes 196616 | tf_op jit(solution)/shard_map/ppermute | solution.py:507
  15.0 3.4 %collective-permute-start.2 = (bf16[32,384]{1,0:T(8,128)(2,1)S(1)}, bf16[32,384]{1,0:T(8,128)(2,1)S(1)}, u32[]{:S(2)}, u32[]{:S(2)}) collective-permute-start(bf16[32,384]{1,0:T(8,128)(2,1)S(1)} %get-tuple-element.41), channel_id=1, source_target_pairs={{0,24},{8,16},{16,8},{24,0},{1,25},{9,17},{17,9},{25,1},{2,26},{10... | collective-permute-start | bytes 73736 | tf_op jit(solution)/shard_map/ppermute | solution.py:510
  15.0 3.4 %collective-permute-start.3 = (bf16[32,384]{1,0:T(8,128)(2,1)S(1)}, bf16[32,384]{1,0:T(8,128)(2,1)S(1)}, u32[]{:S(2)}, u32[]{:S(2)}) collective-permute-start(bf16[32,384]{1,0:T(8,128)(2,1)S(1)} %get-tuple-element.42), channel_id=1, source_target_pairs={{0,8},{8,0},{16,24},{24,16},{1,9},{9,1},{17,25},{25,17},{2,10},{10... | collective-permute-start | bytes 73736 | tf_op jit(solution)/shard_map/ppermute | solution.py:509

commit v6 on v5

--- a/solution.py
+++ b/solution.py
@@ -17,6 +17,7 @@
 OUT_COPIES = 4
 IN_COPIES = 4
 BANK_COPIES = 8
+EARLY = 2
 F32 = jnp.float32
 BF16 = jnp.bfloat16
 VMEM = pl.BlockSpec(memory_space=pltpu.VMEM)
@@ -71,6 +72,10 @@
     return places, rows
 
 
+def is_early():
+    return lax.axis_index("lon") < EARLY
+
+
 class Held:
     names = ("bank", "own", "position", "weights", "mixer", "offset")
     sources = ("labels", "tap", "out_factor", "bias")
@@ -147,16 +152,9 @@
     held = Held(held_refs)
     channels, lat_len, lon_len = feat_ref.shape
     rank = in_ref.shape[0]
-    early = lax.axis_index("lon") != lon_count - 1
     pairs = in_parts(feat_hbm, feat_ref, IN_COPIES)
     pairs += ((slot_hbm, slot_ref), (list_hbm, list_ref), (in_hbm, in_ref))
-    copies = start_copies(pairs, sems)
-
-    @pl.when(early)
-    def _():
-        start_sources(sources, targets, bank_hbm, held.bank, held_sems)
-
-    for copy in copies:
+    for copy in start_copies(pairs, sems):
         copy.wait()
     lane = lane_index((lat_len, LANES))
     batch = LANES // EDGE
@@ -181,11 +179,10 @@
             load = jnp.where(lane == EDGE * lat_len + nth, row, load)
         out_ref[...] = load.astype(BF16)
 
-    @pl.when(early)
+    @pl.when(is_early())
     def _():
-        pairs = tuple(zip(sources, targets)) + in_parts(bank_hbm, held.bank, BANK_COPIES)
-        waits = [pltpu.make_async_copy(source, target, held_sems.at[i]) for i, (source, target) in enumerate(pairs)]
-        build_held(lon_count, list_ref, slot_ref, targets, waits, held)
+        copies = start_sources(sources, targets, bank_hbm, held.bank, held_sems)
+        build_held(lon_count, list_ref, slot_ref, targets, copies, held)
 
 
 def prepare_kernel(lon_count, lat_len, *refs):
@@ -194,7 +191,7 @@
     red_ref, held = refs[14], Held(refs[15:21])
     list_ref, slot_ref, feat_ref, in_ref, rows_ref = refs[21:26]
     targets, sems, held_sems = refs[26:30], refs[30], refs[31]
-    early = lax.axis_index("lon") != lon_count - 1
+    early = is_early()
     pairs = in_parts(feat_hbm, feat_ref, IN_COPIES) + ((in_hbm, in_ref),)
     copies = start_copies(pairs, sems)
     late_pairs = ((slot_hbm, slot_ref), (list_hbm, list_ref))
@@ -228,8 +225,8 @@
         build_held(lon_count, list_ref, slot_ref, targets, waits[2:], held)
 
 
-def pick_kernel(lon_count, lat_len, got_b_ref, got_a_ref, early_bank_ref, late_bank_ref, core_a_ref, core_b_ref):
-    early = lax.axis_index("lon") != lon_count - 1
+def pick_kernel(lat_len, got_b_ref, got_a_ref, early_bank_ref, late_bank_ref, core_a_ref, core_b_ref):
+    early = is_early()
     lane = lane_index((1, LANES))
     for got_ref, core_ref in ((got_b_ref, core_b_ref), (got_a_ref, core_a_ref)):
         head = got_ref[...].astype(F32)[0:1, :]
@@ -491,7 +488,7 @@
     )(*sources, *given)
     row_shape = jax.ShapeDtypeStruct((rank, REACH * lon_len + LANES), BF16)
     core_a, core_b = pl.pallas_call(
-        functools.partial(pick_kernel, lon_count, lat_len),
+        functools.partial(pick_kernel, lat_len),
         out_shape=(core_shape, core_shape),
         in_specs=[VMEM] * 4,
         out_specs=(VMEM,) * 2,

time: 20.9 us -> 20.8 us (level)
  Pallas kernels: 8.4 us -> 8.96 us
  starting transfers between devices: 9.67 us -> 9.28 us
  waiting for transfers between devices: 2.56 us -> 2.23 us
    ppermute x1, starting transfers between devices: 0.01 us -> 0.66 us  [on_device(): row_b = lax.ppermute(row_b, 'lat', lat_second)]
    ppermute x1, starting transfers between devices: 3.4 us -> 2.77 us  [on_device(): core_b = lax.ppermute(core_b, 'lon', lon_second)]
    ppermute x1, waiting for transfers between devices: 0.43 us -> 1 us  [on_device(): got_b = lax.ppermute(pay_b, 'lon', lon_second)]
    ppermute x1, waiting for transfers between devices: 1.78 us -> 1.23 us  [on_device(): got_a = lax.ppermute(pay_a, 'lon', lon_first)]
    ppermute x1, starting transfers between devices: 4.54 us -> 3.99 us  [on_device(): got_b = lax.ppermute(pay_b, 'lon', lon_second)]
    pallas_call x1, Pallas kernels: 3.07 us -> 3.62 us  [on_device(): pl.pallas_call(functools.partial(edge_kernel, lon_count), out_shape=(edge...]
    ppermute x1, waiting for transfers between devices: 0.34 us -> 0.01 us  [on_device(): row_b = lax.ppermute(row_b, 'lat', lat_second)]
  transfers between devices with their start and end apart: 6 -> 6, of which waited for: 3 -> 2; matrix products, arithmetic and copies ran while one was open for 0% -> 0% of each run, Pallas kernels for 18% -> 18%
where the time goes in v6:
time: 20.8 us; the launch traced here: 20.5 us
  starting transfers between devices  9.28 us (45%)
  Pallas kernels  8.96 us (43%)
  waiting for transfers between devices  2.23 us (11%)
    ppermute x1, starting transfers between devices, on_device(): got_b = lax.ppermute(pay_b, 'lon', lon_second)  3.99 us
    pallas_call x1, Pallas kernels, on_device(): pl.pallas_call(functools.partial(edge_kernel, lon_count), out_shape=(edge...  3.62 us
    ppermute x1, starting transfers between devices, on_device(): core_b = lax.ppermute(core_b, 'lon', lon_second)  2.77 us
    ppermute x1, starting transfers between devices, on_device(): row_a = lax.ppermute(row_a, 'lat', lat_first)  1.8 us
    pallas_call x1, Pallas kernels, on_device(): pl.pallas_call(mix_kernel, out_shape=jax.ShapeDtypeStruct(out_shape, BF16...  1.54 us
    pallas_call x1, Pallas kernels, on_device(): pl.pallas_call(functools.partial(inner_kernel, lat_len), out_shape=(jax.S...  1.46 us
    pallas_call x1, Pallas kernels, on_device(): pl.pallas_call(functools.partial(prepare_kernel, lon_count, lat_len), out...  1.42 us
    ppermute x1, waiting for transfers between devices, on_device(): got_a = lax.ppermute(pay_a, 'lon', lon_first)  1.23 us
  transfers between devices with their start and end apart: 6, of which 2 were waited for; matrix products, arithmetic and copies ran while one was open for 0% of the time, Pallas kernels for 18%

profile of v6, /device:TPU:0, one launch (start us, length us, event | category | flops | bytes accessed | tf_op | source)
XLA Modules:
  0.0 20.5 jit_solution(16230192585503972083)
XLA Ops:
  0.0 3.6 %shard_map.91 = (bf16[32,128]{1,0:T(8,128)(2,1)S(1)}, bf16[32,128]{1,0:T(8,128)(2,1)S(1)}, bf16[112,32,512]{2,1,0:T(8,128)(2,1)S(1)}, bf16[2,32,512]{2,1,0:T(8,1...) custom-call(s32[1,1,6]{2,1,0:T(1,128)} %refs_0_.3, ...), custom_call_target="tpu_custom_call" | custom-call | tf_op jit(solution)/shard_map/pallas_call | solution.py:458
  3.6 4.0 %collective-permute-start = (bf16[32,128]{1,0:T(8,128)(2,1)S(1)}, bf16[32,128]{1,0:T(8,128)(2,1)S(1)}, u32[]{:S(2)}, u32[]{:S(2)}) collective-permute-start(bf16[32,128]{1,0:T(8,128)(2,1)S(1)} %get-tuple-element.33), channel_id=1, source_target_pairs={{0,7},{1,2},{2,1},{3,4},{4,3},{5,6},{6,5},{7,0},{8,15},{9,10},{10,... | collective-permute-start | bytes 24584 | tf_op jit(solution)/shard_map/ppermute | solution.py:472
  7.6 0.0 collective-permute-start.1
  7.6 1.4 %shard_map.92 = (bf16[32,2048]{1,0:T(8,128)(2,1)S(1)}, bf16[112,32,512]{2,1,0:T(8,128)(2,1)S(1)}, bf16[2,32,512]{2,1,0:T(8,128)(2,1)S(1)}, s32[16,128]{1,0:T(8,1...) custom-call(s32[1,1,6]{2,1,0:T(1,128)} %refs_0_.3, s32[896]{0:T(1024)} %refs_1_.3, ...), custom_call_target="tpu_custom_call" | custom-call | flops 1000000 | bytes 7340032 | tf_op jit(solution)/shard_map/pallas_call | solution.py:474
  9.0 1.0 %collective-permute-done.got_b_ref = bf16[32,128]{1,0:T(8,128)(2,1)S(1)} collective-permute-done((bf16[32,128]{1,0:T(8,128)(2,1)S(1)}, bf16[32,128]{1,0:T(8,128)(2,1)S(1)}, u32[]{:S(2)}, u32[]{:S(2)}) %collective-permute-start) | collective-permute-done | bytes 8224 | tf_op jit(solution)/shard_map/ppermute | solution.py:472
  10.0 1.2 %collective-permute-done.1.got_a_ref = bf16[32,128]{1,0:T(8,128)(2,1)S(1)} collective-permute-done((bf16[32,128]{1,0:T(8,128)(2,1)S(1)}, bf16[32,128]{1,0:T(8,128)(2,1)S(1)}, u32[]{:S(2)}, u32[]{:S(2)}) %collective-permute-start.1) | collective-permute-done | bytes 8224 | tf_op jit(solution)/shard_map/ppermute | solution.py:473
  11.3 0.1 shard_map.93
  11.4 0.1 collective-permute-start.4
  11.5 2.8 %collective-permute-start.5 = (bf16[2,32,512]{2,1,0:T(8,128)(2,1)S(1)}, bf16[2,32,512]{2,1,0:T(8,128)(2,1)S(1)}, u32[]{:S(2)}, u32[]{:S(2)}) collective-permute-start(bf16[2,32,512]{2,1,0:T(8,128)(2,1)S(1)} %get-tuple-element.37.core_ref), channel_id=1, source_target_pairs={{0,7},{1,2},{2,1},{3,4},{4,3},{5,6},{6,5},{7,0},{8,15},{9,10},{10,... | collective-permute-start | bytes 196616 | tf_op jit(solution)/shard_map/ppermute | solution.py:504
  14.3 0.1 shard_map.94
  14.4 0.7 %collective-permute-start.2 = (bf16[32,384]{1,0:T(8,128)(2,1)S(1)}, bf16[32,384]{1,0:T(8,128)(2,1)S(1)}, u32[]{:S(2)}, u32[]{:S(2)}) collective-permute-start(bf16[32,384]{1,0:T(8,128)(2,1)S(1)} %get-tuple-element.41), channel_id=1, source_target_pairs={{0,24},{8,16},{16,8},{24,0},{1,25},{9,17},{17,9},{25,1},{2,26},{10... | collective-permute-start | bytes 73736 | tf_op jit(solution)/shard_map/ppermute | solution.py:507
  15.1 1.8 %collective-permute-start.3 = (bf16[32,384]{1,0:T(8,128)(2,1)S(1)}, bf16[32,384]{1,0:T(8,128)(2,1)S(1)}, u32[]{:S(2)}, u32[]{:S(2)}) collective-permute-start(bf16[32,384]{1,0:T(8,128)(2,1)S(1)} %get-tuple-element.42), channel_id=1, source_target_pairs={{0,8},{8,0},{16,24},{24,16},{1,9},{9,1},{17,25},{25,17},{2,10},{10... | collective-permute-start | bytes 73736 | tf_op jit(solution)/shard_map/ppermute | solution.py:506
  16.9 1.5 %shard_map.95 = (bf16[512,1536]{1,0:T(8,128)(2,1)S(1)}, bf16[2,400,512]{2,1,0:T(8,128)(2,1)S(1)}) custom-call(bf16[32,2048]{1,0:T(8,128)(2,1)S(1)} %get-tuple-element.32.red_ref, bf16[32,128]{1,0:T(8,128)(2,1)S(1)} %get-tuple-element.38.edge_ref, bf16[256,400]{1,0:T(8,128)(2,1)S(1)} %get-tuple-element.39.weights_ref), custom_call_target="tpu_custom_call" | custom-call | tf_op jit(solution)/shard_map/pallas_call | solution.py:511
  18.3 0.0 collective-permute-done.2.row_b_ref
  18.3 0.0 collective-permute-done.3.row_a_ref
  18.3 0.6 %shard_map.96.border_ref = bf16[512,512]{1,0:T(8,128)(2,1)S(1)} custom-call(bf16[32,384]{1,0:T(8,128)(2,1)S(1)} %collective-permute-done.2.row_b_ref, bf16[32,384]{1,0:T(8,128)(2,1)S(1)} %collective-permute-done.3.row_a_ref, bf16[256,400]{1,0:T(8,128)(2,1)S(1)} %get-tuple-element.39.weights_ref, bf16[2,400,512]{2,1,0:T(8,128)(2,1)S(1)} %get-tuple-element.43.own_stack_ref), custom_call_target="tpu_custom_call" | custom-call | tf_op jit(solution)/shard_map/pallas_call | solution.py:519
  19.0 0.0 collective-permute-done.4.core_a_ref
  19.0 0.0 collective-permute-done.5.core_b_ref
  19.0 1.5 %shard_map.97 = bf16[64,16,128]{2,1,0:T(8,128)(2,1)} custom-call(bf16[512,1536]{1,0:T(8,128)(2,1)S(1)} %get-tuple-element.40.inner_ref, bf16[512,512]{1,0:T(8,128)(2,1)S(1)} %shard_map.96.border_ref, bf16[2,32,512]{2,1,0:T(8,128)(2,1)S(1)} %collective-permute-done.4.core_a_ref, bf16[2,32,512]{2,1,0:T(8,128)(2,1)S(1)} %collective-permute-done.5.core_b_ref, ...), custom_call_target="tpu_custom_call" | custom-call | tf_op jit(solution)/shard_map/pallas_call | solution.py:528
Async XLA Ops:
  3.6 6.4 %collective-permute-start = (bf16[32,128]{1,0:T(8,128)(2,1)S(1)}, bf16[32,128]{1,0:T(8,128)(2,1)S(1)}, u32[]{:S(2)}, u32[]{:S(2)}) collective-permute-start(bf16[32,128]{1,0:T(8,128)(2,1)S(1)} %get-tuple-element.33), channel_id=1, source_target_pairs={{0,7},{1,2},{2,1},{3,4},{4,3},{5,6},{6,5},{7,0},{8,15},{9,10},{10,... | collective-permute-start | bytes 24584 | tf_op jit(solution)/shard_map/ppermute | solution.py:472
  7.6 3.7 %collective-permute-start.1 = (bf16[32,128]{1,0:T(8,128)(2,1)S(1)}, bf16[32,128]{1,0:T(8,128)(2,1)S(1)}, u32[]{:S(2)}, u32[]{:S(2)}) collective-permute-start(bf16[32,128]{1,0:T(8,128)(2,1)S(1)} %get-tuple-element.34), channel_id=1, source_target_pairs={{0,1},{1,0},{2,3},{3,2},{4,5},{5,4},{6,7},{7,6},{8,9},{9,8},{10,11... | collective-permute-start | bytes 24584 | tf_op jit(solution)/shard_map/ppermute | solution.py:473
  11.4 7.6 %collective-permute-start.4 = (bf16[2,32,512]{2,1,0:T(8,128)(2,1)S(1)}, bf16[2,32,512]{2,1,0:T(8,128)(2,1)S(1)}, u32[]{:S(2)}, u32[]{:S(2)}) collective-permute-start(bf16[2,32,512]{2,1,0:T(8,128)(2,1)S(1)} %get-tuple-element.44), channel_id=1, source_target_pairs={{0,1},{1,0},{2,3},{3,2},{4,5},{5,4},{6,7},{7,6},{8,9},{9,8},{10,11... | collective-permute-start | bytes 196616 | tf_op jit(solution)/shard_map/ppermute | solution.py:505
  11.5 7.5 %collective-permute-start.5 = (bf16[2,32,512]{2,1,0:T(8,128)(2,1)S(1)}, bf16[2,32,512]{2,1,0:T(8,128)(2,1)S(1)}, u32[]{:S(2)}, u32[]{:S(2)}) collective-permute-start(bf16[2,32,512]{2,1,0:T(8,128)(2,1)S(1)} %get-tuple-element.37.core_ref), channel_id=1, source_target_pairs={{0,7},{1,2},{2,1},{3,4},{4,3},{5,6},{6,5},{7,0},{8,15},{9,10},{10,... | collective-permute-start | bytes 196616 | tf_op jit(solution)/shard_map/ppermute | solution.py:504
  14.4 3.9 %collective-permute-start.2 = (bf16[32,384]{1,0:T(8,128)(2,1)S(1)}, bf16[32,384]{1,0:T(8,128)(2,1)S(1)}, u32[]{:S(2)}, u32[]{:S(2)}) collective-permute-start(bf16[32,384]{1,0:T(8,128)(2,1)S(1)} %get-tuple-element.41), channel_id=1, source_target_pairs={{0,24},{8,16},{16,8},{24,0},{1,25},{9,17},{17,9},{25,1},{2,26},{10... | collective-permute-start | bytes 73736 | tf_op jit(solution)/shard_map/ppermute | solution.py:507
  15.1 3.3 %collective-permute-start.3 = (bf16[32,384]{1,0:T(8,128)(2,1)S(1)}, bf16[32,384]{1,0:T(8,128)(2,1)S(1)}, u32[]{:S(2)}, u32[]{:S(2)}) collective-permute-start(bf16[32,384]{1,0:T(8,128)(2,1)S(1)} %get-tuple-element.42), channel_id=1, source_target_pairs={{0,8},{8,0},{16,24},{24,16},{1,9},{9,1},{17,25},{25,17},{2,10},{10... | collective-permute-start | bytes 73736 | tf_op jit(solution)/shard_map/ppermute | solution.py:506

commit v7 on v6

--- a/solution.py
+++ b/solution.py
@@ -17,7 +17,7 @@
 OUT_COPIES = 4
 IN_COPIES = 4
 BANK_COPIES = 8
-EARLY = 2
+EARLY = 1
 F32 = jnp.float32
 BF16 = jnp.bfloat16
 VMEM = pl.BlockSpec(memory_space=pltpu.VMEM)
@@ -73,7 +73,7 @@
 
 
 def is_early():
-    return lax.axis_index("lon") < EARLY
+    return lax.axis_index("lon") == EARLY
 
 
 class Held:
@@ -91,8 +91,6 @@
 
 def build_held(lon_count, list_ref, slot_ref, targets, copies, held):
     labels_ref, tap_ref, out_factor_ref, bias_ref = targets
-    for copy in copies[: len(targets)]:
-        copy.wait()
     places, rows = find_rows(list_ref, slot_ref, lon_count, held.bank.shape[0])
     even = (lax.axis_index("lon") % 2) == 0
     order = list(places[0])
@@ -138,7 +136,7 @@
     mine = lax.broadcasted_iota(jnp.int32, shape, 0) // GROUP == lane_index(shape)
     offset = jnp.sum(jnp.where(mine, bias_ref[...], 0.0), axis=1, keepdims=True)
     held.offset[...] = jnp.broadcast_to(offset, held.offset.shape)
-    for copy in copies[len(targets) :]:
+    for copy in copies:
         copy.wait()
     for nth in range(PER_OWNER):
         held.own[nth] = held.bank[rows[0][nth]]
@@ -182,7 +180,18 @@
     @pl.when(is_early())
     def _():
         copies = start_sources(sources, targets, bank_hbm, held.bank, held_sems)
-        build_held(lon_count, list_ref, slot_ref, targets, copies, held)
+        for copy in copies[: len(targets)]:
+            copy.wait()
+        build_held(lon_count, list_ref, slot_ref, targets, copies[len(targets) :], held)
+
+
+def reduce_tile(lat_len, feat_ref, in_ref, rows_ref, red_ref):
+    channels, lon_len = feat_ref.shape[0], feat_ref.shape[2]
+    rows_ref[...] = feat_ref[...].astype(F32).reshape(channels * lat_len, lon_len)
+    cells = jnp.concatenate(
+        [rows_ref[pl.ds(p, channels, stride=lat_len), :].astype(BF16) for p in range(lat_len)], axis=1
+    )
+    red_ref[...] = jnp.dot(in_ref[...], cells, preferred_element_type=F32).astype(BF16)
 
 
 def prepare_kernel(lon_count, lat_len, *refs):
@@ -192,37 +201,26 @@
     list_ref, slot_ref, feat_ref, in_ref, rows_ref = refs[21:26]
     targets, sems, held_sems = refs[26:30], refs[30], refs[31]
     early = is_early()
-    pairs = in_parts(feat_hbm, feat_ref, IN_COPIES) + ((in_hbm, in_ref),)
-    copies = start_copies(pairs, sems)
-    late_pairs = ((slot_hbm, slot_ref), (list_hbm, list_ref))
-    late_pairs += tuple(zip(sources, targets)) + in_parts(bank_hbm, held.bank, BANK_COPIES)
+    shared = in_parts(feat_hbm, feat_ref, IN_COPIES) + ((in_hbm, in_ref),)
+    lists = ((slot_hbm, slot_ref), (list_hbm, list_ref))
+
+    @pl.when(early)
+    def _():
+        copies = start_copies(shared, sems)
+        for name in held.names[1:]:
+            getattr(held, name)[...] = getattr(given, name)[...]
+        for copy in copies:
+            copy.wait()
+        reduce_tile(lat_len, feat_ref, in_ref, rows_ref, red_ref)
 
     @pl.when(jnp.logical_not(early))
     def _():
-        start_copies(late_pairs, held_sems)
-
-    @pl.when(early)
-    def _():
-        for name in held.names[1:]:
-            getattr(held, name)[...] = getattr(given, name)[...]
-
-    for copy in copies:
-        copy.wait()
-    channels, lon_len = feat_ref.shape[0], feat_ref.shape[2]
-    rows_ref[...] = feat_ref[...].astype(F32).reshape(channels * lat_len, lon_len)
-    cells = jnp.concatenate(
-        [rows_ref[pl.ds(p, channels, stride=lat_len), :].astype(BF16) for p in range(lat_len)], axis=1
-    )
-    red_ref[...] = jnp.dot(in_ref[...], cells, preferred_element_type=F32).astype(BF16)
-
-    @pl.when(jnp.logical_not(early))
-    def _():
-        waits = [
-            pltpu.make_async_copy(source, target, held_sems.at[i]) for i, (source, target) in enumerate(late_pairs)
-        ]
-        for copy in waits[:2]:
+        copies = start_copies(shared + lists, sems)
+        others = start_sources(sources, targets, bank_hbm, held.bank, held_sems)
+        for copy in copies + others[: len(targets)]:
             copy.wait()
-        build_held(lon_count, list_ref, slot_ref, targets, waits[2:], held)
+        reduce_tile(lat_len, feat_ref, in_ref, rows_ref, red_ref)
+        build_held(lon_count, list_ref, slot_ref, targets, others[len(targets) :], held)
 
 
 def pick_kernel(lat_len, got_b_ref, got_a_ref, early_bank_ref, late_bank_ref, core_a_ref, core_b_ref):
@@ -480,8 +478,8 @@
             *lists,
             pltpu.VMEM((channels * lat_len, lon_len), F32),
             *targets,
-            pltpu.SemaphoreType.DMA((IN_COPIES + 1,)),
-            pltpu.SemaphoreType.DMA((6 + BANK_COPIES,)),
+            pltpu.SemaphoreType.DMA((IN_COPIES + 3,)),
+            pltpu.SemaphoreType.DMA((4 + BANK_COPIES,)),
         ],
         compiler_params=PARAMS,
         cost_estimate=pl.CostEstimate(flops=10**6, bytes_accessed=kernel_bank.size * 4, transcendentals=0),

time: 20.8 us -> 20.2 us (0.971)
  starting transfers between devices: 9.28 us -> 10.5 us
  waiting for transfers between devices: 2.23 us -> 1.24 us
  Pallas kernels: 8.96 us -> 8.24 us
    ppermute x1, starting transfers between devices: 3.99 us -> 6.04 us  [on_device(): got_b = lax.ppermute(pay_b, 'lon', lon_second)]
    pallas_call x1, Pallas kernels: 3.62 us -> 1.57 us  [on_device(): pl.pallas_call(functools.partial(edge_kernel, lon_count), out_shape=(edge...]
    pallas_call x1, Pallas kernels: 1.42 us -> 2.76 us  [on_device(): pl.pallas_call(functools.partial(prepare_kernel, lon_count, lat_len), out...]
    ppermute x1, waiting for transfers between devices: 1 us -> 0.01 us  [on_device(): got_b = lax.ppermute(pay_b, 'lon', lon_second)]
    ppermute x1, starting transfers between devices: 0.66 us -> 0.01 us  [on_device(): row_b = lax.ppermute(row_b, 'lat', lat_second)]
    ppermute x1, waiting for transfers between devices: 1.23 us -> 0.87 us  [on_device(): got_a = lax.ppermute(pay_a, 'lon', lon_first)]
    ppermute x1, waiting for transfers between devices: 0.01 us -> 0.33 us  [on_device(): row_b = lax.ppermute(row_b, 'lat', lat_second)]
  transfers between devices with their start and end apart: 6 -> 6, of which waited for: 2 -> 2; matrix products, arithmetic and copies ran while one was open for 0% -> 0% of each run, Pallas kernels for 18% -> 25%
where the time goes in v7:
time: 20.2 us; the launch traced here: 20.1 us
  starting transfers between devices  10.5 us (52%)
  Pallas kernels  8.24 us (41%)
  waiting for transfers between devices  1.24 us (6%)
    ppermute x1, starting transfers between devices, on_device(): got_b = lax.ppermute(pay_b, 'lon', lon_second)  6.04 us
    ppermute x1, starting transfers between devices, on_device(): core_b = lax.ppermute(core_b, 'lon', lon_second)  2.77 us
    pallas_call x1, Pallas kernels, on_device(): pl.pallas_call(functools.partial(prepare_kernel, lon_count, lat_len), out...  2.76 us
    ppermute x1, starting transfers between devices, on_device(): row_a = lax.ppermute(row_a, 'lat', lat_first)  1.63 us
    pallas_call x1, Pallas kernels, on_device(): pl.pallas_call(functools.partial(edge_kernel, lon_count), out_shape=(edge...  1.57 us
    pallas_call x1, Pallas kernels, on_device(): pl.pallas_call(mix_kernel, out_shape=jax.ShapeDtypeStruct(out_shape, BF16...  1.53 us
    pallas_call x1, Pallas kernels, on_device(): pl.pallas_call(functools.partial(inner_kernel, lat_len), out_shape=(jax.S...  1.47 us
    ppermute x1, waiting for transfers between devices, on_device(): got_a = lax.ppermute(pay_a, 'lon', lon_first)  0.87 us
  transfers between devices with their start and end apart: 6, of which 2 were waited for; matrix products, arithmetic and copies ran while one was open for 0% of the time, Pallas kernels for 25%

profile of v7, /device:TPU:0, one launch (start us, length us, event | category | flops | bytes accessed | tf_op | source)
XLA Modules:
  0.0 20.1 jit_solution(5250088342624955207)
XLA Ops:
  0.0 1.6 %shard_map.91 = (bf16[32,128]{1,0:T(8,128)(2,1)S(1)}, bf16[32,128]{1,0:T(8,128)(2,1)S(1)}, bf16[112,32,512]{2,1,0:T(8,128)(2,1)S(1)}, bf16[2,32,512]{2,1,0:T(8,1...) custom-call(s32[1,1,6]{2,1,0:T(1,128)} %refs_0_.3, ...), custom_call_target="tpu_custom_call" | custom-call | tf_op jit(solution)/shard_map/pallas_call | solution.py:456
  1.6 6.0 %collective-permute-start = (bf16[32,128]{1,0:T(8,128)(2,1)S(1)}, bf16[32,128]{1,0:T(8,128)(2,1)S(1)}, u32[]{:S(2)}, u32[]{:S(2)}) collective-permute-start(bf16[32,128]{1,0:T(8,128)(2,1)S(1)} %get-tuple-element.33), channel_id=1, source_target_pairs={{0,7},{1,2},{2,1},{3,4},{4,3},{5,6},{6,5},{7,0},{8,15},{9,10},{10,... | collective-permute-start | bytes 24584 | tf_op jit(solution)/shard_map/ppermute | solution.py:470
  7.6 0.0 collective-permute-start.1
  7.6 2.8 %shard_map.92 = (bf16[32,2048]{1,0:T(8,128)(2,1)S(1)}, bf16[112,32,512]{2,1,0:T(8,128)(2,1)S(1)}, bf16[2,32,512]{2,1,0:T(8,128)(2,1)S(1)}, s32[16,128]{1,0:T(8,1...) custom-call(s32[1,1,6]{2,1,0:T(1,128)} %refs_0_.3, s32[896]{0:T(1024)} %refs_1_.3, ...), custom_call_target="tpu_custom_call" | custom-call | flops 1000000 | bytes 7340032 | tf_op jit(solution)/shard_map/pallas_call | solution.py:472
  10.4 0.0 collective-permute-done.got_b_ref
  10.4 0.9 %collective-permute-done.1.got_a_ref = bf16[32,128]{1,0:T(8,128)(2,1)S(1)} collective-permute-done((bf16[32,128]{1,0:T(8,128)(2,1)S(1)}, bf16[32,128]{1,0:T(8,128)(2,1)S(1)}, u32[]{:S(2)}, u32[]{:S(2)}) %collective-permute-start.1) | collective-permute-done | bytes 8224 | tf_op jit(solution)/shard_map/ppermute | solution.py:471
  11.3 0.1 shard_map.93
  11.4 0.1 collective-permute-start.4
  11.5 2.8 %collective-permute-start.5 = (bf16[2,32,512]{2,1,0:T(8,128)(2,1)S(1)}, bf16[2,32,512]{2,1,0:T(8,128)(2,1)S(1)}, u32[]{:S(2)}, u32[]{:S(2)}) collective-permute-start(bf16[2,32,512]{2,1,0:T(8,128)(2,1)S(1)} %get-tuple-element.37.core_ref), channel_id=1, source_target_pairs={{0,7},{1,2},{2,1},{3,4},{4,3},{5,6},{6,5},{7,0},{8,15},{9,10},{10,... | collective-permute-start | bytes 196616 | tf_op jit(solution)/shard_map/ppermute | solution.py:502
  14.3 0.1 shard_map.94
  14.4 0.0 collective-permute-start.2
  14.4 1.6 %collective-permute-start.3 = (bf16[32,384]{1,0:T(8,128)(2,1)S(1)}, bf16[32,384]{1,0:T(8,128)(2,1)S(1)}, u32[]{:S(2)}, u32[]{:S(2)}) collective-permute-start(bf16[32,384]{1,0:T(8,128)(2,1)S(1)} %get-tuple-element.42), channel_id=1, source_target_pairs={{0,8},{8,0},{16,24},{24,16},{1,9},{9,1},{17,25},{25,17},{2,10},{10... | collective-permute-start | bytes 73736 | tf_op jit(solution)/shard_map/ppermute | solution.py:504
  16.0 1.5 %shard_map.95 = (bf16[512,1536]{1,0:T(8,128)(2,1)S(1)}, bf16[2,400,512]{2,1,0:T(8,128)(2,1)S(1)}) custom-call(bf16[32,2048]{1,0:T(8,128)(2,1)S(1)} %get-tuple-element.32.red_ref, bf16[32,128]{1,0:T(8,128)(2,1)S(1)} %get-tuple-element.38.edge_ref, bf16[256,400]{1,0:T(8,128)(2,1)S(1)} %get-tuple-element.39.weights_ref), custom_call_target="tpu_custom_call" | custom-call | tf_op jit(solution)/shard_map/pallas_call | solution.py:509
  17.5 0.3 %collective-permute-done.2.row_b_ref = bf16[32,384]{1,0:T(8,128)(2,1)S(1)} collective-permute-done((bf16[32,384]{1,0:T(8,128)(2,1)S(1)}, bf16[32,384]{1,0:T(8,128)(2,1)S(1)}, u32[]{:S(2)}, u32[]{:S(2)}) %collective-permute-start.2) | collective-permute-done | bytes 24608 | tf_op jit(solution)/shard_map/ppermute | solution.py:505
  17.8 0.0 collective-permute-done.3.row_a_ref
  17.8 0.6 %shard_map.96.border_ref = bf16[512,512]{1,0:T(8,128)(2,1)S(1)} custom-call(bf16[32,384]{1,0:T(8,128)(2,1)S(1)} %collective-permute-done.2.row_b_ref, bf16[32,384]{1,0:T(8,128)(2,1)S(1)} %collective-permute-done.3.row_a_ref, bf16[256,400]{1,0:T(8,128)(2,1)S(1)} %get-tuple-element.39.weights_ref, bf16[2,400,512]{2,1,0:T(8,128)(2,1)S(1)} %get-tuple-element.43.own_stack_ref), custom_call_target="tpu_custom_call" | custom-call | tf_op jit(solution)/shard_map/pallas_call | solution.py:517
  18.5 0.0 collective-permute-done.4.core_a_ref
  18.5 0.0 collective-permute-done.5.core_b_ref
  18.5 1.5 %shard_map.97 = bf16[64,16,128]{2,1,0:T(8,128)(2,1)} custom-call(bf16[512,1536]{1,0:T(8,128)(2,1)S(1)} %get-tuple-element.40.inner_ref, bf16[512,512]{1,0:T(8,128)(2,1)S(1)} %shard_map.96.border_ref, bf16[2,32,512]{2,1,0:T(8,128)(2,1)S(1)} %collective-permute-done.4.core_a_ref, bf16[2,32,512]{2,1,0:T(8,128)(2,1)S(1)} %collective-permute-done.5.core_b_ref, ...), custom_call_target="tpu_custom_call" | custom-call | tf_op jit(solution)/shard_map/pallas_call | solution.py:526
Async XLA Ops:
  1.6 8.8 %collective-permute-start = (bf16[32,128]{1,0:T(8,128)(2,1)S(1)}, bf16[32,128]{1,0:T(8,128)(2,1)S(1)}, u32[]{:S(2)}, u32[]{:S(2)}) collective-permute-start(bf16[32,128]{1,0:T(8,128)(2,1)S(1)} %get-tuple-element.33), channel_id=1, source_target_pairs={{0,7},{1,2},{2,1},{3,4},{4,3},{5,6},{6,5},{7,0},{8,15},{9,10},{10,... | collective-permute-start | bytes 24584 | tf_op jit(solution)/shard_map/ppermute | solution.py:470
  7.6 3.7 %collective-permute-start.1 = (bf16[32,128]{1,0:T(8,128)(2,1)S(1)}, bf16[32,128]{1,0:T(8,128)(2,1)S(1)}, u32[]{:S(2)}, u32[]{:S(2)}) collective-permute-start(bf16[32,128]{1,0:T(8,128)(2,1)S(1)} %get-tuple-element.34), channel_id=1, source_target_pairs={{0,1},{1,0},{2,3},{3,2},{4,5},{5,4},{6,7},{7,6},{8,9},{9,8},{10,11... | collective-permute-start | bytes 24584 | tf_op jit(solution)/shard_map/ppermute | solution.py:471
  11.4 7.1 %collective-permute-start.4 = (bf16[2,32,512]{2,1,0:T(8,128)(2,1)S(1)}, bf16[2,32,512]{2,1,0:T(8,128)(2,1)S(1)}, u32[]{:S(2)}, u32[]{:S(2)}) collective-permute-start(bf16[2,32,512]{2,1,0:T(8,128)(2,1)S(1)} %get-tuple-element.44), channel_id=1, source_target_pairs={{0,1},{1,0},{2,3},{3,2},{4,5},{5,4},{6,7},{7,6},{8,9},{9,8},{10,11... | collective-permute-start | bytes 196616 | tf_op jit(solution)/shard_map/ppermute | solution.py:503
  11.5 7.0 %collective-permute-start.5 = (bf16[2,32,512]{2,1,0:T(8,128)(2,1)S(1)}, bf16[2,32,512]{2,1,0:T(8,128)(2,1)S(1)}, u32[]{:S(2)}, u32[]{:S(2)}) collective-permute-start(bf16[2,32,512]{2,1,0:T(8,128)(2,1)S(1)} %get-tuple-element.37.core_ref), channel_id=1, source_target_pairs={{0,7},{1,2},{2,1},{3,4},{4,3},{5,6},{6,5},{7,0},{8,15},{9,10},{10,... | collective-permute-start | bytes 196616 | tf_op jit(solution)/shard_map/ppermute | solution.py:502
  14.4 3.4 %collective-permute-start.2 = (bf16[32,384]{1,0:T(8,128)(2,1)S(1)}, bf16[32,384]{1,0:T(8,128)(2,1)S(1)}, u32[]{:S(2)}, u32[]{:S(2)}) collective-permute-start(bf16[32,384]{1,0:T(8,128)(2,1)S(1)} %get-tuple-element.41), channel_id=1, source_target_pairs={{0,24},{8,16},{16,8},{24,0},{1,25},{9,17},{17,9},{25,1},{2,26},{10... | collective-permute-start | bytes 73736 | tf_op jit(solution)/shard_map/ppermute | solution.py:505
  14.4 3.4 %collective-permute-start.3 = (bf16[32,384]{1,0:T(8,128)(2,1)S(1)}, bf16[32,384]{1,0:T(8,128)(2,1)S(1)}, u32[]{:S(2)}, u32[]{:S(2)}) collective-permute-start(bf16[32,384]{1,0:T(8,128)(2,1)S(1)} %get-tuple-element.42), channel_id=1, source_target_pairs={{0,8},{8,0},{16,24},{24,16},{1,9},{9,1},{17,25},{25,17},{2,10},{10... | collective-permute-start | bytes 73736 | tf_op jit(solution)/shard_map/ppermute | solution.py:504

commit v8 on v7

--- a/solution.py
+++ b/solution.py
@@ -142,12 +142,24 @@
         held.own[nth] = held.bank[rows[0][nth]]
 
 
-def edge_kernel(lon_count, *refs):
-    list_hbm, slot_hbm, feat_hbm, in_hbm, bank_hbm = refs[:5]
-    sources, (pay_a_ref, pay_b_ref), held_refs = refs[5:9], refs[9:11], refs[11:17]
-    list_ref, slot_ref, feat_ref, in_ref, turned_ref = refs[17:22]
-    targets, sems, held_sems = refs[22:26], refs[26], refs[27]
-    held = Held(held_refs)
+def asked_rows(list_ref, slot_ref, owner, held):
+    lane = lane_index((1, LANES))
+    count = list_ref.shape[2]
+    hits = []
+    for i in range(count):
+        region = list_ref[0, 0, i]
+        row = slot_ref[pl.ds(region // LANES, 1), :]
+        hits.append(jnp.where(lane == region % LANES, row - owner * held, -1))
+    local = jnp.max(jnp.concatenate(hits, axis=0), axis=1, keepdims=True)
+    hit = (local >= 0) & (local < held)
+    least = jnp.min(jnp.where(hit, local, held - 1), axis=0, keepdims=True)
+    greatest = jnp.max(jnp.where(hit, local, 0), axis=0, keepdims=True)
+    return least, greatest
+
+
+def edge_kernel(lon_count, held_rows, *refs):
+    list_hbm, slot_hbm, feat_hbm, in_hbm, pay_a_ref, pay_b_ref = refs[:6]
+    list_ref, slot_ref, feat_ref, in_ref, turned_ref, sems = refs[6:]
     channels, lat_len, lon_len = feat_ref.shape
     rank = in_ref.shape[0]
     pairs = in_parts(feat_hbm, feat_ref, IN_COPIES)
@@ -167,20 +179,31 @@
     )
     edges = jnp.dot(in_ref[...], columns, preferred_element_type=F32)
     edges = jnp.concatenate([edges, jnp.zeros((rank, LANES - EDGE * lat_len), F32)], axis=1)
-    _, rows = find_rows(list_ref, slot_ref, lon_count, held.bank.shape[0])
-    even = (lax.axis_index("lon") % 2) == 0
+    me = lax.axis_index("lon")
+    even = (me % 2) == 0
+    prev, following = lax.rem(me + lon_count - 1, lon_count), lax.rem(me + 1, lon_count)
     lane = lane_index((rank, LANES))
-    for out_ref, wanted in ((pay_a_ref, even), (pay_b_ref, jnp.logical_not(even))):
+    for out_ref, owner in (
+        (pay_a_ref, jnp.where(even, following, prev)),
+        (pay_b_ref, jnp.where(even, prev, following)),
+    ):
         load = edges
-        for nth in range(PER_OWNER):
-            row = jnp.where(wanted, rows[2][nth], rows[1][nth]).astype(F32)
-            load = jnp.where(lane == EDGE * lat_len + nth, row, load)
+        for nth, row in enumerate(asked_rows(list_ref, slot_ref, owner, held_rows)):
+            load = jnp.where(lane == EDGE * lat_len + nth, row.astype(F32), load)
         out_ref[...] = load.astype(BF16)
+
+
+def early_kernel(lon_count, *refs):
+    pay_ref, list_hbm, slot_hbm, bank_hbm, sources = *refs[:4], refs[4:8]
+    passed_ref, held = refs[8], Held(refs[9:15])
+    list_ref, slot_ref, targets, sems, held_sems = *refs[15:17], refs[17:21], *refs[21:]
+    passed_ref[...] = pay_ref[...]
 
     @pl.when(is_early())
     def _():
+        lists = start_copies(((list_hbm, list_ref), (slot_hbm, slot_ref)), sems)
         copies = start_sources(sources, targets, bank_hbm, held.bank, held_sems)
-        for copy in copies[: len(targets)]:
+        for copy in lists + copies[: len(targets)]:
             copy.wait()
         build_held(lon_count, list_ref, slot_ref, targets, copies[len(targets) :], held)
 
@@ -453,21 +476,34 @@
             out_bias.reshape(1, -1),
         )
     )
-    pay_a, pay_b, early_bank, *given = pl.pallas_call(
-        functools.partial(edge_kernel, lon_count),
-        out_shape=(edge_shape, edge_shape, *held_shapes),
-        in_specs=[HBM] * 9,
-        out_specs=(VMEM,) * 8,
+    pay_a, pay_b = pl.pallas_call(
+        functools.partial(edge_kernel, lon_count, held),
+        out_shape=(edge_shape, edge_shape),
+        in_specs=[HBM] * 4,
+        out_specs=(VMEM,) * 2,
         scratch_shapes=[
-            *lists,
+            lists[0],
+            pltpu.VMEM((bank_slot.shape[0] // LANES, LANES), jnp.int32),
+            *lists[2:],
             pltpu.VMEM((channels * EDGE, lat_len), F32),
+            pltpu.SemaphoreType.DMA((IN_COPIES + 3,)),
+        ],
+        compiler_params=PARAMS,
+    )(sources[0], in_hbm(bank_slot.reshape(-1, LANES)), *sources[2:4])
+    got_b = lax.ppermute(pay_b, "lon", lon_second)
+    pay_a, early_bank, *given = pl.pallas_call(
+        functools.partial(early_kernel, lon_count),
+        out_shape=(edge_shape, *held_shapes),
+        in_specs=[VMEM] + [HBM] * 7,
+        out_specs=(VMEM,) * 7,
+        scratch_shapes=[
+            *lists[:2],
             *targets,
-            pltpu.SemaphoreType.DMA((IN_COPIES + 3,)),
+            pltpu.SemaphoreType.DMA((2,)),
             pltpu.SemaphoreType.DMA((4 + BANK_COPIES,)),
         ],
         compiler_params=PARAMS,
-    )(*sources)
-    got_b = lax.ppermute(pay_b, "lon", lon_second)
+    )(pay_a, *sources[:2], *sources[4:])
     got_a = lax.ppermute(pay_a, "lon", lon_first)
     reduced, late_bank, own, position, weights, mixer, offset = pl.pallas_call(
         functools.partial(prepare_kernel, lon_count, lat_len),

time: 20.2 us -> 20.8 us (1.030)
  starting transfers between devices: 10.5 us -> 10.9 us
    ppermute x1, starting transfers between devices: 2.77 us -> 2.02 us  [on_device(): core_b = lax.ppermute(core_b, 'lon', lon_second)]
    ppermute x1, waiting for transfers between devices: 0.03 us -> 0.71 us  [on_device(): core_b = lax.ppermute(core_b, 'lon', lon_second)]
    ppermute x1, starting transfers between devices: 0.01 us -> 0.63 us  [on_device(): got_a = lax.ppermute(pay_a, 'lon', lon_first)]
    ppermute x1, waiting for transfers between devices: 0.87 us -> 0.31 us  [on_device(): got_a = lax.ppermute(pay_a, 'lon', lon_first)]
    ppermute x1, starting transfers between devices: 0.07 us -> 0.63 us  [on_device(): core_a = lax.ppermute(core_a, 'lon', lon_first)]
    pallas_call x1 -> x2, Pallas kernels: 1.57 us -> 1.58 us  [the longest x1 1.45 us: on_device(): pl.pallas_call(functools.partial(edge_kernel, lon_count, held), out_shape...]
  transfers between devices with their start and end apart: 6 -> 6, of which waited for: 2 -> 3; matrix products, arithmetic and copies ran while one was open for 0% -> 0% of each run, Pallas kernels for 25% -> 25%
where the time goes in v8:
time: 20.8 us; the launch traced here: 20.6 us
  starting transfers between devices  10.9 us (52%)
  Pallas kernels  8.25 us (40%)
  waiting for transfers between devices  1.37 us (7%)
    ppermute x1, starting transfers between devices, on_device(): got_b = lax.ppermute(pay_b, 'lon', lon_second)  6.04 us
    pallas_call x1, Pallas kernels, on_device(): pl.pallas_call(functools.partial(prepare_kernel, lon_count, lat_len), out...  2.76 us
    ppermute x1, starting transfers between devices, on_device(): core_b = lax.ppermute(core_b, 'lon', lon_second)  2.02 us
    ppermute x1, starting transfers between devices, on_device(): row_a = lax.ppermute(row_a, 'lat', lat_first)  1.63 us
    pallas_call x1, Pallas kernels, on_device(): pl.pallas_call(mix_kernel, out_shape=jax.ShapeDtypeStruct(out_shape, BF16...  1.54 us
    pallas_call x1, Pallas kernels, on_device(): pl.pallas_call(functools.partial(inner_kernel, lat_len), out_shape=(jax.S...  1.46 us
    pallas_call x1, Pallas kernels, on_device(): pl.pallas_call(functools.partial(edge_kernel, lon_count, held), out_shape...  1.45 us
    ppermute x1, waiting for transfers between devices, on_device(): core_b = lax.ppermute(core_b, 'lon', lon_second)  0.71 us
  transfers between devices with their start and end apart: 6, of which 3 were waited for; matrix products, arithmetic and copies ran while one was open for 0% of the time, Pallas kernels for 25%

profile of v8, /device:TPU:0, one launch (start us, length us, event | category | flops | bytes accessed | tf_op | source)
XLA Modules:
  0.0 20.6 jit_solution(14893686247473738810)
XLA Ops:
  0.0 1.5 %shard_map.91 = (bf16[32,128]{1,0:T(8,128)(2,1)S(1)}, bf16[32,128]{1,0:T(8,128)(2,1)S(1)}) custom-call(s32[1,1,6]{2,1,0:T(1,128)} %refs_0_.3, s32[7,128]{1,0:T(8,128)} %bitcast.3, bf16[64,16,128]{2,1,0:T(8,128)(2,1)} %refs_2_.5, bf16[32,64]{1,0:T(8,128)(2,1)} %refs_3_.5), custom_call_target="tpu_custom_call" | custom-call | tf_op jit(solution)/shard_map/pallas_call | solution.py:479
  1.5 6.0 %collective-permute-start = (bf16[32,128]{1,0:T(8,128)(2,1)S(1)}, bf16[32,128]{1,0:T(8,128)(2,1)S(1)}, u32[]{:S(2)}, u32[]{:S(2)}) collective-permute-start(bf16[32,128]{1,0:T(8,128)(2,1)S(1)} %get-tuple-element.35), channel_id=1, source_target_pairs={{0,7},{1,2},{2,1},{3,4},{4,3},{5,6},{6,5},{7,0},{8,15},{9,10},{10,... | collective-permute-start | bytes 24584 | tf_op jit(solution)/shard_map/ppermute | solution.py:493
  7.5 0.1 shard_map.92
  7.6 0.6 %collective-permute-start.1 = (bf16[32,128]{1,0:T(8,128)(2,1)S(1)}, bf16[32,128]{1,0:T(8,128)(2,1)S(1)}, u32[]{:S(2)}, u32[]{:S(2)}) collective-permute-start(bf16[32,128]{1,0:T(8,128)(2,1)S(1)} %get-tuple-element.36), channel_id=1, source_target_pairs={{0,1},{1,0},{2,3},{3,2},{4,5},{5,4},{6,7},{7,6},{8,9},{9,8},{10,11... | collective-permute-start | bytes 24584 | tf_op jit(solution)/shard_map/ppermute | solution.py:507
  8.3 2.8 %shard_map.93 = (bf16[32,2048]{1,0:T(8,128)(2,1)S(1)}, bf16[112,32,512]{2,1,0:T(8,128)(2,1)S(1)}, bf16[2,32,512]{2,1,0:T(8,128)(2,1)S(1)}, s32[16,128]{1,0:T(8,1...) custom-call(s32[1,1,6]{2,1,0:T(1,128)} %refs_0_.3, s32[896]{0:T(1024)} %refs_1_.3, ...), custom_call_target="tpu_custom_call" | custom-call | flops 1000000 | bytes 7340032 | tf_op jit(solution)/shard_map/pallas_call | solution.py:508
  11.0 0.0 collective-permute-done.got_b_ref
  11.0 0.3 %collective-permute-done.1.got_a_ref = bf16[32,128]{1,0:T(8,128)(2,1)S(1)} collective-permute-done((bf16[32,128]{1,0:T(8,128)(2,1)S(1)}, bf16[32,128]{1,0:T(8,128)(2,1)S(1)}, u32[]{:S(2)}, u32[]{:S(2)}) %collective-permute-start.1) | collective-permute-done | bytes 8224 | tf_op jit(solution)/shard_map/ppermute | solution.py:507
  11.4 0.1 shard_map.94
  11.5 0.6 %collective-permute-start.4 = (bf16[2,32,512]{2,1,0:T(8,128)(2,1)S(1)}, bf16[2,32,512]{2,1,0:T(8,128)(2,1)S(1)}, u32[]{:S(2)}, u32[]{:S(2)}) collective-permute-start(bf16[2,32,512]{2,1,0:T(8,128)(2,1)S(1)} %get-tuple-element.46), channel_id=1, source_target_pairs={{0,1},{1,0},{2,3},{3,2},{4,5},{5,4},{6,7},{7,6},{8,9},{9,8},{10,11... | collective-permute-start | bytes 196616 | tf_op jit(solution)/shard_map/ppermute | solution.py:539
  12.1 2.0 %collective-permute-start.5 = (bf16[2,32,512]{2,1,0:T(8,128)(2,1)S(1)}, bf16[2,32,512]{2,1,0:T(8,128)(2,1)S(1)}, u32[]{:S(2)}, u32[]{:S(2)}) collective-permute-start(bf16[2,32,512]{2,1,0:T(8,128)(2,1)S(1)} %get-tuple-element.39.core_ref), channel_id=1, source_target_pairs={{0,7},{1,2},{2,1},{3,4},{4,3},{5,6},{6,5},{7,0},{8,15},{9,10},{10,... | collective-permute-start | bytes 196616 | tf_op jit(solution)/shard_map/ppermute | solution.py:538
  14.1 0.1 shard_map.95
  14.3 0.0 collective-permute-start.2
  14.3 1.6 %collective-permute-start.3 = (bf16[32,384]{1,0:T(8,128)(2,1)S(1)}, bf16[32,384]{1,0:T(8,128)(2,1)S(1)}, u32[]{:S(2)}, u32[]{:S(2)}) collective-permute-start(bf16[32,384]{1,0:T(8,128)(2,1)S(1)} %get-tuple-element.44), channel_id=1, source_target_pairs={{0,8},{8,0},{16,24},{24,16},{1,9},{9,1},{17,25},{25,17},{2,10},{10... | collective-permute-start | bytes 73736 | tf_op jit(solution)/shard_map/ppermute | solution.py:540
  15.9 1.5 %shard_map.96 = (bf16[512,1536]{1,0:T(8,128)(2,1)S(1)}, bf16[2,400,512]{2,1,0:T(8,128)(2,1)S(1)}) custom-call(bf16[32,2048]{1,0:T(8,128)(2,1)S(1)} %get-tuple-element.34.red_ref, bf16[32,128]{1,0:T(8,128)(2,1)S(1)} %get-tuple-element.40.edge_ref, bf16[256,400]{1,0:T(8,128)(2,1)S(1)} %get-tuple-element.41.weights_ref), custom_call_target="tpu_custom_call" | custom-call | tf_op jit(solution)/shard_map/pallas_call | solution.py:545
  17.4 0.3 %collective-permute-done.2.row_b_ref = bf16[32,384]{1,0:T(8,128)(2,1)S(1)} collective-permute-done((bf16[32,384]{1,0:T(8,128)(2,1)S(1)}, bf16[32,384]{1,0:T(8,128)(2,1)S(1)}, u32[]{:S(2)}, u32[]{:S(2)}) %collective-permute-start.2) | collective-permute-done | bytes 24608 | tf_op jit(solution)/shard_map/ppermute | solution.py:541
  17.7 0.0 collective-permute-done.3.row_a_ref
  17.7 0.6 %shard_map.97.border_ref = bf16[512,512]{1,0:T(8,128)(2,1)S(1)} custom-call(bf16[32,384]{1,0:T(8,128)(2,1)S(1)} %collective-permute-done.2.row_b_ref, bf16[32,384]{1,0:T(8,128)(2,1)S(1)} %collective-permute-done.3.row_a_ref, bf16[256,400]{1,0:T(8,128)(2,1)S(1)} %get-tuple-element.41.weights_ref, bf16[2,400,512]{2,1,0:T(8,128)(2,1)S(1)} %get-tuple-element.45.own_stack_ref), custom_call_target="tpu_custom_call" | custom-call | tf_op jit(solution)/shard_map/pallas_call | solution.py:553
  18.4 0.0 collective-permute-done.4.core_a_ref
  18.4 0.7 %collective-permute-done.5.core_b_ref = bf16[2,32,512]{2,1,0:T(8,128)(2,1)S(1)} collective-permute-done((bf16[2,32,512]{2,1,0:T(8,128)(2,1)S(1)}, bf16[2,32,512]{2,1,0:T(8,128)(2,1)S(1)}, u32[]{:S(2)}, u32[]{:S(2)}) %collective-permute-start.5) | collective-permute-done | bytes 65568 | tf_op jit(solution)/shard_map/ppermute | solution.py:538
  19.1 1.5 %shard_map.98 = bf16[64,16,128]{2,1,0:T(8,128)(2,1)} custom-call(bf16[512,1536]{1,0:T(8,128)(2,1)S(1)} %get-tuple-element.42.inner_ref, bf16[512,512]{1,0:T(8,128)(2,1)S(1)} %shard_map.97.border_ref, bf16[2,32,512]{2,1,0:T(8,128)(2,1)S(1)} %collective-permute-done.4.core_a_ref, bf16[2,32,512]{2,1,0:T(8,128)(2,1)S(1)} %collective-permute-done.5.core_b_ref, ...), custom_call_target="tpu_custom_call" | custom-call | tf_op jit(solution)/shard_map/pallas_call | solution.py:562
Async XLA Ops:
  1.5 9.6 %collective-permute-start = (bf16[32,128]{1,0:T(8,128)(2,1)S(1)}, bf16[32,128]{1,0:T(8,128)(2,1)S(1)}, u32[]{:S(2)}, u32[]{:S(2)}) collective-permute-start(bf16[32,128]{1,0:T(8,128)(2,1)S(1)} %get-tuple-element.35), channel_id=1, source_target_pairs={{0,7},{1,2},{2,1},{3,4},{4,3},{5,6},{6,5},{7,0},{8,15},{9,10},{10,... | collective-permute-start | bytes 24584 | tf_op jit(solution)/shard_map/ppermute | solution.py:493
  7.6 3.7 %collective-permute-start.1 = (bf16[32,128]{1,0:T(8,128)(2,1)S(1)}, bf16[32,128]{1,0:T(8,128)(2,1)S(1)}, u32[]{:S(2)}, u32[]{:S(2)}) collective-permute-start(bf16[32,128]{1,0:T(8,128)(2,1)S(1)} %get-tuple-element.36), channel_id=1, source_target_pairs={{0,1},{1,0},{2,3},{3,2},{4,5},{5,4},{6,7},{7,6},{8,9},{9,8},{10,11... | collective-permute-start | bytes 24584 | tf_op jit(solution)/shard_map/ppermute | solution.py:507
  11.5 6.9 %collective-permute-start.4 = (bf16[2,32,512]{2,1,0:T(8,128)(2,1)S(1)}, bf16[2,32,512]{2,1,0:T(8,128)(2,1)S(1)}, u32[]{:S(2)}, u32[]{:S(2)}) collective-permute-start(bf16[2,32,512]{2,1,0:T(8,128)(2,1)S(1)} %get-tuple-element.46), channel_id=1, source_target_pairs={{0,1},{1,0},{2,3},{3,2},{4,5},{5,4},{6,7},{7,6},{8,9},{9,8},{10,11... | collective-permute-start | bytes 196616 | tf_op jit(solution)/shard_map/ppermute | solution.py:539
  12.1 7.0 %collective-permute-start.5 = (bf16[2,32,512]{2,1,0:T(8,128)(2,1)S(1)}, bf16[2,32,512]{2,1,0:T(8,128)(2,1)S(1)}, u32[]{:S(2)}, u32[]{:S(2)}) collective-permute-start(bf16[2,32,512]{2,1,0:T(8,128)(2,1)S(1)} %get-tuple-element.39.core_ref), channel_id=1, source_target_pairs={{0,7},{1,2},{2,1},{3,4},{4,3},{5,6},{6,5},{7,0},{8,15},{9,10},{10,... | collective-permute-start | bytes 196616 | tf_op jit(solution)/shard_map/ppermute | solution.py:538
  14.3 3.4 %collective-permute-start.2 = (bf16[32,384]{1,0:T(8,128)(2,1)S(1)}, bf16[32,384]{1,0:T(8,128)(2,1)S(1)}, u32[]{:S(2)}, u32[]{:S(2)}) collective-permute-start(bf16[32,384]{1,0:T(8,128)(2,1)S(1)} %get-tuple-element.43), channel_id=1, source_target_pairs={{0,24},{8,16},{16,8},{24,0},{1,25},{9,17},{17,9},{25,1},{2,26},{10... | collective-permute-start | bytes 73736 | tf_op jit(solution)/shard_map/ppermute | solution.py:541
  14.3 3.4 %collective-permute-start.3 = (bf16[32,384]{1,0:T(8,128)(2,1)S(1)}, bf16[32,384]{1,0:T(8,128)(2,1)S(1)}, u32[]{:S(2)}, u32[]{:S(2)}) collective-permute-start(bf16[32,384]{1,0:T(8,128)(2,1)S(1)} %get-tuple-element.44), channel_id=1, source_target_pairs={{0,8},{8,0},{16,24},{24,16},{1,9},{9,1},{17,25},{25,17},{2,10},{10... | collective-permute-start | bytes 73736 | tf_op jit(solution)/shard_map/ppermute | solution.py:540

commit v9 on v7

--- a/solution.py
+++ b/solution.py
@@ -142,45 +142,68 @@
         held.own[nth] = held.bank[rows[0][nth]]
 
 
+def asked_rows(list_ref, slots_ref, owner, held):
+    lane = lane_index((1, LANES))
+    found = []
+    for i in range(list_ref.shape[2]):
+        region = list_ref[0, 0, i]
+        row = slots_ref[pl.ds(region // LANES, 1), :]
+        found.append(jnp.where(lane == region % LANES, row - owner * held, -1))
+    local = jnp.max(jnp.concatenate(found, axis=0), axis=1, keepdims=True)
+    hit = (local >= 0) & (local < held)
+    least = jnp.min(jnp.where(hit, local, held - 1), axis=0, keepdims=True)
+    greatest = jnp.max(jnp.where(hit, local, 0), axis=0, keepdims=True)
+    return least, greatest
+
+
 def edge_kernel(lon_count, *refs):
     list_hbm, slot_hbm, feat_hbm, in_hbm, bank_hbm = refs[:5]
-    sources, (pay_a_ref, pay_b_ref), held_refs = refs[5:9], refs[9:11], refs[11:17]
-    list_ref, slot_ref, feat_ref, in_ref, turned_ref = refs[17:22]
-    targets, sems, held_sems = refs[22:26], refs[26], refs[27]
+    sources, slots_hbm, (pay_a_ref, pay_b_ref), held_refs = refs[5:9], refs[9], refs[10:12], refs[12:18]
+    list_ref, slot_ref, feat_ref, in_ref, turned_ref, slots_ref = refs[18:24]
+    targets, sems, held_sems = refs[24:28], refs[28], refs[29]
     held = Held(held_refs)
     channels, lat_len, lon_len = feat_ref.shape
     rank = in_ref.shape[0]
+    batch = LANES // EDGE
+    parts = channels // batch
     pairs = in_parts(feat_hbm, feat_ref, IN_COPIES)
-    pairs += ((slot_hbm, slot_ref), (list_hbm, list_ref), (in_hbm, in_ref))
-    for copy in start_copies(pairs, sems):
+    pairs += ((slots_hbm, slots_ref), (list_hbm, list_ref), (in_hbm, in_ref))
+    copies = start_copies(pairs, sems)
+    lane = lane_index((lat_len, LANES))
+    for part in range(parts):
+        for copy in copies[part * IN_COPIES // parts : (part + 1) * IN_COPIES // parts]:
+            copy.wait()
+        packed = jnp.zeros((lat_len, LANES), BF16)
+        for c in range(batch):
+            moved = pltpu.roll(feat_ref[part * batch + c], (EDGE * c + REACH) % LANES, 1)
+            packed = jnp.where(lane // EDGE == c, moved, packed)
+        turned_ref[part * LANES : (part + 1) * LANES, :] = jnp.transpose(packed.astype(F32))
+    for copy in copies[IN_COPIES:]:
         copy.wait()
-    lane = lane_index((lat_len, LANES))
-    batch = LANES // EDGE
-    for first in range(0, channels, batch):
-        packed = jnp.zeros((lat_len, LANES), F32)
-        for c in range(batch):
-            moved = pltpu.roll(feat_ref[first + c].astype(F32), (EDGE * c + REACH) % LANES, 1)
-            packed = jnp.where(lane // EDGE == c, moved, packed)
-        turned_ref[first * EDGE : (first + batch) * EDGE, :] = jnp.transpose(packed)
     columns = jnp.concatenate(
         [turned_ref[pl.ds(j, channels, stride=EDGE), :].astype(BF16) for j in range(EDGE)], axis=1
     )
     edges = jnp.dot(in_ref[...], columns, preferred_element_type=F32)
     edges = jnp.concatenate([edges, jnp.zeros((rank, LANES - EDGE * lat_len), F32)], axis=1)
-    _, rows = find_rows(list_ref, slot_ref, lon_count, held.bank.shape[0])
-    even = (lax.axis_index("lon") % 2) == 0
+    me = lax.axis_index("lon")
+    even = (me % 2) == 0
+    prev, following = lax.rem(me + lon_count - 1, lon_count), lax.rem(me + 1, lon_count)
     lane = lane_index((rank, LANES))
-    for out_ref, wanted in ((pay_a_ref, even), (pay_b_ref, jnp.logical_not(even))):
+    for out_ref, owner in (
+        (pay_a_ref, jnp.where(even, following, prev)),
+        (pay_b_ref, jnp.where(even, prev, following)),
+    ):
         load = edges
-        for nth in range(PER_OWNER):
-            row = jnp.where(wanted, rows[2][nth], rows[1][nth]).astype(F32)
-            load = jnp.where(lane == EDGE * lat_len + nth, row, load)
+        for nth, row in enumerate(asked_rows(list_ref, slots_ref, owner, held.bank.shape[0])):
+            load = jnp.where(lane == EDGE * lat_len + nth, row.astype(F32), load)
         out_ref[...] = load.astype(BF16)
 
     @pl.when(is_early())
     def _():
         copies = start_sources(sources, targets, bank_hbm, held.bank, held_sems)
-        for copy in copies[: len(targets)]:
+        scalars = pltpu.make_async_copy(slot_hbm, slot_ref, sems.at[0])
+        scalars.start()
+        for copy in [scalars, *copies[: len(targets)]]:
             copy.wait()
         build_held(lon_count, list_ref, slot_ref, targets, copies[len(targets) :], held)
 
@@ -456,17 +479,18 @@
     pay_a, pay_b, early_bank, *given = pl.pallas_call(
         functools.partial(edge_kernel, lon_count),
         out_shape=(edge_shape, edge_shape, *held_shapes),
-        in_specs=[HBM] * 9,
+        in_specs=[HBM] * 10,
         out_specs=(VMEM,) * 8,
         scratch_shapes=[
             *lists,
             pltpu.VMEM((channels * EDGE, lat_len), F32),
+            pltpu.VMEM((bank_slot.shape[0] // LANES, LANES), jnp.int32),
             *targets,
             pltpu.SemaphoreType.DMA((IN_COPIES + 3,)),
             pltpu.SemaphoreType.DMA((4 + BANK_COPIES,)),
         ],
         compiler_params=PARAMS,
-    )(*sources)
+    )(*sources, in_hbm(bank_slot.reshape(-1, LANES)))
     got_b = lax.ppermute(pay_b, "lon", lon_second)
     got_a = lax.ppermute(pay_a, "lon", lon_first)
     reduced, late_bank, own, position, weights, mixer, offset = pl.pallas_call(

time: 20.2 us -> 20.3 us (level)
  no operation moved by 1% of the time
where the time goes in v9:
time: 20.3 us; the launch traced here: 20.2 us
  starting transfers between devices  10.5 us (52%)
  Pallas kernels  8.35 us (41%)
  waiting for transfers between devices  1.24 us (6%)
    ppermute x1, starting transfers between devices, on_device(): got_b = lax.ppermute(pay_b, 'lon', lon_second)  6.04 us
    ppermute x1, starting transfers between devices, on_device(): core_b = lax.ppermute(core_b, 'lon', lon_second)  2.77 us
    pallas_call x1, Pallas kernels, on_device(): pl.pallas_call(functools.partial(prepare_kernel, lon_count, lat_len), out...  2.76 us
    pallas_call x1, Pallas kernels, on_device(): pl.pallas_call(functools.partial(edge_kernel, lon_count), out_shape=(edge...  1.68 us
    ppermute x1, starting transfers between devices, on_device(): row_a = lax.ppermute(row_a, 'lat', lat_first)  1.63 us
    pallas_call x1, Pallas kernels, on_device(): pl.pallas_call(mix_kernel, out_shape=jax.ShapeDtypeStruct(out_shape, BF16...  1.53 us
    pallas_call x1, Pallas kernels, on_device(): pl.pallas_call(functools.partial(inner_kernel, lat_len), out_shape=(jax.S...  1.46 us
    ppermute x1, waiting for transfers between devices, on_device(): got_a = lax.ppermute(pay_a, 'lon', lon_first)  0.87 us
  transfers between devices with their start and end apart: 6, of which 2 were waited for; matrix products, arithmetic and copies ran while one was open for 0% of the time, Pallas kernels for 25%

profile of v9, /device:TPU:0, one launch (start us, length us, event | category | flops | bytes accessed | tf_op | source)
XLA Modules:
  0.0 20.2 jit_solution(1511601689973223031)
XLA Ops:
  0.0 1.7 %shard_map.91 = (bf16[32,128]{1,0:T(8,128)(2,1)S(1)}, bf16[32,128]{1,0:T(8,128)(2,1)S(1)}, bf16[112,32,512]{2,1,0:T(8,128)(2,1)S(1)}, bf16[2,32,512]{2,1,0:T(8,1...) custom-call(s32[1,1,6]{2,1,0:T(1,128)} %refs_0_.3, ...), custom_call_target="tpu_custom_call" | custom-call | tf_op jit(solution)/shard_map/pallas_call | solution.py:479
  1.7 6.0 %collective-permute-start = (bf16[32,128]{1,0:T(8,128)(2,1)S(1)}, bf16[32,128]{1,0:T(8,128)(2,1)S(1)}, u32[]{:S(2)}, u32[]{:S(2)}) collective-permute-start(bf16[32,128]{1,0:T(8,128)(2,1)S(1)} %get-tuple-element.33), channel_id=1, source_target_pairs={{0,7},{1,2},{2,1},{3,4},{4,3},{5,6},{6,5},{7,0},{8,15},{9,10},{10,... | collective-permute-start | bytes 24584 | tf_op jit(solution)/shard_map/ppermute | solution.py:494
  7.7 0.0 collective-permute-start.1
  7.7 2.8 %shard_map.92 = (bf16[32,2048]{1,0:T(8,128)(2,1)S(1)}, bf16[112,32,512]{2,1,0:T(8,128)(2,1)S(1)}, bf16[2,32,512]{2,1,0:T(8,128)(2,1)S(1)}, s32[16,128]{1,0:T(8,1...) custom-call(s32[1,1,6]{2,1,0:T(1,128)} %refs_0_.3, s32[896]{0:T(1024)} %refs_1_.3, ...), custom_call_target="tpu_custom_call" | custom-call | flops 1000000 | bytes 7340032 | tf_op jit(solution)/shard_map/pallas_call | solution.py:496
  10.5 0.0 collective-permute-done.got_b_ref
  10.5 0.9 %collective-permute-done.1.got_a_ref = bf16[32,128]{1,0:T(8,128)(2,1)S(1)} collective-permute-done((bf16[32,128]{1,0:T(8,128)(2,1)S(1)}, bf16[32,128]{1,0:T(8,128)(2,1)S(1)}, u32[]{:S(2)}, u32[]{:S(2)}) %collective-permute-start.1) | collective-permute-done | bytes 8224 | tf_op jit(solution)/shard_map/ppermute | solution.py:495
  11.4 0.1 shard_map.93
  11.5 0.1 collective-permute-start.4
  11.6 2.8 %collective-permute-start.5 = (bf16[2,32,512]{2,1,0:T(8,128)(2,1)S(1)}, bf16[2,32,512]{2,1,0:T(8,128)(2,1)S(1)}, u32[]{:S(2)}, u32[]{:S(2)}) collective-permute-start(bf16[2,32,512]{2,1,0:T(8,128)(2,1)S(1)} %get-tuple-element.37.core_ref), channel_id=1, source_target_pairs={{0,7},{1,2},{2,1},{3,4},{4,3},{5,6},{6,5},{7,0},{8,15},{9,10},{10,... | collective-permute-start | bytes 196616 | tf_op jit(solution)/shard_map/ppermute | solution.py:526
  14.4 0.1 shard_map.94
  14.5 0.0 collective-permute-start.2
  14.5 1.6 %collective-permute-start.3 = (bf16[32,384]{1,0:T(8,128)(2,1)S(1)}, bf16[32,384]{1,0:T(8,128)(2,1)S(1)}, u32[]{:S(2)}, u32[]{:S(2)}) collective-permute-start(bf16[32,384]{1,0:T(8,128)(2,1)S(1)} %get-tuple-element.42), channel_id=1, source_target_pairs={{0,8},{8,0},{16,24},{24,16},{1,9},{9,1},{17,25},{25,17},{2,10},{10... | collective-permute-start | bytes 73736 | tf_op jit(solution)/shard_map/ppermute | solution.py:528
  16.2 1.5 %shard_map.95 = (bf16[512,1536]{1,0:T(8,128)(2,1)S(1)}, bf16[2,400,512]{2,1,0:T(8,128)(2,1)S(1)}) custom-call(bf16[32,2048]{1,0:T(8,128)(2,1)S(1)} %get-tuple-element.32.red_ref, bf16[32,128]{1,0:T(8,128)(2,1)S(1)} %get-tuple-element.38.edge_ref, bf16[256,400]{1,0:T(8,128)(2,1)S(1)} %get-tuple-element.39.weights_ref), custom_call_target="tpu_custom_call" | custom-call | tf_op jit(solution)/shard_map/pallas_call | solution.py:533
  17.6 0.3 %collective-permute-done.2.row_b_ref = bf16[32,384]{1,0:T(8,128)(2,1)S(1)} collective-permute-done((bf16[32,384]{1,0:T(8,128)(2,1)S(1)}, bf16[32,384]{1,0:T(8,128)(2,1)S(1)}, u32[]{:S(2)}, u32[]{:S(2)}) %collective-permute-start.2) | collective-permute-done | bytes 24608 | tf_op jit(solution)/shard_map/ppermute | solution.py:529
  18.0 0.0 collective-permute-done.3.row_a_ref
  18.0 0.6 %shard_map.96.border_ref = bf16[512,512]{1,0:T(8,128)(2,1)S(1)} custom-call(bf16[32,384]{1,0:T(8,128)(2,1)S(1)} %collective-permute-done.2.row_b_ref, bf16[32,384]{1,0:T(8,128)(2,1)S(1)} %collective-permute-done.3.row_a_ref, bf16[256,400]{1,0:T(8,128)(2,1)S(1)} %get-tuple-element.39.weights_ref, bf16[2,400,512]{2,1,0:T(8,128)(2,1)S(1)} %get-tuple-element.43.own_stack_ref), custom_call_target="tpu_custom_call" | custom-call | tf_op jit(solution)/shard_map/pallas_call | solution.py:541
  18.6 0.0 collective-permute-done.4.core_a_ref
  18.6 0.0 collective-permute-done.5.core_b_ref
  18.6 1.5 %shard_map.97 = bf16[64,16,128]{2,1,0:T(8,128)(2,1)} custom-call(bf16[512,1536]{1,0:T(8,128)(2,1)S(1)} %get-tuple-element.40.inner_ref, bf16[512,512]{1,0:T(8,128)(2,1)S(1)} %shard_map.96.border_ref, bf16[2,32,512]{2,1,0:T(8,128)(2,1)S(1)} %collective-permute-done.4.core_a_ref, bf16[2,32,512]{2,1,0:T(8,128)(2,1)S(1)} %collective-permute-done.5.core_b_ref, ...), custom_call_target="tpu_custom_call" | custom-call | tf_op jit(solution)/shard_map/pallas_call | solution.py:550
Async XLA Ops:
  1.7 8.8 %collective-permute-start = (bf16[32,128]{1,0:T(8,128)(2,1)S(1)}, bf16[32,128]{1,0:T(8,128)(2,1)S(1)}, u32[]{:S(2)}, u32[]{:S(2)}) collective-permute-start(bf16[32,128]{1,0:T(8,128)(2,1)S(1)} %get-tuple-element.33), channel_id=1, source_target_pairs={{0,7},{1,2},{2,1},{3,4},{4,3},{5,6},{6,5},{7,0},{8,15},{9,10},{10,... | collective-permute-start | bytes 24584 | tf_op jit(solution)/shard_map/ppermute | solution.py:494
  7.7 3.7 %collective-permute-start.1 = (bf16[32,128]{1,0:T(8,128)(2,1)S(1)}, bf16[32,128]{1,0:T(8,128)(2,1)S(1)}, u32[]{:S(2)}, u32[]{:S(2)}) collective-permute-start(bf16[32,128]{1,0:T(8,128)(2,1)S(1)} %get-tuple-element.34), channel_id=1, source_target_pairs={{0,1},{1,0},{2,3},{3,2},{4,5},{5,4},{6,7},{7,6},{8,9},{9,8},{10,11... | collective-permute-start | bytes 24584 | tf_op jit(solution)/shard_map/ppermute | solution.py:495
  11.5 7.1 %collective-permute-start.4 = (bf16[2,32,512]{2,1,0:T(8,128)(2,1)S(1)}, bf16[2,32,512]{2,1,0:T(8,128)(2,1)S(1)}, u32[]{:S(2)}, u32[]{:S(2)}) collective-permute-start(bf16[2,32,512]{2,1,0:T(8,128)(2,1)S(1)} %get-tuple-element.44), channel_id=1, source_target_pairs={{0,1},{1,0},{2,3},{3,2},{4,5},{5,4},{6,7},{7,6},{8,9},{9,8},{10,11... | collective-permute-start | bytes 196616 | tf_op jit(solution)/shard_map/ppermute | solution.py:527
  11.6 7.0 %collective-permute-start.5 = (bf16[2,32,512]{2,1,0:T(8,128)(2,1)S(1)}, bf16[2,32,512]{2,1,0:T(8,128)(2,1)S(1)}, u32[]{:S(2)}, u32[]{:S(2)}) collective-permute-start(bf16[2,32,512]{2,1,0:T(8,128)(2,1)S(1)} %get-tuple-element.37.core_ref), channel_id=1, source_target_pairs={{0,7},{1,2},{2,1},{3,4},{4,3},{5,6},{6,5},{7,0},{8,15},{9,10},{10,... | collective-permute-start | bytes 196616 | tf_op jit(solution)/shard_map/ppermute | solution.py:526
  14.5 3.4 %collective-permute-start.2 = (bf16[32,384]{1,0:T(8,128)(2,1)S(1)}, bf16[32,384]{1,0:T(8,128)(2,1)S(1)}, u32[]{:S(2)}, u32[]{:S(2)}) collective-permute-start(bf16[32,384]{1,0:T(8,128)(2,1)S(1)} %get-tuple-element.41), channel_id=1, source_target_pairs={{0,24},{8,16},{16,8},{24,0},{1,25},{9,17},{17,9},{25,1},{2,26},{10... | collective-permute-start | bytes 73736 | tf_op jit(solution)/shard_map/ppermute | solution.py:529
  14.5 3.4 %collective-permute-start.3 = (bf16[32,384]{1,0:T(8,128)(2,1)S(1)}, bf16[32,384]{1,0:T(8,128)(2,1)S(1)}, u32[]{:S(2)}, u32[]{:S(2)}) collective-permute-start(bf16[32,384]{1,0:T(8,128)(2,1)S(1)} %get-tuple-element.42), channel_id=1, source_target_pairs={{0,8},{8,0},{16,24},{24,16},{1,9},{9,1},{17,25},{25,17},{2,10},{10... | collective-permute-start | bytes 73736 | tf_op jit(solution)/shard_map/ppermute | solution.py:528

commit v10 on v7

--- a/solution.py
+++ b/solution.py
@@ -388,12 +388,13 @@
     groups = [jnp.concatenate(pieces[g : g + GROUP], axis=0) for g in range(0, lat_len, GROUP)]
     channels = stage_ref.shape[0]
     share = channels // OUT_COPIES
+    outputs = [jnp.dot(mixer_ref[...], hidden, preferred_element_type=F32) for hidden in groups]
     copies = []
     for part in range(OUT_COPIES):
         span = slice(part * share * GROUP, (part + 1) * share * GROUP)
         blocks = []
-        for hidden in groups:
-            output = jnp.dot(mixer_ref[span, :], hidden, preferred_element_type=F32) + offset_ref[span, :]
+        for output in outputs:
+            output = output[span] + offset_ref[span, :]
             mixed = 0.5 * output * (1.0 + jnp.tanh(0.5 * output))
             blocks.append(mixed.reshape(share, GROUP, lon_len))
         held = slice(part * share, (part + 1) * share)

time: 20.2 us -> 20.2 us (level)
  no operation moved by 1% of the time
where the time goes in v10:
time: 20.2 us; the launch traced here: 20.1 us
  starting transfers between devices  10.5 us (52%)
  Pallas kernels  8.24 us (41%)
  waiting for transfers between devices  1.24 us (6%)
    ppermute x1, starting transfers between devices, on_device(): got_b = lax.ppermute(pay_b, 'lon', lon_second)  6.04 us
    ppermute x1, starting transfers between devices, on_device(): core_b = lax.ppermute(core_b, 'lon', lon_second)  2.77 us
    pallas_call x1, Pallas kernels, on_device(): pl.pallas_call(functools.partial(prepare_kernel, lon_count, lat_len), out...  2.76 us
    ppermute x1, starting transfers between devices, on_device(): row_a = lax.ppermute(row_a, 'lat', lat_first)  1.63 us
    pallas_call x1, Pallas kernels, on_device(): pl.pallas_call(functools.partial(edge_kernel, lon_count), out_shape=(edge...  1.57 us
    pallas_call x1, Pallas kernels, on_device(): pl.pallas_call(mix_kernel, out_shape=jax.ShapeDtypeStruct(out_shape, BF16...  1.53 us
    pallas_call x1, Pallas kernels, on_device(): pl.pallas_call(functools.partial(inner_kernel, lat_len), out_shape=(jax.S...  1.47 us
    ppermute x1, waiting for transfers between devices, on_device(): got_a = lax.ppermute(pay_a, 'lon', lon_first)  0.87 us
  transfers between devices with their start and end apart: 6, of which 2 were waited for; matrix products, arithmetic and copies ran while one was open for 0% of the time, Pallas kernels for 25%

profile of v10, /device:TPU:0, one launch (start us, length us, event | category | flops | bytes accessed | tf_op | source)
XLA Modules:
  0.0 20.1 jit_solution(3360357150520492402)
XLA Ops:
  0.0 1.6 %shard_map.91 = (bf16[32,128]{1,0:T(8,128)(2,1)S(1)}, bf16[32,128]{1,0:T(8,128)(2,1)S(1)}, bf16[112,32,512]{2,1,0:T(8,128)(2,1)S(1)}, bf16[2,32,512]{2,1,0:T(8,1...) custom-call(s32[1,1,6]{2,1,0:T(1,128)} %refs_0_.3, ...), custom_call_target="tpu_custom_call" | custom-call | tf_op jit(solution)/shard_map/pallas_call | solution.py:457
  1.6 6.0 %collective-permute-start = (bf16[32,128]{1,0:T(8,128)(2,1)S(1)}, bf16[32,128]{1,0:T(8,128)(2,1)S(1)}, u32[]{:S(2)}, u32[]{:S(2)}) collective-permute-start(bf16[32,128]{1,0:T(8,128)(2,1)S(1)} %get-tuple-element.33), channel_id=1, source_target_pairs={{0,7},{1,2},{2,1},{3,4},{4,3},{5,6},{6,5},{7,0},{8,15},{9,10},{10,... | collective-permute-start | bytes 24584 | tf_op jit(solution)/shard_map/ppermute | solution.py:471
  7.6 0.0 collective-permute-start.1
  7.6 2.8 %shard_map.92 = (bf16[32,2048]{1,0:T(8,128)(2,1)S(1)}, bf16[112,32,512]{2,1,0:T(8,128)(2,1)S(1)}, bf16[2,32,512]{2,1,0:T(8,128)(2,1)S(1)}, s32[16,128]{1,0:T(8,1...) custom-call(s32[1,1,6]{2,1,0:T(1,128)} %refs_0_.3, s32[896]{0:T(1024)} %refs_1_.3, ...), custom_call_target="tpu_custom_call" | custom-call | flops 1000000 | bytes 7340032 | tf_op jit(solution)/shard_map/pallas_call | solution.py:473
  10.4 0.0 collective-permute-done.got_b_ref
  10.4 0.9 %collective-permute-done.1.got_a_ref = bf16[32,128]{1,0:T(8,128)(2,1)S(1)} collective-permute-done((bf16[32,128]{1,0:T(8,128)(2,1)S(1)}, bf16[32,128]{1,0:T(8,128)(2,1)S(1)}, u32[]{:S(2)}, u32[]{:S(2)}) %collective-permute-start.1) | collective-permute-done | bytes 8224 | tf_op jit(solution)/shard_map/ppermute | solution.py:472
  11.3 0.1 shard_map.93
  11.4 0.1 collective-permute-start.4
  11.5 2.8 %collective-permute-start.5 = (bf16[2,32,512]{2,1,0:T(8,128)(2,1)S(1)}, bf16[2,32,512]{2,1,0:T(8,128)(2,1)S(1)}, u32[]{:S(2)}, u32[]{:S(2)}) collective-permute-start(bf16[2,32,512]{2,1,0:T(8,128)(2,1)S(1)} %get-tuple-element.37.core_ref), channel_id=1, source_target_pairs={{0,7},{1,2},{2,1},{3,4},{4,3},{5,6},{6,5},{7,0},{8,15},{9,10},{10,... | collective-permute-start | bytes 196616 | tf_op jit(solution)/shard_map/ppermute | solution.py:503
  14.3 0.1 shard_map.94
  14.4 0.0 collective-permute-start.2
  14.4 1.6 %collective-permute-start.3 = (bf16[32,384]{1,0:T(8,128)(2,1)S(1)}, bf16[32,384]{1,0:T(8,128)(2,1)S(1)}, u32[]{:S(2)}, u32[]{:S(2)}) collective-permute-start(bf16[32,384]{1,0:T(8,128)(2,1)S(1)} %get-tuple-element.42), channel_id=1, source_target_pairs={{0,8},{8,0},{16,24},{24,16},{1,9},{9,1},{17,25},{25,17},{2,10},{10... | collective-permute-start | bytes 73736 | tf_op jit(solution)/shard_map/ppermute | solution.py:505
  16.0 1.5 %shard_map.95 = (bf16[512,1536]{1,0:T(8,128)(2,1)S(1)}, bf16[2,400,512]{2,1,0:T(8,128)(2,1)S(1)}) custom-call(bf16[32,2048]{1,0:T(8,128)(2,1)S(1)} %get-tuple-element.32.red_ref, bf16[32,128]{1,0:T(8,128)(2,1)S(1)} %get-tuple-element.38.edge_ref, bf16[256,400]{1,0:T(8,128)(2,1)S(1)} %get-tuple-element.39.weights_ref), custom_call_target="tpu_custom_call" | custom-call | tf_op jit(solution)/shard_map/pallas_call | solution.py:510
  17.5 0.3 %collective-permute-done.2.row_b_ref = bf16[32,384]{1,0:T(8,128)(2,1)S(1)} collective-permute-done((bf16[32,384]{1,0:T(8,128)(2,1)S(1)}, bf16[32,384]{1,0:T(8,128)(2,1)S(1)}, u32[]{:S(2)}, u32[]{:S(2)}) %collective-permute-start.2) | collective-permute-done | bytes 24608 | tf_op jit(solution)/shard_map/ppermute | solution.py:506
  17.8 0.0 collective-permute-done.3.row_a_ref
  17.8 0.6 %shard_map.96.border_ref = bf16[512,512]{1,0:T(8,128)(2,1)S(1)} custom-call(bf16[32,384]{1,0:T(8,128)(2,1)S(1)} %collective-permute-done.2.row_b_ref, bf16[32,384]{1,0:T(8,128)(2,1)S(1)} %collective-permute-done.3.row_a_ref, bf16[256,400]{1,0:T(8,128)(2,1)S(1)} %get-tuple-element.39.weights_ref, bf16[2,400,512]{2,1,0:T(8,128)(2,1)S(1)} %get-tuple-element.43.own_stack_ref), custom_call_target="tpu_custom_call" | custom-call | tf_op jit(solution)/shard_map/pallas_call | solution.py:518
  18.5 0.0 collective-permute-done.4.core_a_ref
  18.5 0.0 collective-permute-done.5.core_b_ref
  18.5 1.5 %shard_map.97 = bf16[64,16,128]{2,1,0:T(8,128)(2,1)} custom-call(bf16[512,1536]{1,0:T(8,128)(2,1)S(1)} %get-tuple-element.40.inner_ref, bf16[512,512]{1,0:T(8,128)(2,1)S(1)} %shard_map.96.border_ref, bf16[2,32,512]{2,1,0:T(8,128)(2,1)S(1)} %collective-permute-done.4.core_a_ref, bf16[2,32,512]{2,1,0:T(8,128)(2,1)S(1)} %collective-permute-done.5.core_b_ref, ...), custom_call_target="tpu_custom_call" | custom-call | tf_op jit(solution)/shard_map/pallas_call | solution.py:527
Async XLA Ops:
  1.6 8.8 %collective-permute-start = (bf16[32,128]{1,0:T(8,128)(2,1)S(1)}, bf16[32,128]{1,0:T(8,128)(2,1)S(1)}, u32[]{:S(2)}, u32[]{:S(2)}) collective-permute-start(bf16[32,128]{1,0:T(8,128)(2,1)S(1)} %get-tuple-element.33), channel_id=1, source_target_pairs={{0,7},{1,2},{2,1},{3,4},{4,3},{5,6},{6,5},{7,0},{8,15},{9,10},{10,... | collective-permute-start | bytes 24584 | tf_op jit(solution)/shard_map/ppermute | solution.py:471
  7.6 3.7 %collective-permute-start.1 = (bf16[32,128]{1,0:T(8,128)(2,1)S(1)}, bf16[32,128]{1,0:T(8,128)(2,1)S(1)}, u32[]{:S(2)}, u32[]{:S(2)}) collective-permute-start(bf16[32,128]{1,0:T(8,128)(2,1)S(1)} %get-tuple-element.34), channel_id=1, source_target_pairs={{0,1},{1,0},{2,3},{3,2},{4,5},{5,4},{6,7},{7,6},{8,9},{9,8},{10,11... | collective-permute-start | bytes 24584 | tf_op jit(solution)/shard_map/ppermute | solution.py:472
  11.4 7.1 %collective-permute-start.4 = (bf16[2,32,512]{2,1,0:T(8,128)(2,1)S(1)}, bf16[2,32,512]{2,1,0:T(8,128)(2,1)S(1)}, u32[]{:S(2)}, u32[]{:S(2)}) collective-permute-start(bf16[2,32,512]{2,1,0:T(8,128)(2,1)S(1)} %get-tuple-element.44), channel_id=1, source_target_pairs={{0,1},{1,0},{2,3},{3,2},{4,5},{5,4},{6,7},{7,6},{8,9},{9,8},{10,11... | collective-permute-start | bytes 196616 | tf_op jit(solution)/shard_map/ppermute | solution.py:504
  11.5 7.0 %collective-permute-start.5 = (bf16[2,32,512]{2,1,0:T(8,128)(2,1)S(1)}, bf16[2,32,512]{2,1,0:T(8,128)(2,1)S(1)}, u32[]{:S(2)}, u32[]{:S(2)}) collective-permute-start(bf16[2,32,512]{2,1,0:T(8,128)(2,1)S(1)} %get-tuple-element.37.core_ref), channel_id=1, source_target_pairs={{0,7},{1,2},{2,1},{3,4},{4,3},{5,6},{6,5},{7,0},{8,15},{9,10},{10,... | collective-permute-start | bytes 196616 | tf_op jit(solution)/shard_map/ppermute | solution.py:503
  14.4 3.4 %collective-permute-start.2 = (bf16[32,384]{1,0:T(8,128)(2,1)S(1)}, bf16[32,384]{1,0:T(8,128)(2,1)S(1)}, u32[]{:S(2)}, u32[]{:S(2)}) collective-permute-start(bf16[32,384]{1,0:T(8,128)(2,1)S(1)} %get-tuple-element.41), channel_id=1, source_target_pairs={{0,24},{8,16},{16,8},{24,0},{1,25},{9,17},{17,9},{25,1},{2,26},{10... | collective-permute-start | bytes 73736 | tf_op jit(solution)/shard_map/ppermute | solution.py:506
  14.4 3.4 %collective-permute-start.3 = (bf16[32,384]{1,0:T(8,128)(2,1)S(1)}, bf16[32,384]{1,0:T(8,128)(2,1)S(1)}, u32[]{:S(2)}, u32[]{:S(2)}) collective-permute-start(bf16[32,384]{1,0:T(8,128)(2,1)S(1)} %get-tuple-element.42), channel_id=1, source_target_pairs={{0,8},{8,0},{16,24},{24,16},{1,9},{9,1},{17,25},{25,17},{2,10},{10... | collective-permute-start | bytes 73736 | tf_op jit(solution)/shard_map/ppermute | solution.py:505

commit v11 on v9

--- a/solution.py
+++ b/solution.py
@@ -165,21 +165,18 @@
     channels, lat_len, lon_len = feat_ref.shape
     rank = in_ref.shape[0]
     batch = LANES // EDGE
-    parts = channels // batch
     pairs = in_parts(feat_hbm, feat_ref, IN_COPIES)
     pairs += ((slots_hbm, slots_ref), (list_hbm, list_ref), (in_hbm, in_ref))
     copies = start_copies(pairs, sems)
+    for copy in copies:
+        copy.wait()
     lane = lane_index((lat_len, LANES))
-    for part in range(parts):
-        for copy in copies[part * IN_COPIES // parts : (part + 1) * IN_COPIES // parts]:
-            copy.wait()
-        packed = jnp.zeros((lat_len, LANES), BF16)
+    for part in range(channels // batch):
+        packed = jnp.zeros((lat_len, LANES), F32)
         for c in range(batch):
-            moved = pltpu.roll(feat_ref[part * batch + c], (EDGE * c + REACH) % LANES, 1)
+            moved = pltpu.roll(feat_ref[part * batch + c].astype(F32), (EDGE * c + REACH) % LANES, 1)
             packed = jnp.where(lane // EDGE == c, moved, packed)
-        turned_ref[part * LANES : (part + 1) * LANES, :] = jnp.transpose(packed.astype(F32))
-    for copy in copies[IN_COPIES:]:
-        copy.wait()
+        turned_ref[part * LANES : (part + 1) * LANES, :] = jnp.transpose(packed)
     columns = jnp.concatenate(
         [turned_ref[pl.ds(j, channels, stride=EDGE), :].astype(BF16) for j in range(EDGE)], axis=1
     )
@@ -411,12 +408,13 @@
     groups = [jnp.concatenate(pieces[g : g + GROUP], axis=0) for g in range(0, lat_len, GROUP)]
     channels = stage_ref.shape[0]
     share = channels // OUT_COPIES
+    outputs = [jnp.dot(mixer_ref[...], hidden, preferred_element_type=F32) for hidden in groups]
     copies = []
     for part in range(OUT_COPIES):
         span = slice(part * share * GROUP, (part + 1) * share * GROUP)
         blocks = []
-        for hidden in groups:
-            output = jnp.dot(mixer_ref[span, :], hidden, preferred_element_type=F32) + offset_ref[span, :]
+        for output in outputs:
+            output = output[span] + offset_ref[span, :]
             mixed = 0.5 * output * (1.0 + jnp.tanh(0.5 * output))
             blocks.append(mixed.reshape(share, GROUP, lon_len))
         held = slice(part * share, (part + 1) * share)

time: 20.3 us -> 20.2 us (level)
  no operation moved by 1% of the time
where the time goes in v11:
time: 20.2 us; the launch traced here: 20 us
  starting transfers between devices  10.5 us (52%)
  Pallas kernels  8.22 us (41%)
  waiting for transfers between devices  1.24 us (6%)
    ppermute x1, starting transfers between devices, on_device(): got_b = lax.ppermute(pay_b, 'lon', lon_second)  6.04 us
    ppermute x1, starting transfers between devices, on_device(): core_b = lax.ppermute(core_b, 'lon', lon_second)  2.77 us
    pallas_call x1, Pallas kernels, on_device(): pl.pallas_call(functools.partial(prepare_kernel, lon_count, lat_len), out...  2.76 us
    ppermute x1, starting transfers between devices, on_device(): row_a = lax.ppermute(row_a, 'lat', lat_first)  1.63 us
    pallas_call x1, Pallas kernels, on_device(): pl.pallas_call(functools.partial(edge_kernel, lon_count), out_shape=(edge...  1.56 us
    pallas_call x1, Pallas kernels, on_device(): pl.pallas_call(mix_kernel, out_shape=jax.ShapeDtypeStruct(out_shape, BF16...  1.53 us
    pallas_call x1, Pallas kernels, on_device(): pl.pallas_call(functools.partial(inner_kernel, lat_len), out_shape=(jax.S...  1.47 us
    ppermute x1, waiting for transfers between devices, on_device(): got_a = lax.ppermute(pay_a, 'lon', lon_first)  0.87 us
  transfers between devices with their start and end apart: 6, of which 2 were waited for; matrix products, arithmetic and copies ran while one was open for 0% of the time, Pallas kernels for 25%

profile of v11, /device:TPU:0, one launch (start us, length us, event | category | flops | bytes accessed | tf_op | source)
XLA Modules:
  0.0 20.0 jit_solution(3587487631187042765)
XLA Ops:
  0.0 1.6 %shard_map.91 = (bf16[32,128]{1,0:T(8,128)(2,1)S(1)}, bf16[32,128]{1,0:T(8,128)(2,1)S(1)}, bf16[112,32,512]{2,1,0:T(8,128)(2,1)S(1)}, bf16[2,32,512]{2,1,0:T(8,1...) custom-call(s32[1,1,6]{2,1,0:T(1,128)} %refs_0_.3, ...), custom_call_target="tpu_custom_call" | custom-call | tf_op jit(solution)/shard_map/pallas_call | solution.py:477
  1.6 6.0 %collective-permute-start = (bf16[32,128]{1,0:T(8,128)(2,1)S(1)}, bf16[32,128]{1,0:T(8,128)(2,1)S(1)}, u32[]{:S(2)}, u32[]{:S(2)}) collective-permute-start(bf16[32,128]{1,0:T(8,128)(2,1)S(1)} %get-tuple-element.33), channel_id=1, source_target_pairs={{0,7},{1,2},{2,1},{3,4},{4,3},{5,6},{6,5},{7,0},{8,15},{9,10},{10,... | collective-permute-start | bytes 24584 | tf_op jit(solution)/shard_map/ppermute | solution.py:492
  7.6 0.0 collective-permute-start.1
  7.6 2.8 %shard_map.92 = (bf16[32,2048]{1,0:T(8,128)(2,1)S(1)}, bf16[112,32,512]{2,1,0:T(8,128)(2,1)S(1)}, bf16[2,32,512]{2,1,0:T(8,128)(2,1)S(1)}, s32[16,128]{1,0:T(8,1...) custom-call(s32[1,1,6]{2,1,0:T(1,128)} %refs_0_.3, s32[896]{0:T(1024)} %refs_1_.3, ...), custom_call_target="tpu_custom_call" | custom-call | flops 1000000 | bytes 7340032 | tf_op jit(solution)/shard_map/pallas_call | solution.py:494
  10.4 0.0 collective-permute-done.got_b_ref
  10.4 0.9 %collective-permute-done.1.got_a_ref = bf16[32,128]{1,0:T(8,128)(2,1)S(1)} collective-permute-done((bf16[32,128]{1,0:T(8,128)(2,1)S(1)}, bf16[32,128]{1,0:T(8,128)(2,1)S(1)}, u32[]{:S(2)}, u32[]{:S(2)}) %collective-permute-start.1) | collective-permute-done | bytes 8224 | tf_op jit(solution)/shard_map/ppermute | solution.py:493
  11.3 0.1 shard_map.93
  11.4 0.1 collective-permute-start.4
  11.5 2.8 %collective-permute-start.5 = (bf16[2,32,512]{2,1,0:T(8,128)(2,1)S(1)}, bf16[2,32,512]{2,1,0:T(8,128)(2,1)S(1)}, u32[]{:S(2)}, u32[]{:S(2)}) collective-permute-start(bf16[2,32,512]{2,1,0:T(8,128)(2,1)S(1)} %get-tuple-element.37.core_ref), channel_id=1, source_target_pairs={{0,7},{1,2},{2,1},{3,4},{4,3},{5,6},{6,5},{7,0},{8,15},{9,10},{10,... | collective-permute-start | bytes 196616 | tf_op jit(solution)/shard_map/ppermute | solution.py:524
  14.3 0.1 shard_map.94
  14.4 0.0 collective-permute-start.2
  14.4 1.6 %collective-permute-start.3 = (bf16[32,384]{1,0:T(8,128)(2,1)S(1)}, bf16[32,384]{1,0:T(8,128)(2,1)S(1)}, u32[]{:S(2)}, u32[]{:S(2)}) collective-permute-start(bf16[32,384]{1,0:T(8,128)(2,1)S(1)} %get-tuple-element.42), channel_id=1, source_target_pairs={{0,8},{8,0},{16,24},{24,16},{1,9},{9,1},{17,25},{25,17},{2,10},{10... | collective-permute-start | bytes 73736 | tf_op jit(solution)/shard_map/ppermute | solution.py:526
  16.0 1.5 %shard_map.95 = (bf16[512,1536]{1,0:T(8,128)(2,1)S(1)}, bf16[2,400,512]{2,1,0:T(8,128)(2,1)S(1)}) custom-call(bf16[32,2048]{1,0:T(8,128)(2,1)S(1)} %get-tuple-element.32.red_ref, bf16[32,128]{1,0:T(8,128)(2,1)S(1)} %get-tuple-element.38.edge_ref, bf16[256,400]{1,0:T(8,128)(2,1)S(1)} %get-tuple-element.39.weights_ref), custom_call_target="tpu_custom_call" | custom-call | tf_op jit(solution)/shard_map/pallas_call | solution.py:531
  17.5 0.3 %collective-permute-done.2.row_b_ref = bf16[32,384]{1,0:T(8,128)(2,1)S(1)} collective-permute-done((bf16[32,384]{1,0:T(8,128)(2,1)S(1)}, bf16[32,384]{1,0:T(8,128)(2,1)S(1)}, u32[]{:S(2)}, u32[]{:S(2)}) %collective-permute-start.2) | collective-permute-done | bytes 24608 | tf_op jit(solution)/shard_map/ppermute | solution.py:527
  17.8 0.0 collective-permute-done.3.row_a_ref
  17.8 0.6 %shard_map.96.border_ref = bf16[512,512]{1,0:T(8,128)(2,1)S(1)} custom-call(bf16[32,384]{1,0:T(8,128)(2,1)S(1)} %collective-permute-done.2.row_b_ref, bf16[32,384]{1,0:T(8,128)(2,1)S(1)} %collective-permute-done.3.row_a_ref, bf16[256,400]{1,0:T(8,128)(2,1)S(1)} %get-tuple-element.39.weights_ref, bf16[2,400,512]{2,1,0:T(8,128)(2,1)S(1)} %get-tuple-element.43.own_stack_ref), custom_call_target="tpu_custom_call" | custom-call | tf_op jit(solution)/shard_map/pallas_call | solution.py:539
  18.5 0.0 collective-permute-done.4.core_a_ref
  18.5 0.0 collective-permute-done.5.core_b_ref
  18.5 1.5 %shard_map.97 = bf16[64,16,128]{2,1,0:T(8,128)(2,1)} custom-call(bf16[512,1536]{1,0:T(8,128)(2,1)S(1)} %get-tuple-element.40.inner_ref, bf16[512,512]{1,0:T(8,128)(2,1)S(1)} %shard_map.96.border_ref, bf16[2,32,512]{2,1,0:T(8,128)(2,1)S(1)} %collective-permute-done.4.core_a_ref, bf16[2,32,512]{2,1,0:T(8,128)(2,1)S(1)} %collective-permute-done.5.core_b_ref, ...), custom_call_target="tpu_custom_call" | custom-call | tf_op jit(solution)/shard_map/pallas_call | solution.py:548
Async XLA Ops:
  1.6 8.8 %collective-permute-start = (bf16[32,128]{1,0:T(8,128)(2,1)S(1)}, bf16[32,128]{1,0:T(8,128)(2,1)S(1)}, u32[]{:S(2)}, u32[]{:S(2)}) collective-permute-start(bf16[32,128]{1,0:T(8,128)(2,1)S(1)} %get-tuple-element.33), channel_id=1, source_target_pairs={{0,7},{1,2},{2,1},{3,4},{4,3},{5,6},{6,5},{7,0},{8,15},{9,10},{10,... | collective-permute-start | bytes 24584 | tf_op jit(solution)/shard_map/ppermute | solution.py:492
  7.6 3.7 %collective-permute-start.1 = (bf16[32,128]{1,0:T(8,128)(2,1)S(1)}, bf16[32,128]{1,0:T(8,128)(2,1)S(1)}, u32[]{:S(2)}, u32[]{:S(2)}) collective-permute-start(bf16[32,128]{1,0:T(8,128)(2,1)S(1)} %get-tuple-element.34), channel_id=1, source_target_pairs={{0,1},{1,0},{2,3},{3,2},{4,5},{5,4},{6,7},{7,6},{8,9},{9,8},{10,11... | collective-permute-start | bytes 24584 | tf_op jit(solution)/shard_map/ppermute | solution.py:493
  11.4 7.1 %collective-permute-start.4 = (bf16[2,32,512]{2,1,0:T(8,128)(2,1)S(1)}, bf16[2,32,512]{2,1,0:T(8,128)(2,1)S(1)}, u32[]{:S(2)}, u32[]{:S(2)}) collective-permute-start(bf16[2,32,512]{2,1,0:T(8,128)(2,1)S(1)} %get-tuple-element.44), channel_id=1, source_target_pairs={{0,1},{1,0},{2,3},{3,2},{4,5},{5,4},{6,7},{7,6},{8,9},{9,8},{10,11... | collective-permute-start | bytes 196616 | tf_op jit(solution)/shard_map/ppermute | solution.py:525
  11.5 7.0 %collective-permute-start.5 = (bf16[2,32,512]{2,1,0:T(8,128)(2,1)S(1)}, bf16[2,32,512]{2,1,0:T(8,128)(2,1)S(1)}, u32[]{:S(2)}, u32[]{:S(2)}) collective-permute-start(bf16[2,32,512]{2,1,0:T(8,128)(2,1)S(1)} %get-tuple-element.37.core_ref), channel_id=1, source_target_pairs={{0,7},{1,2},{2,1},{3,4},{4,3},{5,6},{6,5},{7,0},{8,15},{9,10},{10,... | collective-permute-start | bytes 196616 | tf_op jit(solution)/shard_map/ppermute | solution.py:524
  14.4 3.4 %collective-permute-start.2 = (bf16[32,384]{1,0:T(8,128)(2,1)S(1)}, bf16[32,384]{1,0:T(8,128)(2,1)S(1)}, u32[]{:S(2)}, u32[]{:S(2)}) collective-permute-start(bf16[32,384]{1,0:T(8,128)(2,1)S(1)} %get-tuple-element.41), channel_id=1, source_target_pairs={{0,24},{8,16},{16,8},{24,0},{1,25},{9,17},{17,9},{25,1},{2,26},{10... | collective-permute-start | bytes 73736 | tf_op jit(solution)/shard_map/ppermute | solution.py:527
  14.4 3.4 %collective-permute-start.3 = (bf16[32,384]{1,0:T(8,128)(2,1)S(1)}, bf16[32,384]{1,0:T(8,128)(2,1)S(1)}, u32[]{:S(2)}, u32[]{:S(2)}) collective-permute-start(bf16[32,384]{1,0:T(8,128)(2,1)S(1)} %get-tuple-element.42), channel_id=1, source_target_pairs={{0,8},{8,0},{16,24},{24,16},{1,9},{9,1},{17,25},{25,17},{2,10},{10... | collective-permute-start | bytes 73736 | tf_op jit(solution)/shard_map/ppermute | solution.py:526

commit v12 on v11

--- a/solution.py
+++ b/solution.py
@@ -394,6 +394,7 @@
     for start in range(REACH, lat_len - REACH, STEP):
         chunks.append((inner_ref, start - REACH, [*range(start, start + STEP)]))
     by_row = {}
+    finished = []
     for ref, first, rows in chunks:
         width = len(rows) * lon_len
         every = jnp.dot(cores, ref[:, first * lon_len : first * lon_len + width], preferred_element_type=F32)
@@ -404,19 +405,17 @@
         hidden = hidden.astype(BF16)
         for i, r in enumerate(rows):
             by_row[r] = hidden[:, i * lon_len : (i + 1) * lon_len]
-    pieces = [by_row[r] for r in range(lat_len)]
-    groups = [jnp.concatenate(pieces[g : g + GROUP], axis=0) for g in range(0, lat_len, GROUP)]
+        group = range(len(finished) * GROUP, (len(finished) + 1) * GROUP)
+        if len(finished) * GROUP < lat_len and all(r in by_row for r in group):
+            stacked = jnp.concatenate([by_row[r] for r in group], axis=0)
+            output = jnp.dot(mixer_ref[...], stacked, preferred_element_type=F32) + offset_ref[...]
+            finished.append(output / (1.0 + jnp.exp(-output)))
     channels = stage_ref.shape[0]
     share = channels // OUT_COPIES
-    outputs = [jnp.dot(mixer_ref[...], hidden, preferred_element_type=F32) for hidden in groups]
     copies = []
     for part in range(OUT_COPIES):
         span = slice(part * share * GROUP, (part + 1) * share * GROUP)
-        blocks = []
-        for output in outputs:
-            output = output[span] + offset_ref[span, :]
-            mixed = 0.5 * output * (1.0 + jnp.tanh(0.5 * output))
-            blocks.append(mixed.reshape(share, GROUP, lon_len))
+        blocks = [mixed[span].reshape(share, GROUP, lon_len) for mixed in finished]
         held = slice(part * share, (part + 1) * share)
         stage_ref[held] = jnp.concatenate(blocks, axis=1).astype(BF16)
         copy = pltpu.make_async_copy(stage_ref.at[held], out_hbm.at[held], sems.at[part])

time: 20.2 us -> 20.5 us (1.015)
  Pallas kernels: 8.22 us -> 8.49 us
    pallas_call x1, Pallas kernels: 1.53 us -> 1.79 us  [on_device(): pl.pallas_call(mix_kernel, out_shape=jax.ShapeDtypeStruct(out_shape, BF16...]
where the time goes in v12:
time: 20.5 us; the launch traced here: 20.3 us
  starting transfers between devices  10.5 us (51%)
  Pallas kernels  8.49 us (41%)
  waiting for transfers between devices  1.24 us (6%)
    ppermute x1, starting transfers between devices, on_device(): got_b = lax.ppermute(pay_b, 'lon', lon_second)  6.04 us
    ppermute x1, starting transfers between devices, on_device(): core_b = lax.ppermute(core_b, 'lon', lon_second)  2.77 us
    pallas_call x1, Pallas kernels, on_device(): pl.pallas_call(functools.partial(prepare_kernel, lon_count, lat_len), out...  2.76 us
    pallas_call x1, Pallas kernels, on_device(): pl.pallas_call(mix_kernel, out_shape=jax.ShapeDtypeStruct(out_shape, BF16...  1.79 us
    ppermute x1, starting transfers between devices, on_device(): row_a = lax.ppermute(row_a, 'lat', lat_first)  1.63 us
    pallas_call x1, Pallas kernels, on_device(): pl.pallas_call(functools.partial(edge_kernel, lon_count), out_shape=(edge...  1.56 us
    pallas_call x1, Pallas kernels, on_device(): pl.pallas_call(functools.partial(inner_kernel, lat_len), out_shape=(jax.S...  1.47 us
    ppermute x1, waiting for transfers between devices, on_device(): got_a = lax.ppermute(pay_a, 'lon', lon_first)  0.87 us
  transfers between devices with their start and end apart: 6, of which 2 were waited for; matrix products, arithmetic and copies ran while one was open for 0% of the time, Pallas kernels for 25%

profile of v12, /device:TPU:0, one launch (start us, length us, event | category | flops | bytes accessed | tf_op | source)
XLA Modules:
  0.0 20.3 jit_solution(975929048799507492)
XLA Ops:
  0.0 1.6 %shard_map.91 = (bf16[32,128]{1,0:T(8,128)(2,1)S(1)}, bf16[32,128]{1,0:T(8,128)(2,1)S(1)}, bf16[112,32,512]{2,1,0:T(8,128)(2,1)S(1)}, bf16[2,32,512]{2,1,0:T(8,1...) custom-call(s32[1,1,6]{2,1,0:T(1,128)} %refs_0_.3, ...), custom_call_target="tpu_custom_call" | custom-call | tf_op jit(solution)/shard_map/pallas_call | solution.py:476
  1.6 6.0 %collective-permute-start = (bf16[32,128]{1,0:T(8,128)(2,1)S(1)}, bf16[32,128]{1,0:T(8,128)(2,1)S(1)}, u32[]{:S(2)}, u32[]{:S(2)}) collective-permute-start(bf16[32,128]{1,0:T(8,128)(2,1)S(1)} %get-tuple-element.33), channel_id=1, source_target_pairs={{0,7},{1,2},{2,1},{3,4},{4,3},{5,6},{6,5},{7,0},{8,15},{9,10},{10,... | collective-permute-start | bytes 24584 | tf_op jit(solution)/shard_map/ppermute | solution.py:491
  7.6 0.0 collective-permute-start.1
  7.6 2.8 %shard_map.92 = (bf16[32,2048]{1,0:T(8,128)(2,1)S(1)}, bf16[112,32,512]{2,1,0:T(8,128)(2,1)S(1)}, bf16[2,32,512]{2,1,0:T(8,128)(2,1)S(1)}, s32[16,128]{1,0:T(8,1...) custom-call(s32[1,1,6]{2,1,0:T(1,128)} %refs_0_.3, s32[896]{0:T(1024)} %refs_1_.3, ...), custom_call_target="tpu_custom_call" | custom-call | flops 1000000 | bytes 7340032 | tf_op jit(solution)/shard_map/pallas_call | solution.py:493
  10.4 0.0 collective-permute-done.got_b_ref
  10.4 0.9 %collective-permute-done.1.got_a_ref = bf16[32,128]{1,0:T(8,128)(2,1)S(1)} collective-permute-done((bf16[32,128]{1,0:T(8,128)(2,1)S(1)}, bf16[32,128]{1,0:T(8,128)(2,1)S(1)}, u32[]{:S(2)}, u32[]{:S(2)}) %collective-permute-start.1) | collective-permute-done | bytes 8224 | tf_op jit(solution)/shard_map/ppermute | solution.py:492
  11.3 0.1 shard_map.93
  11.4 0.1 collective-permute-start.4
  11.5 2.8 %collective-permute-start.5 = (bf16[2,32,512]{2,1,0:T(8,128)(2,1)S(1)}, bf16[2,32,512]{2,1,0:T(8,128)(2,1)S(1)}, u32[]{:S(2)}, u32[]{:S(2)}) collective-permute-start(bf16[2,32,512]{2,1,0:T(8,128)(2,1)S(1)} %get-tuple-element.37.core_ref), channel_id=1, source_target_pairs={{0,7},{1,2},{2,1},{3,4},{4,3},{5,6},{6,5},{7,0},{8,15},{9,10},{10,... | collective-permute-start | bytes 196616 | tf_op jit(solution)/shard_map/ppermute | solution.py:523
  14.3 0.1 shard_map.94
  14.4 0.0 collective-permute-start.2
  14.4 1.6 %collective-permute-start.3 = (bf16[32,384]{1,0:T(8,128)(2,1)S(1)}, bf16[32,384]{1,0:T(8,128)(2,1)S(1)}, u32[]{:S(2)}, u32[]{:S(2)}) collective-permute-start(bf16[32,384]{1,0:T(8,128)(2,1)S(1)} %get-tuple-element.42), channel_id=1, source_target_pairs={{0,8},{8,0},{16,24},{24,16},{1,9},{9,1},{17,25},{25,17},{2,10},{10... | collective-permute-start | bytes 73736 | tf_op jit(solution)/shard_map/ppermute | solution.py:525
  16.0 1.5 %shard_map.95 = (bf16[512,1536]{1,0:T(8,128)(2,1)S(1)}, bf16[2,400,512]{2,1,0:T(8,128)(2,1)S(1)}) custom-call(bf16[32,2048]{1,0:T(8,128)(2,1)S(1)} %get-tuple-element.32.red_ref, bf16[32,128]{1,0:T(8,128)(2,1)S(1)} %get-tuple-element.38.edge_ref, bf16[256,400]{1,0:T(8,128)(2,1)S(1)} %get-tuple-element.39.weights_ref), custom_call_target="tpu_custom_call" | custom-call | tf_op jit(solution)/shard_map/pallas_call | solution.py:530
  17.5 0.3 %collective-permute-done.2.row_b_ref = bf16[32,384]{1,0:T(8,128)(2,1)S(1)} collective-permute-done((bf16[32,384]{1,0:T(8,128)(2,1)S(1)}, bf16[32,384]{1,0:T(8,128)(2,1)S(1)}, u32[]{:S(2)}, u32[]{:S(2)}) %collective-permute-start.2) | collective-permute-done | bytes 24608 | tf_op jit(solution)/shard_map/ppermute | solution.py:526
  17.8 0.0 collective-permute-done.3.row_a_ref
  17.8 0.6 %shard_map.96.border_ref = bf16[512,512]{1,0:T(8,128)(2,1)S(1)} custom-call(bf16[32,384]{1,0:T(8,128)(2,1)S(1)} %collective-permute-done.2.row_b_ref, bf16[32,384]{1,0:T(8,128)(2,1)S(1)} %collective-permute-done.3.row_a_ref, bf16[256,400]{1,0:T(8,128)(2,1)S(1)} %get-tuple-element.39.weights_ref, bf16[2,400,512]{2,1,0:T(8,128)(2,1)S(1)} %get-tuple-element.43.own_stack_ref), custom_call_target="tpu_custom_call" | custom-call | tf_op jit(solution)/shard_map/pallas_call | solution.py:538
  18.5 0.0 collective-permute-done.4.core_a_ref
  18.5 0.0 collective-permute-done.5.core_b_ref
  18.5 1.8 %shard_map.97 = bf16[64,16,128]{2,1,0:T(8,128)(2,1)} custom-call(bf16[512,1536]{1,0:T(8,128)(2,1)S(1)} %get-tuple-element.40.inner_ref, bf16[512,512]{1,0:T(8,128)(2,1)S(1)} %shard_map.96.border_ref, bf16[2,32,512]{2,1,0:T(8,128)(2,1)S(1)} %collective-permute-done.4.core_a_ref, bf16[2,32,512]{2,1,0:T(8,128)(2,1)S(1)} %collective-permute-done.5.core_b_ref, ...), custom_call_target="tpu_custom_call" | custom-call | tf_op jit(solution)/shard_map/pallas_call | solution.py:547
Async XLA Ops:
  1.6 8.8 %collective-permute-start = (bf16[32,128]{1,0:T(8,128)(2,1)S(1)}, bf16[32,128]{1,0:T(8,128)(2,1)S(1)}, u32[]{:S(2)}, u32[]{:S(2)}) collective-permute-start(bf16[32,128]{1,0:T(8,128)(2,1)S(1)} %get-tuple-element.33), channel_id=1, source_target_pairs={{0,7},{1,2},{2,1},{3,4},{4,3},{5,6},{6,5},{7,0},{8,15},{9,10},{10,... | collective-permute-start | bytes 24584 | tf_op jit(solution)/shard_map/ppermute | solution.py:491
  7.6 3.7 %collective-permute-start.1 = (bf16[32,128]{1,0:T(8,128)(2,1)S(1)}, bf16[32,128]{1,0:T(8,128)(2,1)S(1)}, u32[]{:S(2)}, u32[]{:S(2)}) collective-permute-start(bf16[32,128]{1,0:T(8,128)(2,1)S(1)} %get-tuple-element.34), channel_id=1, source_target_pairs={{0,1},{1,0},{2,3},{3,2},{4,5},{5,4},{6,7},{7,6},{8,9},{9,8},{10,11... | collective-permute-start | bytes 24584 | tf_op jit(solution)/shard_map/ppermute | solution.py:492
  11.4 7.1 %collective-permute-start.4 = (bf16[2,32,512]{2,1,0:T(8,128)(2,1)S(1)}, bf16[2,32,512]{2,1,0:T(8,128)(2,1)S(1)}, u32[]{:S(2)}, u32[]{:S(2)}) collective-permute-start(bf16[2,32,512]{2,1,0:T(8,128)(2,1)S(1)} %get-tuple-element.44), channel_id=1, source_target_pairs={{0,1},{1,0},{2,3},{3,2},{4,5},{5,4},{6,7},{7,6},{8,9},{9,8},{10,11... | collective-permute-start | bytes 196616 | tf_op jit(solution)/shard_map/ppermute | solution.py:524
  11.5 7.0 %collective-permute-start.5 = (bf16[2,32,512]{2,1,0:T(8,128)(2,1)S(1)}, bf16[2,32,512]{2,1,0:T(8,128)(2,1)S(1)}, u32[]{:S(2)}, u32[]{:S(2)}) collective-permute-start(bf16[2,32,512]{2,1,0:T(8,128)(2,1)S(1)} %get-tuple-element.37.core_ref), channel_id=1, source_target_pairs={{0,7},{1,2},{2,1},{3,4},{4,3},{5,6},{6,5},{7,0},{8,15},{9,10},{10,... | collective-permute-start | bytes 196616 | tf_op jit(solution)/shard_map/ppermute | solution.py:523
  14.4 3.4 %collective-permute-start.2 = (bf16[32,384]{1,0:T(8,128)(2,1)S(1)}, bf16[32,384]{1,0:T(8,128)(2,1)S(1)}, u32[]{:S(2)}, u32[]{:S(2)}) collective-permute-start(bf16[32,384]{1,0:T(8,128)(2,1)S(1)} %get-tuple-element.41), channel_id=1, source_target_pairs={{0,24},{8,16},{16,8},{24,0},{1,25},{9,17},{17,9},{25,1},{2,26},{10... | collective-permute-start | bytes 73736 | tf_op jit(solution)/shard_map/ppermute | solution.py:526
  14.4 3.4 %collective-permute-start.3 = (bf16[32,384]{1,0:T(8,128)(2,1)S(1)}, bf16[32,384]{1,0:T(8,128)(2,1)S(1)}, u32[]{:S(2)}, u32[]{:S(2)}) collective-permute-start(bf16[32,384]{1,0:T(8,128)(2,1)S(1)} %get-tuple-element.42), channel_id=1, source_target_pairs={{0,8},{8,0},{16,24},{24,16},{1,9},{9,1},{17,25},{25,17},{2,10},{10... | collective-permute-start | bytes 73736 | tf_op jit(solution)/shard_map/ppermute | solution.py:525

commit v13 on v11

--- a/solution.py
+++ b/solution.py
@@ -16,8 +16,6 @@
 STEP = 4
 OUT_COPIES = 4
 IN_COPIES = 4
-BANK_COPIES = 8
-EARLY = 1
 F32 = jnp.float32
 BF16 = jnp.bfloat16
 VMEM = pl.BlockSpec(memory_space=pltpu.VMEM)
@@ -72,26 +70,16 @@
     return places, rows
 
 
-def is_early():
-    return lax.axis_index("lon") == EARLY
-
-
 class Held:
-    names = ("bank", "own", "position", "weights", "mixer", "offset")
+    names = ("own", "position", "weights", "mixer", "offset")
     sources = ("labels", "tap", "out_factor", "bias")
 
     def __init__(self, refs):
         self.__dict__.update(zip(self.names, refs))
 
 
-def start_sources(sources, targets, bank_hbm, bank_ref, sems):
-    pairs = tuple(zip(sources, targets))
-    return start_copies(pairs + in_parts(bank_hbm, bank_ref, BANK_COPIES), sems)
-
-
-def build_held(lon_count, list_ref, slot_ref, targets, copies, held):
+def build_held(places, targets, held):
     labels_ref, tap_ref, out_factor_ref, bias_ref = targets
-    places, rows = find_rows(list_ref, slot_ref, lon_count, held.bank.shape[0])
     even = (lax.axis_index("lon") % 2) == 0
     order = list(places[0])
     order += [jnp.where(even, places[2][nth], places[1][nth]) for nth in range(PER_OWNER)]
@@ -136,10 +124,6 @@
     mine = lax.broadcasted_iota(jnp.int32, shape, 0) // GROUP == lane_index(shape)
     offset = jnp.sum(jnp.where(mine, bias_ref[...], 0.0), axis=1, keepdims=True)
     held.offset[...] = jnp.broadcast_to(offset, held.offset.shape)
-    for copy in copies:
-        copy.wait()
-    for nth in range(PER_OWNER):
-        held.own[nth] = held.bank[rows[0][nth]]
 
 
 def asked_rows(list_ref, slots_ref, owner, held):
@@ -156,12 +140,9 @@
     return least, greatest
 
 
-def edge_kernel(lon_count, *refs):
-    list_hbm, slot_hbm, feat_hbm, in_hbm, bank_hbm = refs[:5]
-    sources, slots_hbm, (pay_a_ref, pay_b_ref), held_refs = refs[5:9], refs[9], refs[10:12], refs[12:18]
-    list_ref, slot_ref, feat_ref, in_ref, turned_ref, slots_ref = refs[18:24]
-    targets, sems, held_sems = refs[24:28], refs[28], refs[29]
-    held = Held(held_refs)
+def edge_kernel(lon_count, held_rows, *refs):
+    list_hbm, slots_hbm, feat_hbm, in_hbm, pay_a_ref, pay_b_ref = refs[:6]
+    list_ref, slots_ref, feat_ref, in_ref, turned_ref, sems = refs[6:]
     channels, lat_len, lon_len = feat_ref.shape
     rank = in_ref.shape[0]
     batch = LANES // EDGE
@@ -191,18 +172,9 @@
         (pay_b_ref, jnp.where(even, prev, following)),
     ):
         load = edges
-        for nth, row in enumerate(asked_rows(list_ref, slots_ref, owner, held.bank.shape[0])):
+        for nth, row in enumerate(asked_rows(list_ref, slots_ref, owner, held_rows)):
             load = jnp.where(lane == EDGE * lat_len + nth, row.astype(F32), load)
         out_ref[...] = load.astype(BF16)
-
-    @pl.when(is_early())
-    def _():
-        copies = start_sources(sources, targets, bank_hbm, held.bank, held_sems)
-        scalars = pltpu.make_async_copy(slot_hbm, slot_ref, sems.at[0])
-        scalars.start()
-        for copy in [scalars, *copies[: len(targets)]]:
-            copy.wait()
-        build_held(lon_count, list_ref, slot_ref, targets, copies[len(targets) :], held)
 
 
 def reduce_tile(lat_len, feat_ref, in_ref, rows_ref, red_ref):
@@ -216,41 +188,28 @@
 
 def prepare_kernel(lon_count, lat_len, *refs):
     list_hbm, slot_hbm, feat_hbm, in_hbm, bank_hbm = refs[:5]
-    sources, given = refs[5:9], Held((None, *refs[9:14]))
-    red_ref, held = refs[14], Held(refs[15:21])
-    list_ref, slot_ref, feat_ref, in_ref, rows_ref = refs[21:26]
-    targets, sems, held_sems = refs[26:30], refs[30], refs[31]
-    early = is_early()
-    shared = in_parts(feat_hbm, feat_ref, IN_COPIES) + ((in_hbm, in_ref),)
-    lists = ((slot_hbm, slot_ref), (list_hbm, list_ref))
-
-    @pl.when(early)
-    def _():
-        copies = start_copies(shared, sems)
-        for name in held.names[1:]:
-            getattr(held, name)[...] = getattr(given, name)[...]
-        for copy in copies:
-            copy.wait()
-        reduce_tile(lat_len, feat_ref, in_ref, rows_ref, red_ref)
-
-    @pl.when(jnp.logical_not(early))
-    def _():
-        copies = start_copies(shared + lists, sems)
-        others = start_sources(sources, targets, bank_hbm, held.bank, held_sems)
-        for copy in copies + others[: len(targets)]:
-            copy.wait()
-        reduce_tile(lat_len, feat_ref, in_ref, rows_ref, red_ref)
-        build_held(lon_count, list_ref, slot_ref, targets, others[len(targets) :], held)
-
-
-def pick_kernel(lat_len, got_b_ref, got_a_ref, early_bank_ref, late_bank_ref, core_a_ref, core_b_ref):
-    early = is_early()
+    sources, red_ref, held = refs[5:9], refs[10], Held(refs[11:16])
+    list_ref, slot_ref, feat_ref, in_ref, rows_ref = refs[16:21]
+    targets, sems = refs[21:25], refs[25]
+    pairs = ((list_hbm, list_ref), (slot_hbm, slot_ref)) + in_parts(feat_hbm, feat_ref, IN_COPIES)
+    pairs += ((in_hbm, in_ref), *zip(sources, targets))
+    for copy in start_copies(pairs, sems):
+        copy.wait()
+    places, rows = find_rows(list_ref, slot_ref, lon_count, bank_hbm.shape[0])
+    own = start_copies(tuple((bank_hbm.at[row], held.own.at[nth]) for nth, row in enumerate(rows[0])), sems)
+    reduce_tile(lat_len, feat_ref, in_ref, rows_ref, red_ref)
+    build_held(places, targets, held)
+    for copy in own:
+        copy.wait()
+
+
+def pick_kernel(lat_len, got_b_ref, got_a_ref, own_hbm, bank_ref, core_a_ref, core_b_ref):
     lane = lane_index((1, LANES))
     for got_ref, core_ref in ((got_b_ref, core_b_ref), (got_a_ref, core_a_ref)):
         head = got_ref[...].astype(F32)[0:1, :]
         for nth in range(PER_OWNER):
             row = jnp.sum(jnp.where(lane == EDGE * lat_len + nth, head, 0.0)).astype(jnp.int32)
-            core_ref[nth] = jnp.where(early, early_bank_ref[row], late_bank_ref[row])
+            core_ref[nth] = bank_ref[row]
 
 
 def rows_kernel(lat_len, got_b_ref, got_a_ref, core_ref, red_ref, edge_ref, row_a_ref, row_b_ref):
@@ -441,7 +400,6 @@
     edge_shape = jax.ShapeDtypeStruct((rank, LANES), BF16)
     core_shape = jax.ShapeDtypeStruct((PER_OWNER, core_rows, core_cols), BF16)
     held_shapes = (
-        jax.ShapeDtypeStruct(kernel_bank.shape, BF16),
         core_shape,
         jax.ShapeDtypeStruct(labels.shape, jnp.int32),
         jax.ShapeDtypeStruct((tap_rank * rank // 2, taps * rank // 2), BF16),
@@ -474,46 +432,45 @@
             out_bias.reshape(1, -1),
         )
     )
-    pay_a, pay_b, early_bank, *given = pl.pallas_call(
-        functools.partial(edge_kernel, lon_count),
-        out_shape=(edge_shape, edge_shape, *held_shapes),
-        in_specs=[HBM] * 10,
-        out_specs=(VMEM,) * 8,
+    pay_a, pay_b = pl.pallas_call(
+        functools.partial(edge_kernel, lon_count, held),
+        out_shape=(edge_shape, edge_shape),
+        in_specs=[HBM] * 4,
+        out_specs=(VMEM,) * 2,
         scratch_shapes=[
-            *lists,
+            lists[0],
+            pltpu.VMEM((bank_slot.shape[0] // LANES, LANES), jnp.int32),
+            *lists[2:],
             pltpu.VMEM((channels * EDGE, lat_len), F32),
-            pltpu.VMEM((bank_slot.shape[0] // LANES, LANES), jnp.int32),
-            *targets,
             pltpu.SemaphoreType.DMA((IN_COPIES + 3,)),
-            pltpu.SemaphoreType.DMA((4 + BANK_COPIES,)),
         ],
         compiler_params=PARAMS,
-    )(*sources, in_hbm(bank_slot.reshape(-1, LANES)))
+        cost_estimate=pl.CostEstimate(flops=2 * 10**9, bytes_accessed=4 * 10**6, transcendentals=0),
+    )(sources[0], in_hbm(bank_slot.reshape(-1, LANES)), *sources[2:4])
     got_b = lax.ppermute(pay_b, "lon", lon_second)
     got_a = lax.ppermute(pay_a, "lon", lon_first)
-    reduced, late_bank, own, position, weights, mixer, offset = pl.pallas_call(
+    reduced, own, position, weights, mixer, offset = pl.pallas_call(
         functools.partial(prepare_kernel, lon_count, lat_len),
         out_shape=(jax.ShapeDtypeStruct((rank, cells), BF16), *held_shapes),
-        in_specs=[HBM] * 9 + [VMEM] * 5,
-        out_specs=(VMEM,) * 7,
+        in_specs=[HBM] * 9 + [HBM],
+        out_specs=(VMEM,) * 6,
         scratch_shapes=[
             *lists,
             pltpu.VMEM((channels * lat_len, lon_len), F32),
             *targets,
-            pltpu.SemaphoreType.DMA((IN_COPIES + 3,)),
-            pltpu.SemaphoreType.DMA((4 + BANK_COPIES,)),
+            pltpu.SemaphoreType.DMA((IN_COPIES + 7,)),
         ],
         compiler_params=PARAMS,
-        cost_estimate=pl.CostEstimate(flops=10**6, bytes_accessed=kernel_bank.size * 4, transcendentals=0),
-    )(*sources, *given)
+        cost_estimate=pl.CostEstimate(flops=10**5, bytes_accessed=10**5, transcendentals=0),
+    )(*sources, pay_a)
     row_shape = jax.ShapeDtypeStruct((rank, REACH * lon_len + LANES), BF16)
     core_a, core_b = pl.pallas_call(
         functools.partial(pick_kernel, lat_len),
         out_shape=(core_shape, core_shape),
-        in_specs=[VMEM] * 4,
+        in_specs=[VMEM, VMEM, HBM, VMEM],
         out_specs=(VMEM,) * 2,
         compiler_params=PARAMS,
-    )(got_b, got_a, early_bank, late_bank)
+    )(got_b, got_a, own, kernel_bank)
     edges, row_a, row_b = pl.pallas_call(
         functools.partial(rows_kernel, lat_len),
         out_shape=(edge_shape, row_shape, row_shape),

time: 20.2 us -> 20.9 us (1.035)
  waiting for transfers between devices: 1.24 us -> 2.34 us
  Pallas kernels: 8.22 us -> 7.69 us
    ppermute x1, starting transfers between devices: 0.07 us -> 0.82 us  [on_device(): core_a = lax.ppermute(core_a, 'lon', lon_first)]
    ppermute x1, starting transfers between devices: 2.77 us -> 2.03 us  [on_device(): core_b = lax.ppermute(core_b, 'lon', lon_second)]
    ppermute x1, waiting for transfers between devices: 0.03 us -> 0.7 us  [on_device(): core_b = lax.ppermute(core_b, 'lon', lon_second)]
    ppermute x1, waiting for transfers between devices: 0.87 us -> 1.29 us  [on_device(): got_a = lax.ppermute(pay_a, 'lon', lon_first)]
    pallas_call x1, Pallas kernels: 2.76 us -> 2.34 us  [on_device(): pl.pallas_call(functools.partial(prepare_kernel, lon_count, lat_len), out...]
  transfers between devices with their start and end apart: 6 -> 6, of which waited for: 2 -> 3; matrix products, arithmetic and copies ran while one was open for 0% -> 0% of each run, Pallas kernels for 25% -> 22%
where the time goes in v13:
time: 20.9 us; the launch traced here: 20.6 us
  starting transfers between devices  10.5 us (50%)
  Pallas kernels  7.69 us (37%)
  waiting for transfers between devices  2.34 us (11%)
    ppermute x1, starting transfers between devices, on_device(): got_b = lax.ppermute(pay_b, 'lon', lon_second)  6.04 us
    pallas_call x1, Pallas kernels, on_device(): pl.pallas_call(functools.partial(prepare_kernel, lon_count, lat_len), out...  2.34 us
    ppermute x1, starting transfers between devices, on_device(): core_b = lax.ppermute(core_b, 'lon', lon_second)  2.03 us
    ppermute x1, starting transfers between devices, on_device(): row_a = lax.ppermute(row_a, 'lat', lat_first)  1.63 us
    pallas_call x1, Pallas kernels, on_device(): pl.pallas_call(mix_kernel, out_shape=jax.ShapeDtypeStruct(out_shape, BF16...  1.53 us
    pallas_call x1, Pallas kernels, on_device(): pl.pallas_call(functools.partial(inner_kernel, lat_len), out_shape=(jax.S...  1.46 us
    pallas_call x1, Pallas kernels, on_device(): pl.pallas_call(functools.partial(edge_kernel, lon_count, held), out_shape...  1.45 us
    ppermute x1, waiting for transfers between devices, on_device(): got_a = lax.ppermute(pay_a, 'lon', lon_first)  1.29 us
  transfers between devices with their start and end apart: 6, of which 3 were waited for; matrix products, arithmetic and copies ran while one was open for 0% of the time, Pallas kernels for 22%

profile of v13, /device:TPU:0, one launch (start us, length us, event | category | flops | bytes accessed | tf_op | source)
XLA Modules:
  0.0 20.6 jit_solution(12785191693317952142)
XLA Ops:
  0.0 1.5 %shard_map.91 = (bf16[32,128]{1,0:T(8,128)(2,1)S(1)}, bf16[32,128]{1,0:T(8,128)(2,1)S(1)}) custom-call(s32[1,1,6]{2,1,0:T(1,128)} %refs_0_.3, s32[7,128]{1,0:T(8,128)} %bitcast.4, bf16[64,16,128]{2,1,0:T(8,128)(2,1)} %refs_2_.3, bf16[32,64]{1,0:T(8,128)(2,1)} %refs_3_.3), custom_call_target="tpu_custom_call" | custom-call | flops 2000000000 | bytes 4000000 | tf_op jit(solution)/shard_map/pallas_call | solution.py:435
  1.5 0.0 copy-start
  1.5 6.0 %collective-permute-start = (bf16[32,128]{1,0:T(8,128)(2,1)S(1)}, bf16[32,128]{1,0:T(8,128)(2,1)S(1)}, u32[]{:S(2)}, u32[]{:S(2)}) collective-permute-start(bf16[32,128]{1,0:T(8,128)(2,1)S(1)} %get-tuple-element.22), channel_id=1, source_target_pairs={{0,7},{1,2},{2,1},{3,4},{4,3},{5,6},{6,5},{7,0},{8,15},{9,10},{10,... | collective-permute-start | bytes 24584 | tf_op jit(solution)/shard_map/ppermute | solution.py:450
  7.5 0.0 collective-permute-start.1
  7.5 2.3 %shard_map.92 = (bf16[32,2048]{1,0:T(8,128)(2,1)S(1)}, bf16[2,32,512]{2,1,0:T(8,128)(2,1)S(1)}, s32[16,128]{1,0:T(8,128)S(1)}, bf16[256,400]{1,0:T(8,128)(2,1)S(...) custom-call(s32[1,1,6]{2,1,0:T(1,128)} %refs_0_.3, s32[896]{0:T(1024)} %refs_1_.1, ...), custom_call_target="tpu_custom_call" | custom-call | flops 100000 | bytes 100000 | tf_op jit(solution)/shard_map/pallas_call | solution.py:452
  9.9 0.0 collective-permute-done.got_b_ref
  9.9 1.3 %collective-permute-done.1.got_a_ref = bf16[32,128]{1,0:T(8,128)(2,1)S(1)} collective-permute-done((bf16[32,128]{1,0:T(8,128)(2,1)S(1)}, bf16[32,128]{1,0:T(8,128)(2,1)S(1)}, u32[]{:S(2)}, u32[]{:S(2)}) %collective-permute-start.1) | collective-permute-done | bytes 8224 | tf_op jit(solution)/shard_map/ppermute | solution.py:451
  11.2 0.0 copy-done
  11.2 0.1 shard_map.93
  11.3 0.8 %collective-permute-start.4 = (bf16[2,32,512]{2,1,0:T(8,128)(2,1)S(1)}, bf16[2,32,512]{2,1,0:T(8,128)(2,1)S(1)}, u32[]{:S(2)}, u32[]{:S(2)}) collective-permute-start(bf16[2,32,512]{2,1,0:T(8,128)(2,1)S(1)} %get-tuple-element.31), channel_id=1, source_target_pairs={{0,1},{1,0},{2,3},{3,2},{4,5},{5,4},{6,7},{7,6},{8,9},{9,8},{10,11... | collective-permute-start | bytes 196616 | tf_op jit(solution)/shard_map/ppermute | solution.py:482
  12.1 2.0 %collective-permute-start.5 = (bf16[2,32,512]{2,1,0:T(8,128)(2,1)S(1)}, bf16[2,32,512]{2,1,0:T(8,128)(2,1)S(1)}, u32[]{:S(2)}, u32[]{:S(2)}) collective-permute-start(bf16[2,32,512]{2,1,0:T(8,128)(2,1)S(1)} %get-tuple-element.24.core_ref), channel_id=1, source_target_pairs={{0,7},{1,2},{2,1},{3,4},{4,3},{5,6},{6,5},{7,0},{8,15},{9,10},{10,... | collective-permute-start | bytes 196616 | tf_op jit(solution)/shard_map/ppermute | solution.py:481
  14.2 0.1 shard_map.94
  14.3 0.0 collective-permute-start.2
  14.3 1.6 %collective-permute-start.3 = (bf16[32,384]{1,0:T(8,128)(2,1)S(1)}, bf16[32,384]{1,0:T(8,128)(2,1)S(1)}, u32[]{:S(2)}, u32[]{:S(2)}) collective-permute-start(bf16[32,384]{1,0:T(8,128)(2,1)S(1)} %get-tuple-element.29), channel_id=1, source_target_pairs={{0,8},{8,0},{16,24},{24,16},{1,9},{9,1},{17,25},{25,17},{2,10},{10... | collective-permute-start | bytes 73736 | tf_op jit(solution)/shard_map/ppermute | solution.py:483
  15.9 1.5 %shard_map.95 = (bf16[512,1536]{1,0:T(8,128)(2,1)S(1)}, bf16[2,400,512]{2,1,0:T(8,128)(2,1)S(1)}) custom-call(bf16[32,2048]{1,0:T(8,128)(2,1)S(1)} %get-tuple-element.21.red_ref, bf16[32,128]{1,0:T(8,128)(2,1)S(1)} %get-tuple-element.25.edge_ref, bf16[256,400]{1,0:T(8,128)(2,1)S(1)} %get-tuple-element.26.weights_ref), custom_call_target="tpu_custom_call" | custom-call | tf_op jit(solution)/shard_map/pallas_call | solution.py:488
  17.4 0.3 %collective-permute-done.2.row_b_ref = bf16[32,384]{1,0:T(8,128)(2,1)S(1)} collective-permute-done((bf16[32,384]{1,0:T(8,128)(2,1)S(1)}, bf16[32,384]{1,0:T(8,128)(2,1)S(1)}, u32[]{:S(2)}, u32[]{:S(2)}) %collective-permute-start.2) | collective-permute-done | bytes 24608 | tf_op jit(solution)/shard_map/ppermute | solution.py:484
  17.7 0.0 collective-permute-done.3.row_a_ref
  17.7 0.6 %shard_map.96.border_ref = bf16[512,512]{1,0:T(8,128)(2,1)S(1)} custom-call(bf16[32,384]{1,0:T(8,128)(2,1)S(1)} %collective-permute-done.2.row_b_ref, bf16[32,384]{1,0:T(8,128)(2,1)S(1)} %collective-permute-done.3.row_a_ref, bf16[256,400]{1,0:T(8,128)(2,1)S(1)} %get-tuple-element.26.weights_ref, bf16[2,400,512]{2,1,0:T(8,128)(2,1)S(1)} %get-tuple-element.30.own_stack_ref), custom_call_target="tpu_custom_call" | custom-call | tf_op jit(solution)/shard_map/pallas_call | solution.py:496
  18.4 0.0 collective-permute-done.4.core_a_ref
  18.4 0.7 %collective-permute-done.5.core_b_ref = bf16[2,32,512]{2,1,0:T(8,128)(2,1)S(1)} collective-permute-done((bf16[2,32,512]{2,1,0:T(8,128)(2,1)S(1)}, bf16[2,32,512]{2,1,0:T(8,128)(2,1)S(1)}, u32[]{:S(2)}, u32[]{:S(2)}) %collective-permute-start.5) | collective-permute-done | bytes 65568 | tf_op jit(solution)/shard_map/ppermute | solution.py:481
  19.1 1.5 %shard_map.97 = bf16[64,16,128]{2,1,0:T(8,128)(2,1)} custom-call(bf16[512,1536]{1,0:T(8,128)(2,1)S(1)} %get-tuple-element.27.inner_ref, bf16[512,512]{1,0:T(8,128)(2,1)S(1)} %shard_map.96.border_ref, bf16[2,32,512]{2,1,0:T(8,128)(2,1)S(1)} %collective-permute-done.4.core_a_ref, bf16[2,32,512]{2,1,0:T(8,128)(2,1)S(1)} %collective-permute-done.5.core_b_ref, ...), custom_call_target="tpu_custom_call" | custom-call | tf_op jit(solution)/shard_map/pallas_call | solution.py:505
Async XLA Ops:
  1.5 9.7 %copy-start = (bf16[112,32,512]{2,1,0:T(8,128)(2,1)S(1)}, bf16[112,32,512]{2,1,0:T(8,128)(2,1)}, u32[]{:S(2)}) copy-start(bf16[112,32,512]{2,1,0:T(8,128)(2,1)} %bank_ref.1) | copy-start | bytes 11010052
  1.5 8.4 %collective-permute-start = (bf16[32,128]{1,0:T(8,128)(2,1)S(1)}, bf16[32,128]{1,0:T(8,128)(2,1)S(1)}, u32[]{:S(2)}, u32[]{:S(2)}) collective-permute-start(bf16[32,128]{1,0:T(8,128)(2,1)S(1)} %get-tuple-element.22), channel_id=1, source_target_pairs={{0,7},{1,2},{2,1},{3,4},{4,3},{5,6},{6,5},{7,0},{8,15},{9,10},{10,... | collective-permute-start | bytes 24584 | tf_op jit(solution)/shard_map/ppermute | solution.py:450
  7.5 3.7 %collective-permute-start.1 = (bf16[32,128]{1,0:T(8,128)(2,1)S(1)}, bf16[32,128]{1,0:T(8,128)(2,1)S(1)}, u32[]{:S(2)}, u32[]{:S(2)}) collective-permute-start(bf16[32,128]{1,0:T(8,128)(2,1)S(1)} %get-tuple-element.20.refs_9_), channel_id=1, source_target_pairs={{0,1},{1,0},{2,3},{3,2},{4,5},{5,4},{6,7},{7,6},{8,9},{9,8},{10,11... | collective-permute-start | bytes 24584 | tf_op jit(solution)/shard_map/ppermute | solution.py:451
  11.3 7.1 %collective-permute-start.4 = (bf16[2,32,512]{2,1,0:T(8,128)(2,1)S(1)}, bf16[2,32,512]{2,1,0:T(8,128)(2,1)S(1)}, u32[]{:S(2)}, u32[]{:S(2)}) collective-permute-start(bf16[2,32,512]{2,1,0:T(8,128)(2,1)S(1)} %get-tuple-element.31), channel_id=1, source_target_pairs={{0,1},{1,0},{2,3},{3,2},{4,5},{5,4},{6,7},{7,6},{8,9},{9,8},{10,11... | collective-permute-start | bytes 196616 | tf_op jit(solution)/shard_map/ppermute | solution.py:482
  12.1 7.0 %collective-permute-start.5 = (bf16[2,32,512]{2,1,0:T(8,128)(2,1)S(1)}, bf16[2,32,512]{2,1,0:T(8,128)(2,1)S(1)}, u32[]{:S(2)}, u32[]{:S(2)}) collective-permute-start(bf16[2,32,512]{2,1,0:T(8,128)(2,1)S(1)} %get-tuple-element.24.core_ref), channel_id=1, source_target_pairs={{0,7},{1,2},{2,1},{3,4},{4,3},{5,6},{6,5},{7,0},{8,15},{9,10},{10,... | collective-permute-start | bytes 196616 | tf_op jit(solution)/shard_map/ppermute | solution.py:481
  14.3 3.4 %collective-permute-start.2 = (bf16[32,384]{1,0:T(8,128)(2,1)S(1)}, bf16[32,384]{1,0:T(8,128)(2,1)S(1)}, u32[]{:S(2)}, u32[]{:S(2)}) collective-permute-start(bf16[32,384]{1,0:T(8,128)(2,1)S(1)} %get-tuple-element.28), channel_id=1, source_target_pairs={{0,24},{8,16},{16,8},{24,0},{1,25},{9,17},{17,9},{25,1},{2,26},{10... | collective-permute-start | bytes 73736 | tf_op jit(solution)/shard_map/ppermute | solution.py:484
  14.3 3.4 %collective-permute-start.3 = (bf16[32,384]{1,0:T(8,128)(2,1)S(1)}, bf16[32,384]{1,0:T(8,128)(2,1)S(1)}, u32[]{:S(2)}, u32[]{:S(2)}) collective-permute-start(bf16[32,384]{1,0:T(8,128)(2,1)S(1)} %get-tuple-element.29), channel_id=1, source_target_pairs={{0,8},{8,0},{16,24},{24,16},{1,9},{9,1},{17,25},{25,17},{2,10},{10... | collective-permute-start | bytes 73736 | tf_op jit(solution)/shard_map/ppermute | solution.py:483

commit v14 on v13

--- a/solution.py
+++ b/solution.py
@@ -71,15 +71,15 @@
 
 
 class Held:
-    names = ("own", "position", "weights", "mixer", "offset")
-    sources = ("labels", "tap", "out_factor", "bias")
+    names = ("own", "position", "weights")
+    sources = ("labels", "tap")
 
     def __init__(self, refs):
         self.__dict__.update(zip(self.names, refs))
 
 
 def build_held(places, targets, held):
-    labels_ref, tap_ref, out_factor_ref, bias_ref = targets
+    labels_ref, tap_ref = targets
     even = (lax.axis_index("lon") % 2) == 0
     order = list(places[0])
     order += [jnp.where(even, places[2][nth], places[1][nth]) for nth in range(PER_OWNER)]
@@ -90,9 +90,8 @@
         position = jnp.where(labels == place, index, position)
     held.position[...] = position
 
-    rank, out_channels = out_factor_ref.shape
-    half = rank // 2
     tap_rank, taps = tap_ref.shape
+    half = held.weights.shape[0] // tap_rank
     shape = (tap_rank * half, taps * half)
     spread = (
         lax.broadcasted_iota(jnp.int32, (shape[0], tap_rank), 0) // half == lane_index((shape[0], tap_rank))
@@ -105,6 +104,9 @@
     same = lax.broadcasted_iota(jnp.int32, shape, 0) % half == lane_index(shape) % half
     held.weights[...] = jnp.where(same, wide, 0.0).astype(BF16)
 
+
+def build_mixer(out_factor_ref, bias_ref, mixer_ref, offset_ref):
+    rank, out_channels = out_factor_ref.shape
     shape = (out_channels * GROUP, rank * GROUP)
     spread = (
         lax.broadcasted_iota(jnp.int32, (shape[0], out_channels), 0) // GROUP
@@ -118,12 +120,18 @@
     ).astype(BF16)
     wide = jnp.dot(tall, repeat, preferred_element_type=F32)
     same = lax.broadcasted_iota(jnp.int32, shape, 0) % GROUP == lane_index(shape) // rank
-    held.mixer[...] = jnp.where(same, wide, 0.0).astype(BF16)
-
-    shape = (out_channels * GROUP, out_channels)
-    mine = lax.broadcasted_iota(jnp.int32, shape, 0) // GROUP == lane_index(shape)
-    offset = jnp.sum(jnp.where(mine, bias_ref[...], 0.0), axis=1, keepdims=True)
-    held.offset[...] = jnp.broadcast_to(offset, held.offset.shape)
+    mixer_ref[...] = jnp.where(same, wide, 0.0).astype(BF16)
+
+    square = (out_channels, out_channels)
+    diagonal = lax.broadcasted_iota(jnp.int32, square, 0) == lane_index(square)
+    column = jnp.sum(jnp.where(diagonal, bias_ref[...], 0.0), axis=1, keepdims=True)
+    rest = jnp.broadcast_to(column, (out_channels, offset_ref.shape[1]))
+    total = jnp.zeros(offset_ref.shape, F32)
+    for _ in range(3):
+        piece = rest.astype(BF16)
+        rest = rest - piece.astype(F32)
+        total = total + jnp.dot(spread, piece, preferred_element_type=F32)
+    offset_ref[...] = total
 
 
 def asked_rows(list_ref, slots_ref, owner, held):
@@ -188,9 +196,9 @@
 
 def prepare_kernel(lon_count, lat_len, *refs):
     list_hbm, slot_hbm, feat_hbm, in_hbm, bank_hbm = refs[:5]
-    sources, red_ref, held = refs[5:9], refs[10], Held(refs[11:16])
-    list_ref, slot_ref, feat_ref, in_ref, rows_ref = refs[16:21]
-    targets, sems = refs[21:25], refs[25]
+    sources, red_ref, held = refs[5:7], refs[8], Held(refs[9:12])
+    list_ref, slot_ref, feat_ref, in_ref, rows_ref = refs[12:17]
+    targets, sems = refs[17:19], refs[19]
     pairs = ((list_hbm, list_ref), (slot_hbm, slot_ref)) + in_parts(feat_hbm, feat_ref, IN_COPIES)
     pairs += ((in_hbm, in_ref), *zip(sources, targets))
     for copy in start_copies(pairs, sems):
@@ -281,8 +289,21 @@
     return slots
 
 
-def inner_kernel(lat_len, red_ref, edge_ref, weights_ref, tapped_ref, halo_stack_ref, stack_ref):
+def inner_kernel(
+    lat_len,
+    red_ref,
+    edge_ref,
+    weights_ref,
+    out_factor_ref,
+    bias_ref,
+    tapped_ref,
+    halo_stack_ref,
+    mixer_ref,
+    offset_ref,
+    stack_ref,
+):
     rank = red_ref.shape[0]
+    build_mixer(out_factor_ref, bias_ref, mixer_ref, offset_ref)
     lon_len = red_ref.shape[1] // lat_len
     slots = {p: p - REACH for p in range(REACH, lat_len - REACH)}
     edges = edge_ref[...].astype(F32)
@@ -403,8 +424,6 @@
         core_shape,
         jax.ShapeDtypeStruct(labels.shape, jnp.int32),
         jax.ShapeDtypeStruct((tap_rank * rank // 2, taps * rank // 2), BF16),
-        jax.ShapeDtypeStruct((out_channels * GROUP, rank * GROUP), BF16),
-        jax.ShapeDtypeStruct((out_channels * GROUP, lon_len), F32),
     )
     lists = [
         pltpu.SMEM(tile_regions.shape, jnp.int32),
@@ -415,8 +434,6 @@
     targets = [
         pltpu.VMEM(labels.shape, jnp.int32),
         pltpu.VMEM(tap_factor.shape, BF16),
-        pltpu.VMEM(out_factor.shape[::-1], BF16),
-        pltpu.VMEM((1, out_channels), F32),
     ]
     sources = tuple(
         in_hbm(x)
@@ -428,8 +445,6 @@
             kernel_bank,
             labels,
             tap_factor,
-            out_factor.T,
-            out_bias.reshape(1, -1),
         )
     )
     pay_a, pay_b = pl.pallas_call(
@@ -449,16 +464,16 @@
     )(sources[0], in_hbm(bank_slot.reshape(-1, LANES)), *sources[2:4])
     got_b = lax.ppermute(pay_b, "lon", lon_second)
     got_a = lax.ppermute(pay_a, "lon", lon_first)
-    reduced, own, position, weights, mixer, offset = pl.pallas_call(
+    reduced, own, position, weights = pl.pallas_call(
         functools.partial(prepare_kernel, lon_count, lat_len),
         out_shape=(jax.ShapeDtypeStruct((rank, cells), BF16), *held_shapes),
-        in_specs=[HBM] * 9 + [HBM],
-        out_specs=(VMEM,) * 6,
+        in_specs=[HBM] * 8,
+        out_specs=(VMEM,) * 4,
         scratch_shapes=[
             *lists,
             pltpu.VMEM((channels * lat_len, lon_len), F32),
             *targets,
-            pltpu.SemaphoreType.DMA((IN_COPIES + 7,)),
+            pltpu.SemaphoreType.DMA((IN_COPIES + 5,)),
         ],
         compiler_params=PARAMS,
         cost_estimate=pl.CostEstimate(flops=10**5, bytes_accessed=10**5, transcendentals=0),
@@ -485,14 +500,19 @@
     border_cells = 2 * REACH * lon_len
     stack_rows = taps * rank // 2
     halo_stack_shape = jax.ShapeDtypeStruct((2, stack_rows, border_cells), BF16)
-    inner, halo_stack = pl.pallas_call(
+    inner, halo_stack, mixer, offset = pl.pallas_call(
         functools.partial(inner_kernel, lat_len),
-        out_shape=(jax.ShapeDtypeStruct((tap_rank * rank, cells - border_cells), BF16), halo_stack_shape),
-        in_specs=[VMEM] * 3,
-        out_specs=(VMEM,) * 2,
+        out_shape=(
+            jax.ShapeDtypeStruct((tap_rank * rank, cells - border_cells), BF16),
+            halo_stack_shape,
+            jax.ShapeDtypeStruct((out_channels * GROUP, rank * GROUP), BF16),
+            jax.ShapeDtypeStruct((out_channels * GROUP, lon_len), F32),
+        ),
+        in_specs=[VMEM] * 5,
+        out_specs=(VMEM,) * 4,
         scratch_shapes=[pltpu.VMEM((2, stack_rows, cells - border_cells), BF16)],
         compiler_params=PARAMS,
-    )(reduced, edges, weights)
+    )(reduced, edges, weights, out_factor.T, out_bias.reshape(1, -1))
     border = pl.pallas_call(
         functools.partial(border_kernel, lat_len, lat_count),
         out_shape=jax.ShapeDtypeStruct((tap_rank * rank, border_cells), BF16),

time: 20.9 us -> 20.7 us (level)
  no operation moved by 1% of the time
where the time goes in v14:
time: 20.7 us; the launch traced here: 20.5 us
  starting transfers between devices  10.5 us (51%)
  Pallas kernels  7.68 us (37%)
  waiting for transfers between devices  2.18 us (11%)
    ppermute x1, starting transfers between devices, on_device(): got_b = lax.ppermute(pay_b, 'lon', lon_second)  6.04 us
    ppermute x1, starting transfers between devices, on_device(): core_b = lax.ppermute(core_b, 'lon', lon_second)  2.2 us
    pallas_call x1, Pallas kernels, on_device(): pl.pallas_call(functools.partial(prepare_kernel, lon_count, lat_len), out...  2.19 us
    ppermute x1, starting transfers between devices, on_device(): row_a = lax.ppermute(row_a, 'lat', lat_first)  1.63 us
    pallas_call x1, Pallas kernels, on_device(): pl.pallas_call(functools.partial(inner_kernel, lat_len), out_shape=(jax.S...  1.6 us
    pallas_call x1, Pallas kernels, on_device(): pl.pallas_call(mix_kernel, out_shape=jax.ShapeDtypeStruct(out_shape, BF16...  1.54 us
    pallas_call x1, Pallas kernels, on_device(): pl.pallas_call(functools.partial(edge_kernel, lon_count, held), out_shape...  1.45 us
    ppermute x1, waiting for transfers between devices, on_device(): got_a = lax.ppermute(pay_a, 'lon', lon_first)  1.44 us
  transfers between devices with their start and end apart: 6, of which 3 were waited for; matrix products, arithmetic and copies ran while one was open for 0% of the time, Pallas kernels for 22%

profile of v14, /device:TPU:0, one launch (start us, length us, event | category | flops | bytes accessed | tf_op | source)
XLA Modules:
  0.0 20.5 jit_solution(2506248942273209159)
XLA Ops:
  0.0 1.5 %shard_map.91 = (bf16[32,128]{1,0:T(8,128)(2,1)S(1)}, bf16[32,128]{1,0:T(8,128)(2,1)S(1)}) custom-call(s32[1,1,6]{2,1,0:T(1,128)} %refs_0_.3, s32[7,128]{1,0:T(8,128)} %bitcast.5, bf16[64,16,128]{2,1,0:T(8,128)(2,1)} %refs_2_.3, bf16[32,64]{1,0:T(8,128)(2,1)} %refs_3_.3), custom_call_target="tpu_custom_call" | custom-call | flops 2000000000 | bytes 4000000 | tf_op jit(solution)/shard_map/pallas_call | solution.py:450
  1.5 0.0 copy-start
  1.5 6.0 %collective-permute-start = (bf16[32,128]{1,0:T(8,128)(2,1)S(1)}, bf16[32,128]{1,0:T(8,128)(2,1)S(1)}, u32[]{:S(2)}, u32[]{:S(2)}) collective-permute-start(bf16[32,128]{1,0:T(8,128)(2,1)S(1)} %get-tuple-element.22), channel_id=1, source_target_pairs={{0,7},{1,2},{2,1},{3,4},{4,3},{5,6},{6,5},{7,0},{8,15},{9,10},{10,... | collective-permute-start | bytes 24584 | tf_op jit(solution)/shard_map/ppermute | solution.py:465
  7.5 0.0 copy-start.1
  7.5 0.0 copy-start.2
  7.5 0.0 collective-permute-start.1
  7.5 2.2 %shard_map.92 = (bf16[32,2048]{1,0:T(8,128)(2,1)S(1)}, bf16[2,32,512]{2,1,0:T(8,128)(2,1)S(1)}, s32[16,128]{1,0:T(8,128)S(1)}, bf16[256,400]{1,0:T(8,128)(2,1)S(1)}) custom-call(s32[1,1,6]{2,1,0:T(1,128)} %refs_0_.3, s32[896]{0:T(1024)} %refs_1_.1, bf16[64,16,128]{2,1,0:T(8,128)(2,1)} %refs_2_.3, bf16[32,64]{1,0:T(8,128)(2,1)} %refs_3_.3, ...), custom_call_target="tpu_custom_call" | custom-call | flops 100000 | bytes 100000 | tf_op jit(solution)/shard_map/pallas_call | solution.py:467
  9.7 0.0 collective-permute-done.got_b_ref
  9.7 1.4 %collective-permute-done.1.got_a_ref = bf16[32,128]{1,0:T(8,128)(2,1)S(1)} collective-permute-done((bf16[32,128]{1,0:T(8,128)(2,1)S(1)}, bf16[32,128]{1,0:T(8,128)(2,1)S(1)}, u32[]{:S(2)}, u32[]{:S(2)}) %collective-permute-start.1) | collective-permute-done | bytes 8224 | tf_op jit(solution)/shard_map/ppermute | solution.py:466
  11.2 0.0 copy-done
  11.2 0.1 shard_map.93
  11.3 0.6 %collective-permute-start.4 = (bf16[2,32,512]{2,1,0:T(8,128)(2,1)S(1)}, bf16[2,32,512]{2,1,0:T(8,128)(2,1)S(1)}, u32[]{:S(2)}, u32[]{:S(2)}) collective-permute-start(bf16[2,32,512]{2,1,0:T(8,128)(2,1)S(1)} %get-tuple-element.31), channel_id=1, source_target_pairs={{0,1},{1,0},{2,3},{3,2},{4,5},{5,4},{6,7},{7,6},{8,9},{9,8},{10,11... | collective-permute-start | bytes 196616 | tf_op jit(solution)/shard_map/ppermute | solution.py:497
  12.0 2.2 %collective-permute-start.5 = (bf16[2,32,512]{2,1,0:T(8,128)(2,1)S(1)}, bf16[2,32,512]{2,1,0:T(8,128)(2,1)S(1)}, u32[]{:S(2)}, u32[]{:S(2)}) collective-permute-start(bf16[2,32,512]{2,1,0:T(8,128)(2,1)S(1)} %get-tuple-element.24.core_ref), channel_id=1, source_target_pairs={{0,7},{1,2},{2,1},{3,4},{4,3},{5,6},{6,5},{7,0},{8,15},{9,10},{10,... | collective-permute-start | bytes 196616 | tf_op jit(solution)/shard_map/ppermute | solution.py:496
  14.2 0.1 shard_map.94
  14.3 0.0 collective-permute-start.2
  14.3 1.6 %collective-permute-start.3 = (bf16[32,384]{1,0:T(8,128)(2,1)S(1)}, bf16[32,384]{1,0:T(8,128)(2,1)S(1)}, u32[]{:S(2)}, u32[]{:S(2)}) collective-permute-start(bf16[32,384]{1,0:T(8,128)(2,1)S(1)} %get-tuple-element.29), channel_id=1, source_target_pairs={{0,8},{8,0},{16,24},{24,16},{1,9},{9,1},{17,25},{25,17},{2,10},{10... | collective-permute-start | bytes 73736 | tf_op jit(solution)/shard_map/ppermute | solution.py:498
  15.9 0.0 copy-done.1
  15.9 0.0 copy-done.2
  15.9 1.6 %shard_map.95 = (bf16[512,1536]{1,0:T(8,128)(2,1)S(1)}, bf16[2,400,512]{2,1,0:T(8,128)(2,1)S(1)}, bf16[512,256]{1,0:T(8,128)(2,1)S(1)}, f32[512,128]{1,0:T(8,128)S(1)}) custom-call(bf16[32,2048]{1,0:T(8,128)(2,1)S(1)} %get-tuple-element.21.red_ref, bf16[32,128]{1,0:T(8,128)(2,1)S(1)} %get-tuple-element.25.edge_ref, ...), custom_call_target="tpu_custom_call" | custom-call | tf_op jit(solution)/shard_map/pallas_call | solution.py:503
  17.5 0.2 collective-permute-done.2.row_b_ref
  17.7 0.0 collective-permute-done.3.row_a_ref
  17.7 0.6 %shard_map.96.border_ref = bf16[512,512]{1,0:T(8,128)(2,1)S(1)} custom-call(bf16[32,384]{1,0:T(8,128)(2,1)S(1)} %collective-permute-done.2.row_b_ref, bf16[32,384]{1,0:T(8,128)(2,1)S(1)} %collective-permute-done.3.row_a_ref, bf16[256,400]{1,0:T(8,128)(2,1)S(1)} %get-tuple-element.26.weights_ref, bf16[2,400,512]{2,1,0:T(8,128)(2,1)S(1)} %get-tuple-element.30.own_stack_ref), custom_call_target="tpu_custom_call" | custom-call | tf_op jit(solution)/shard_map/pallas_call | solution.py:516
  18.4 0.0 collective-permute-done.4.core_a_ref
  18.4 0.5 %collective-permute-done.5.core_b_ref = bf16[2,32,512]{2,1,0:T(8,128)(2,1)S(1)} collective-permute-done((bf16[2,32,512]{2,1,0:T(8,128)(2,1)S(1)}, bf16[2,32,512]{2,1,0:T(8,128)(2,1)S(1)}, u32[]{:S(2)}, u32[]{:S(2)}) %collective-permute-start.5) | collective-permute-done | bytes 65568 | tf_op jit(solution)/shard_map/ppermute | solution.py:496
  18.9 1.5 %shard_map.97 = bf16[64,16,128]{2,1,0:T(8,128)(2,1)} custom-call(bf16[512,1536]{1,0:T(8,128)(2,1)S(1)} %get-tuple-element.27.inner_ref, bf16[512,512]{1,0:T(8,128)(2,1)S(1)} %shard_map.96.border_ref, bf16[2,32,512]{2,1,0:T(8,128)(2,1)S(1)} %collective-permute-done.4.core_a_ref, bf16[2,32,512]{2,1,0:T(8,128)(2,1)S(1)} %collective-permute-done.5.core_b_ref, ...), custom_call_target="tpu_custom_call" | custom-call | tf_op jit(solution)/shard_map/pallas_call | solution.py:525
Async XLA Ops:
  1.5 9.7 %copy-start = (bf16[112,32,512]{2,1,0:T(8,128)(2,1)S(1)}, bf16[112,32,512]{2,1,0:T(8,128)(2,1)}, u32[]{:S(2)}) copy-start(bf16[112,32,512]{2,1,0:T(8,128)(2,1)} %bank_ref.1) | copy-start | bytes 11010052
  1.5 8.2 %collective-permute-start = (bf16[32,128]{1,0:T(8,128)(2,1)S(1)}, bf16[32,128]{1,0:T(8,128)(2,1)S(1)}, u32[]{:S(2)}, u32[]{:S(2)}) collective-permute-start(bf16[32,128]{1,0:T(8,128)(2,1)S(1)} %get-tuple-element.22), channel_id=1, source_target_pairs={{0,7},{1,2},{2,1},{3,4},{4,3},{5,6},{6,5},{7,0},{8,15},{9,10},{10,... | collective-permute-start | bytes 24584 | tf_op jit(solution)/shard_map/ppermute | solution.py:465
  7.5 8.4 %copy-start.1 = (bf16[64,32]{0,1:T(8,128)(2,1)S(1)}, bf16[64,32]{0,1:T(8,128)(2,1)}, u32[]{:S(2)}) copy-start(bf16[64,32]{0,1:T(8,128)(2,1)} %param.16) | copy-start | bytes 12292
  7.5 8.4 %copy-start.2 = (f32[64]{0:T(128)S(1)}, f32[64]{0:T(128)}, u32[]{:S(2)}) copy-start(f32[64]{0:T(128)} %param.17) | copy-start | bytes 772
  7.5 3.7 %collective-permute-start.1 = (bf16[32,128]{1,0:T(8,128)(2,1)S(1)}, bf16[32,128]{1,0:T(8,128)(2,1)S(1)}, u32[]{:S(2)}, u32[]{:S(2)}) collective-permute-start(bf16[32,128]{1,0:T(8,128)(2,1)S(1)} %get-tuple-element.20.refs_7_), channel_id=1, source_target_pairs={{0,1},{1,0},{2,3},{3,2},{4,5},{5,4},{6,7},{7,6},{8,9},{9,8},{10,11... | collective-permute-start | bytes 24584 | tf_op jit(solution)/shard_map/ppermute | solution.py:466
  11.3 7.1 %collective-permute-start.4 = (bf16[2,32,512]{2,1,0:T(8,128)(2,1)S(1)}, bf16[2,32,512]{2,1,0:T(8,128)(2,1)S(1)}, u32[]{:S(2)}, u32[]{:S(2)}) collective-permute-start(bf16[2,32,512]{2,1,0:T(8,128)(2,1)S(1)} %get-tuple-element.31), channel_id=1, source_target_pairs={{0,1},{1,0},{2,3},{3,2},{4,5},{5,4},{6,7},{7,6},{8,9},{9,8},{10,11... | collective-permute-start | bytes 196616 | tf_op jit(solution)/shard_map/ppermute | solution.py:497
  12.0 7.0 %collective-permute-start.5 = (bf16[2,32,512]{2,1,0:T(8,128)(2,1)S(1)}, bf16[2,32,512]{2,1,0:T(8,128)(2,1)S(1)}, u32[]{:S(2)}, u32[]{:S(2)}) collective-permute-start(bf16[2,32,512]{2,1,0:T(8,128)(2,1)S(1)} %get-tuple-element.24.core_ref), channel_id=1, source_target_pairs={{0,7},{1,2},{2,1},{3,4},{4,3},{5,6},{6,5},{7,0},{8,15},{9,10},{10,... | collective-permute-start | bytes 196616 | tf_op jit(solution)/shard_map/ppermute | solution.py:496
  14.3 3.4 %collective-permute-start.2 = (bf16[32,384]{1,0:T(8,128)(2,1)S(1)}, bf16[32,384]{1,0:T(8,128)(2,1)S(1)}, u32[]{:S(2)}, u32[]{:S(2)}) collective-permute-start(bf16[32,384]{1,0:T(8,128)(2,1)S(1)} %get-tuple-element.28), channel_id=1, source_target_pairs={{0,24},{8,16},{16,8},{24,0},{1,25},{9,17},{17,9},{25,1},{2,26},{10... | collective-permute-start | bytes 73736 | tf_op jit(solution)/shard_map/ppermute | solution.py:499
  14.3 3.4 %collective-permute-start.3 = (bf16[32,384]{1,0:T(8,128)(2,1)S(1)}, bf16[32,384]{1,0:T(8,128)(2,1)S(1)}, u32[]{:S(2)}, u32[]{:S(2)}) collective-permute-start(bf16[32,384]{1,0:T(8,128)(2,1)S(1)} %get-tuple-element.29), channel_id=1, source_target_pairs={{0,8},{8,0},{16,24},{24,16},{1,9},{9,1},{17,25},{25,17},{2,10},{10... | collective-permute-start | bytes 73736 | tf_op jit(solution)/shard_map/ppermute | solution.py:498

commit v15 on v14

--- a/solution.py
+++ b/solution.py
@@ -71,7 +71,7 @@
 
 
 class Held:
-    names = ("own", "position", "weights")
+    names = ("own_rows", "position", "weights")
     sources = ("labels", "tap")
 
     def __init__(self, refs):
@@ -204,14 +204,16 @@
     for copy in start_copies(pairs, sems):
         copy.wait()
     places, rows = find_rows(list_ref, slot_ref, lon_count, bank_hbm.shape[0])
-    own = start_copies(tuple((bank_hbm.at[row], held.own.at[nth]) for nth, row in enumerate(rows[0])), sems)
+    lane = lane_index((1, LANES))
+    own_rows = jnp.zeros((1, LANES), jnp.int32)
+    for nth, row in enumerate(rows[0]):
+        own_rows = jnp.where(lane == nth, row, own_rows)
+    held.own_rows[...] = own_rows
     reduce_tile(lat_len, feat_ref, in_ref, rows_ref, red_ref)
     build_held(places, targets, held)
-    for copy in own:
-        copy.wait()
-
-
-def pick_kernel(lat_len, got_b_ref, got_a_ref, own_hbm, bank_ref, core_a_ref, core_b_ref):
+
+
+def pick_kernel(lat_len, got_b_ref, got_a_ref, own_rows_hbm, bank_ref, core_a_ref, core_b_ref):
     lane = lane_index((1, LANES))
     for got_ref, core_ref in ((got_b_ref, core_b_ref), (got_a_ref, core_a_ref)):
         head = got_ref[...].astype(F32)[0:1, :]
@@ -296,13 +298,20 @@
     weights_ref,
     out_factor_ref,
     bias_ref,
+    own_rows_ref,
+    bank_ref,
     tapped_ref,
     halo_stack_ref,
     mixer_ref,
     offset_ref,
+    own_ref,
     stack_ref,
 ):
     rank = red_ref.shape[0]
+    head = own_rows_ref[...].astype(F32)
+    for nth in range(PER_OWNER):
+        row = jnp.sum(jnp.where(lane_index((1, LANES)) == nth, head, 0.0)).astype(jnp.int32)
+        own_ref[nth] = bank_ref[row]
     build_mixer(out_factor_ref, bias_ref, mixer_ref, offset_ref)
     lon_len = red_ref.shape[1] // lat_len
     slots = {p: p - REACH for p in range(REACH, lat_len - REACH)}
@@ -421,7 +430,7 @@
     edge_shape = jax.ShapeDtypeStruct((rank, LANES), BF16)
     core_shape = jax.ShapeDtypeStruct((PER_OWNER, core_rows, core_cols), BF16)
     held_shapes = (
-        core_shape,
+        jax.ShapeDtypeStruct((1, LANES), jnp.int32),
         jax.ShapeDtypeStruct(labels.shape, jnp.int32),
         jax.ShapeDtypeStruct((tap_rank * rank // 2, taps * rank // 2), BF16),
     )
@@ -464,7 +473,7 @@
     )(sources[0], in_hbm(bank_slot.reshape(-1, LANES)), *sources[2:4])
     got_b = lax.ppermute(pay_b, "lon", lon_second)
     got_a = lax.ppermute(pay_a, "lon", lon_first)
-    reduced, own, position, weights = pl.pallas_call(
+    reduced, own_rows, position, weights = pl.pallas_call(
         functools.partial(prepare_kernel, lon_count, lat_len),
         out_shape=(jax.ShapeDtypeStruct((rank, cells), BF16), *held_shapes),
         in_specs=[HBM] * 8,
@@ -485,7 +494,7 @@
         in_specs=[VMEM, VMEM, HBM, VMEM],
         out_specs=(VMEM,) * 2,
         compiler_params=PARAMS,
-    )(got_b, got_a, own, kernel_bank)
+    )(got_b, got_a, own_rows, kernel_bank)
     edges, row_a, row_b = pl.pallas_call(
         functools.partial(rows_kernel, lat_len),
         out_shape=(edge_shape, row_shape, row_shape),
@@ -500,19 +509,20 @@
     border_cells = 2 * REACH * lon_len
     stack_rows = taps * rank // 2
     halo_stack_shape = jax.ShapeDtypeStruct((2, stack_rows, border_cells), BF16)
-    inner, halo_stack, mixer, offset = pl.pallas_call(
+    inner, halo_stack, mixer, offset, own = pl.pallas_call(
         functools.partial(inner_kernel, lat_len),
         out_shape=(
             jax.ShapeDtypeStruct((tap_rank * rank, cells - border_cells), BF16),
             halo_stack_shape,
             jax.ShapeDtypeStruct((out_channels * GROUP, rank * GROUP), BF16),
             jax.ShapeDtypeStruct((out_channels * GROUP, lon_len), F32),
+            core_shape,
         ),
-        in_specs=[VMEM] * 5,
-        out_specs=(VMEM,) * 4,
+        in_specs=[VMEM] * 7,
+        out_specs=(VMEM,) * 5,
         scratch_shapes=[pltpu.VMEM((2, stack_rows, cells - border_cells), BF16)],
         compiler_params=PARAMS,
-    )(reduced, edges, weights, out_factor.T, out_bias.reshape(1, -1))
+    )(reduced, edges, weights, out_factor.T, out_bias.reshape(1, -1), own_rows, kernel_bank)
     border = pl.pallas_call(
         functools.partial(border_kernel, lat_len, lat_count),
         out_shape=jax.ShapeDtypeStruct((tap_rank * rank, border_cells), BF16),

time: 20.7 us -> 20.2 us (0.976)
  Pallas kernels: 7.68 us -> 7 us
    pallas_call x1, Pallas kernels: 2.19 us -> 1.51 us  [on_device(): pl.pallas_call(functools.partial(prepare_kernel, lon_count, lat_len), out...]
    ppermute x1, waiting for transfers between devices: 1.44 us -> 2.02 us  [on_device(): got_a = lax.ppermute(pay_a, 'lon', lon_first)]
    ppermute x1, starting transfers between devices: 0.64 us -> 0.07 us  [on_device(): core_a = lax.ppermute(core_a, 'lon', lon_first)]
    ppermute x1, starting transfers between devices: 2.2 us -> 2.76 us  [on_device(): core_b = lax.ppermute(core_b, 'lon', lon_second)]
    ppermute x1, waiting for transfers between devices: 0.54 us -> 0.04 us  [on_device(): core_b = lax.ppermute(core_b, 'lon', lon_second)]
  transfers between devices with their start and end apart: 6 -> 6, of which waited for: 3 -> 3; matrix products, arithmetic and copies ran while one was open for 0% -> 0% of each run, Pallas kernels for 22% -> 19%
where the time goes in v15:
time: 20.2 us; the launch traced here: 20 us
  starting transfers between devices  10.5 us (52%)
  Pallas kernels  7 us (35%)
  waiting for transfers between devices  2.36 us (12%)
    ppermute x1, starting transfers between devices, on_device(): got_b = lax.ppermute(pay_b, 'lon', lon_second)  6.04 us
    ppermute x1, starting transfers between devices, on_device(): core_b = lax.ppermute(core_b, 'lon', lon_second)  2.76 us
    ppermute x1, waiting for transfers between devices, on_device(): got_a = lax.ppermute(pay_a, 'lon', lon_first)  2.02 us
    ppermute x1, starting transfers between devices, on_device(): row_a = lax.ppermute(row_a, 'lat', lat_first)  1.63 us
    pallas_call x1, Pallas kernels, on_device(): pl.pallas_call(functools.partial(inner_kernel, lat_len), out_shape=(jax.S...  1.6 us
    pallas_call x1, Pallas kernels, on_device(): pl.pallas_call(mix_kernel, out_shape=jax.ShapeDtypeStruct(out_shape, BF16...  1.53 us
    pallas_call x1, Pallas kernels, on_device(): pl.pallas_call(functools.partial(prepare_kernel, lon_count, lat_len), out...  1.51 us
    pallas_call x1, Pallas kernels, on_device(): pl.pallas_call(functools.partial(edge_kernel, lon_count, held), out_shape...  1.46 us
  transfers between devices with their start and end apart: 6, of which 3 were waited for; matrix products, arithmetic and copies ran while one was open for 0% of the time, Pallas kernels for 19%

profile of v15, /device:TPU:0, one launch (start us, length us, event | category | flops | bytes accessed | tf_op | source)
XLA Modules:
  0.0 20.0 jit_solution(14109641877133274318)
XLA Ops:
  0.0 1.5 %shard_map.91 = (bf16[32,128]{1,0:T(8,128)(2,1)S(1)}, bf16[32,128]{1,0:T(8,128)(2,1)S(1)}) custom-call(s32[1,1,6]{2,1,0:T(1,128)} %refs_0_.3, s32[7,128]{1,0:T(8,128)} %bitcast.5, bf16[64,16,128]{2,1,0:T(8,128)(2,1)} %refs_2_.3, bf16[32,64]{1,0:T(8,128)(2,1)} %refs_3_.3), custom_call_target="tpu_custom_call" | custom-call | flops 2000000000 | bytes 4000000 | tf_op jit(solution)/shard_map/pallas_call | solution.py:459
  1.5 0.0 copy-start
  1.5 6.0 %collective-permute-start = (bf16[32,128]{1,0:T(8,128)(2,1)S(1)}, bf16[32,128]{1,0:T(8,128)(2,1)S(1)}, u32[]{:S(2)}, u32[]{:S(2)}) collective-permute-start(bf16[32,128]{1,0:T(8,128)(2,1)S(1)} %get-tuple-element.23), channel_id=1, source_target_pairs={{0,7},{1,2},{2,1},{3,4},{4,3},{5,6},{6,5},{7,0},{8,15},{9,10},{10,... | collective-permute-start | bytes 24584 | tf_op jit(solution)/shard_map/ppermute | solution.py:474
  7.5 0.0 copy-start.1
  7.5 0.0 copy-start.2
  7.5 0.0 collective-permute-start.1
  7.5 1.5 %shard_map.92 = (bf16[32,2048]{1,0:T(8,128)(2,1)S(1)}, s32[1,128]{1,0:T(1,128)S(1)}, s32[16,128]{1,0:T(8,128)S(1)}, bf16[256,400]{1,0:T(8,128)(2,1)S(1)}) custom-call(s32[1,1,6]{2,1,0:T(1,128)} %refs_0_.3, s32[896]{0:T(1024)} %refs_1_.1, bf16[64,16,128]{2,1,0:T(8,128)(2,1)} %refs_2_.3, bf16[32,64]{1,0:T(8,128)(2,1)} %refs_3_.3, ...), custom_call_target="tpu_custom_call" | custom-call | flops 100000 | bytes 100000 | tf_op jit(solution)/shard_map/pallas_call | solution.py:476
  9.0 0.1 collective-permute-done.got_b_ref
  9.1 2.0 %collective-permute-done.1.got_a_ref = bf16[32,128]{1,0:T(8,128)(2,1)S(1)} collective-permute-done((bf16[32,128]{1,0:T(8,128)(2,1)S(1)}, bf16[32,128]{1,0:T(8,128)(2,1)S(1)}, u32[]{:S(2)}, u32[]{:S(2)}) %collective-permute-start.1) | collective-permute-done | bytes 8224 | tf_op jit(solution)/shard_map/ppermute | solution.py:475
  11.2 0.0 copy-done
  11.2 0.1 shard_map.93
  11.3 0.1 collective-permute-start.4
  11.4 2.8 %collective-permute-start.5 = (bf16[2,32,512]{2,1,0:T(8,128)(2,1)S(1)}, bf16[2,32,512]{2,1,0:T(8,128)(2,1)S(1)}, u32[]{:S(2)}, u32[]{:S(2)}) collective-permute-start(bf16[2,32,512]{2,1,0:T(8,128)(2,1)S(1)} %get-tuple-element.25.core_ref), channel_id=1, source_target_pairs={{0,7},{1,2},{2,1},{3,4},{4,3},{5,6},{6,5},{7,0},{8,15},{9,10},{10,... | collective-permute-start | bytes 196616 | tf_op jit(solution)/shard_map/ppermute | solution.py:505
  14.2 0.1 shard_map.94
  14.3 0.0 collective-permute-start.2
  14.3 1.6 %collective-permute-start.3 = (bf16[32,384]{1,0:T(8,128)(2,1)S(1)}, bf16[32,384]{1,0:T(8,128)(2,1)S(1)}, u32[]{:S(2)}, u32[]{:S(2)}) collective-permute-start(bf16[32,384]{1,0:T(8,128)(2,1)S(1)} %get-tuple-element.30), channel_id=1, source_target_pairs={{0,8},{8,0},{16,24},{24,16},{1,9},{9,1},{17,25},{25,17},{2,10},{10... | collective-permute-start | bytes 73736 | tf_op jit(solution)/shard_map/ppermute | solution.py:507
  15.9 0.0 copy-done.1
  15.9 0.0 copy-done.2
  15.9 1.6 %shard_map.95 = (bf16[512,1536]{1,0:T(8,128)(2,1)S(1)}, bf16[2,400,512]{2,1,0:T(8,128)(2,1)S(1)}, bf16[512,256]{1,0:T(8,128)(2,1)S(1)}, f32[512,128]{1,0:T(8,128)S(1)}, bf16[2,32,512]{2,1,0:T(8,128)(2,1)S(1)}) custom-call(bf16[32,2048]{1,0:T(8,128)(2,1)S(1)} %get-tuple-element.22.red_ref, bf16[32,128]{1,0:T(8,128)(2,1)S(1)} %get-tuple-element.26.edge_ref, ...), custom_call_target="tpu_custom_call" | custom-call | tf_op jit(solution)/shard_map/pallas_call | solution.py:512
  17.5 0.2 collective-permute-done.2.row_b_ref
  17.7 0.0 collective-permute-done.3.row_a_ref
  17.7 0.6 %shard_map.96.border_ref = bf16[512,512]{1,0:T(8,128)(2,1)S(1)} custom-call(bf16[32,384]{1,0:T(8,128)(2,1)S(1)} %collective-permute-done.2.row_b_ref, bf16[32,384]{1,0:T(8,128)(2,1)S(1)} %collective-permute-done.3.row_a_ref, bf16[256,400]{1,0:T(8,128)(2,1)S(1)} %get-tuple-element.27.weights_ref, bf16[2,400,512]{2,1,0:T(8,128)(2,1)S(1)} %get-tuple-element.31.own_stack_ref), custom_call_target="tpu_custom_call" | custom-call | tf_op jit(solution)/shard_map/pallas_call | solution.py:526
  18.4 0.0 collective-permute-done.4.core_a_ref
  18.4 0.0 collective-permute-done.5.core_b_ref
  18.4 1.5 %shard_map.97 = bf16[64,16,128]{2,1,0:T(8,128)(2,1)} custom-call(bf16[512,1536]{1,0:T(8,128)(2,1)S(1)} %get-tuple-element.28.inner_ref, bf16[512,512]{1,0:T(8,128)(2,1)S(1)} %shard_map.96.border_ref, bf16[2,32,512]{2,1,0:T(8,128)(2,1)S(1)} %collective-permute-done.4.core_a_ref, bf16[2,32,512]{2,1,0:T(8,128)(2,1)S(1)} %collective-permute-done.5.core_b_ref, ...), custom_call_target="tpu_custom_call" | custom-call | tf_op jit(solution)/shard_map/pallas_call | solution.py:535
Async XLA Ops:
  1.5 9.7 %copy-start = (bf16[112,32,512]{2,1,0:T(8,128)(2,1)S(1)}, bf16[112,32,512]{2,1,0:T(8,128)(2,1)}, u32[]{:S(2)}) copy-start(bf16[112,32,512]{2,1,0:T(8,128)(2,1)} %bank_ref.3) | copy-start | bytes 11010052
  1.5 7.7 %collective-permute-start = (bf16[32,128]{1,0:T(8,128)(2,1)S(1)}, bf16[32,128]{1,0:T(8,128)(2,1)S(1)}, u32[]{:S(2)}, u32[]{:S(2)}) collective-permute-start(bf16[32,128]{1,0:T(8,128)(2,1)S(1)} %get-tuple-element.23), channel_id=1, source_target_pairs={{0,7},{1,2},{2,1},{3,4},{4,3},{5,6},{6,5},{7,0},{8,15},{9,10},{10,... | collective-permute-start | bytes 24584 | tf_op jit(solution)/shard_map/ppermute | solution.py:474
  7.5 8.4 %copy-start.1 = (bf16[64,32]{0,1:T(8,128)(2,1)S(1)}, bf16[64,32]{0,1:T(8,128)(2,1)}, u32[]{:S(2)}) copy-start(bf16[64,32]{0,1:T(8,128)(2,1)} %param.16) | copy-start | bytes 12292
  7.5 8.4 %copy-start.2 = (f32[64]{0:T(128)S(1)}, f32[64]{0:T(128)}, u32[]{:S(2)}) copy-start(f32[64]{0:T(128)} %param.17) | copy-start | bytes 772
  7.5 3.7 %collective-permute-start.1 = (bf16[32,128]{1,0:T(8,128)(2,1)S(1)}, bf16[32,128]{1,0:T(8,128)(2,1)S(1)}, u32[]{:S(2)}, u32[]{:S(2)}) collective-permute-start(bf16[32,128]{1,0:T(8,128)(2,1)S(1)} %get-tuple-element.21.refs_7_), channel_id=1, source_target_pairs={{0,1},{1,0},{2,3},{3,2},{4,5},{5,4},{6,7},{7,6},{8,9},{9,8},{10,11... | collective-permute-start | bytes 24584 | tf_op jit(solution)/shard_map/ppermute | solution.py:475
  11.3 7.1 %collective-permute-start.4 = (bf16[2,32,512]{2,1,0:T(8,128)(2,1)S(1)}, bf16[2,32,512]{2,1,0:T(8,128)(2,1)S(1)}, u32[]{:S(2)}, u32[]{:S(2)}) collective-permute-start(bf16[2,32,512]{2,1,0:T(8,128)(2,1)S(1)} %get-tuple-element.32), channel_id=1, source_target_pairs={{0,1},{1,0},{2,3},{3,2},{4,5},{5,4},{6,7},{7,6},{8,9},{9,8},{10,11... | collective-permute-start | bytes 196616 | tf_op jit(solution)/shard_map/ppermute | solution.py:506
  11.4 7.0 %collective-permute-start.5 = (bf16[2,32,512]{2,1,0:T(8,128)(2,1)S(1)}, bf16[2,32,512]{2,1,0:T(8,128)(2,1)S(1)}, u32[]{:S(2)}, u32[]{:S(2)}) collective-permute-start(bf16[2,32,512]{2,1,0:T(8,128)(2,1)S(1)} %get-tuple-element.25.core_ref), channel_id=1, source_target_pairs={{0,7},{1,2},{2,1},{3,4},{4,3},{5,6},{6,5},{7,0},{8,15},{9,10},{10,... | collective-permute-start | bytes 196616 | tf_op jit(solution)/shard_map/ppermute | solution.py:505
  14.3 3.4 %collective-permute-start.2 = (bf16[32,384]{1,0:T(8,128)(2,1)S(1)}, bf16[32,384]{1,0:T(8,128)(2,1)S(1)}, u32[]{:S(2)}, u32[]{:S(2)}) collective-permute-start(bf16[32,384]{1,0:T(8,128)(2,1)S(1)} %get-tuple-element.29), channel_id=1, source_target_pairs={{0,24},{8,16},{16,8},{24,0},{1,25},{9,17},{17,9},{25,1},{2,26},{10... | collective-permute-start | bytes 73736 | tf_op jit(solution)/shard_map/ppermute | solution.py:508
  14.3 3.4 %collective-permute-start.3 = (bf16[32,384]{1,0:T(8,128)(2,1)S(1)}, bf16[32,384]{1,0:T(8,128)(2,1)S(1)}, u32[]{:S(2)}, u32[]{:S(2)}) collective-permute-start(bf16[32,384]{1,0:T(8,128)(2,1)S(1)} %get-tuple-element.30), channel_id=1, source_target_pairs={{0,8},{8,0},{16,24},{24,16},{1,9},{9,1},{17,25},{25,17},{2,10},{10... | collective-permute-start | bytes 73736 | tf_op jit(solution)/shard_map/ppermute | solution.py:507

commit v16 on v15

--- a/solution.py
+++ b/solution.py
@@ -15,7 +15,7 @@
 GROUP = 8
 STEP = 4
 OUT_COPIES = 4
-IN_COPIES = 4
+IN_COPIES = 1
 F32 = jnp.float32
 BF16 = jnp.bfloat16
 VMEM = pl.BlockSpec(memory_space=pltpu.VMEM)

time: 20.2 us -> 20.1 us (level)
  no operation moved by 1% of the time
where the time goes in v16:
time: 20.1 us; the launch traced here: 19.9 us
  starting transfers between devices  10.5 us (52%)
  Pallas kernels  6.98 us (35%)
  waiting for transfers between devices  2.38 us (12%)
    ppermute x1, starting transfers between devices, on_device(): got_b = lax.ppermute(pay_b, 'lon', lon_second)  6.04 us
    ppermute x1, starting transfers between devices, on_device(): core_b = lax.ppermute(core_b, 'lon', lon_second)  2.76 us
    ppermute x1, waiting for transfers between devices, on_device(): got_a = lax.ppermute(pay_a, 'lon', lon_first)  2.02 us
    ppermute x1, starting transfers between devices, on_device(): row_a = lax.ppermute(row_a, 'lat', lat_first)  1.63 us
    pallas_call x1, Pallas kernels, on_device(): pl.pallas_call(functools.partial(inner_kernel, lat_len), out_shape=(jax.S...  1.6 us
    pallas_call x1, Pallas kernels, on_device(): pl.pallas_call(mix_kernel, out_shape=jax.ShapeDtypeStruct(out_shape, BF16...  1.53 us
    pallas_call x1, Pallas kernels, on_device(): pl.pallas_call(functools.partial(prepare_kernel, lon_count, lat_len), out...  1.5 us
    pallas_call x1, Pallas kernels, on_device(): pl.pallas_call(functools.partial(edge_kernel, lon_count, held), out_shape...  1.44 us
  transfers between devices with their start and end apart: 6, of which 3 were waited for; matrix products, arithmetic and copies ran while one was open for 0% of the time, Pallas kernels for 19%

profile of v16, /device:TPU:0, one launch (start us, length us, event | category | flops | bytes accessed | tf_op | source)
XLA Modules:
  0.0 19.9 jit_solution(16652685833133962345)
XLA Ops:
  0.0 1.4 %shard_map.91 = (bf16[32,128]{1,0:T(8,128)(2,1)S(1)}, bf16[32,128]{1,0:T(8,128)(2,1)S(1)}) custom-call(s32[1,1,6]{2,1,0:T(1,128)} %refs_0_.3, s32[7,128]{1,0:T(8,128)} %bitcast.5, bf16[64,16,128]{2,1,0:T(8,128)(2,1)} %refs_2_.3, bf16[32,64]{1,0:T(8,128)(2,1)} %refs_3_.3), custom_call_target="tpu_custom_call" | custom-call | flops 2000000000 | bytes 4000000 | tf_op jit(solution)/shard_map/pallas_call | solution.py:459
  1.5 0.0 copy-start
  1.5 6.0 %collective-permute-start = (bf16[32,128]{1,0:T(8,128)(2,1)S(1)}, bf16[32,128]{1,0:T(8,128)(2,1)S(1)}, u32[]{:S(2)}, u32[]{:S(2)}) collective-permute-start(bf16[32,128]{1,0:T(8,128)(2,1)S(1)} %get-tuple-element.23), channel_id=1, source_target_pairs={{0,7},{1,2},{2,1},{3,4},{4,3},{5,6},{6,5},{7,0},{8,15},{9,10},{10,... | collective-permute-start | bytes 24584 | tf_op jit(solution)/shard_map/ppermute | solution.py:474
  7.5 0.0 copy-start.1
  7.5 0.0 copy-start.2
  7.5 0.0 collective-permute-start.1
  7.5 1.5 %shard_map.92 = (bf16[32,2048]{1,0:T(8,128)(2,1)S(1)}, s32[1,128]{1,0:T(1,128)S(1)}, s32[16,128]{1,0:T(8,128)S(1)}, bf16[256,400]{1,0:T(8,128)(2,1)S(1)}) custom-call(s32[1,1,6]{2,1,0:T(1,128)} %refs_0_.3, s32[896]{0:T(1024)} %refs_1_.1, bf16[64,16,128]{2,1,0:T(8,128)(2,1)} %refs_2_.3, bf16[32,64]{1,0:T(8,128)(2,1)} %refs_3_.3, ...), custom_call_target="tpu_custom_call" | custom-call | flops 100000 | bytes 100000 | tf_op jit(solution)/shard_map/pallas_call | solution.py:476
  9.0 0.1 collective-permute-done.got_b_ref
  9.1 2.0 %collective-permute-done.1.got_a_ref = bf16[32,128]{1,0:T(8,128)(2,1)S(1)} collective-permute-done((bf16[32,128]{1,0:T(8,128)(2,1)S(1)}, bf16[32,128]{1,0:T(8,128)(2,1)S(1)}, u32[]{:S(2)}, u32[]{:S(2)}) %collective-permute-start.1) | collective-permute-done | bytes 8224 | tf_op jit(solution)/shard_map/ppermute | solution.py:475
  11.2 0.0 copy-done
  11.2 0.1 shard_map.93
  11.3 0.1 collective-permute-start.4
  11.4 2.8 %collective-permute-start.5 = (bf16[2,32,512]{2,1,0:T(8,128)(2,1)S(1)}, bf16[2,32,512]{2,1,0:T(8,128)(2,1)S(1)}, u32[]{:S(2)}, u32[]{:S(2)}) collective-permute-start(bf16[2,32,512]{2,1,0:T(8,128)(2,1)S(1)} %get-tuple-element.25.core_ref), channel_id=1, source_target_pairs={{0,7},{1,2},{2,1},{3,4},{4,3},{5,6},{6,5},{7,0},{8,15},{9,10},{10,... | collective-permute-start | bytes 196616 | tf_op jit(solution)/shard_map/ppermute | solution.py:505
  14.1 0.1 shard_map.94
  14.3 0.0 collective-permute-start.2
  14.3 1.6 %collective-permute-start.3 = (bf16[32,384]{1,0:T(8,128)(2,1)S(1)}, bf16[32,384]{1,0:T(8,128)(2,1)S(1)}, u32[]{:S(2)}, u32[]{:S(2)}) collective-permute-start(bf16[32,384]{1,0:T(8,128)(2,1)S(1)} %get-tuple-element.30), channel_id=1, source_target_pairs={{0,8},{8,0},{16,24},{24,16},{1,9},{9,1},{17,25},{25,17},{2,10},{10... | collective-permute-start | bytes 73736 | tf_op jit(solution)/shard_map/ppermute | solution.py:507
  15.9 0.0 copy-done.1
  15.9 0.0 copy-done.2
  15.9 1.6 %shard_map.95 = (bf16[512,1536]{1,0:T(8,128)(2,1)S(1)}, bf16[2,400,512]{2,1,0:T(8,128)(2,1)S(1)}, bf16[512,256]{1,0:T(8,128)(2,1)S(1)}, f32[512,128]{1,0:T(8,128)S(1)}, bf16[2,32,512]{2,1,0:T(8,128)(2,1)S(1)}) custom-call(bf16[32,2048]{1,0:T(8,128)(2,1)S(1)} %get-tuple-element.22.red_ref, bf16[32,128]{1,0:T(8,128)(2,1)S(1)} %get-tuple-element.26.edge_ref, ...), custom_call_target="tpu_custom_call" | custom-call | tf_op jit(solution)/shard_map/pallas_call | solution.py:512
  17.5 0.2 collective-permute-done.2.row_b_ref
  17.7 0.0 collective-permute-done.3.row_a_ref
  17.7 0.6 %shard_map.96.border_ref = bf16[512,512]{1,0:T(8,128)(2,1)S(1)} custom-call(bf16[32,384]{1,0:T(8,128)(2,1)S(1)} %collective-permute-done.2.row_b_ref, bf16[32,384]{1,0:T(8,128)(2,1)S(1)} %collective-permute-done.3.row_a_ref, bf16[256,400]{1,0:T(8,128)(2,1)S(1)} %get-tuple-element.27.weights_ref, bf16[2,400,512]{2,1,0:T(8,128)(2,1)S(1)} %get-tuple-element.31.own_stack_ref), custom_call_target="tpu_custom_call" | custom-call | tf_op jit(solution)/shard_map/pallas_call | solution.py:526
  18.4 0.0 collective-permute-done.4.core_a_ref
  18.4 0.0 collective-permute-done.5.core_b_ref
  18.4 1.5 %shard_map.97 = bf16[64,16,128]{2,1,0:T(8,128)(2,1)} custom-call(bf16[512,1536]{1,0:T(8,128)(2,1)S(1)} %get-tuple-element.28.inner_ref, bf16[512,512]{1,0:T(8,128)(2,1)S(1)} %shard_map.96.border_ref, bf16[2,32,512]{2,1,0:T(8,128)(2,1)S(1)} %collective-permute-done.4.core_a_ref, bf16[2,32,512]{2,1,0:T(8,128)(2,1)S(1)} %collective-permute-done.5.core_b_ref, ...), custom_call_target="tpu_custom_call" | custom-call | tf_op jit(solution)/shard_map/pallas_call | solution.py:535
Async XLA Ops:
  1.5 9.7 %copy-start = (bf16[112,32,512]{2,1,0:T(8,128)(2,1)S(1)}, bf16[112,32,512]{2,1,0:T(8,128)(2,1)}, u32[]{:S(2)}) copy-start(bf16[112,32,512]{2,1,0:T(8,128)(2,1)} %bank_ref.3) | copy-start | bytes 11010052
  1.5 7.7 %collective-permute-start = (bf16[32,128]{1,0:T(8,128)(2,1)S(1)}, bf16[32,128]{1,0:T(8,128)(2,1)S(1)}, u32[]{:S(2)}, u32[]{:S(2)}) collective-permute-start(bf16[32,128]{1,0:T(8,128)(2,1)S(1)} %get-tuple-element.23), channel_id=1, source_target_pairs={{0,7},{1,2},{2,1},{3,4},{4,3},{5,6},{6,5},{7,0},{8,15},{9,10},{10,... | collective-permute-start | bytes 24584 | tf_op jit(solution)/shard_map/ppermute | solution.py:474
  7.5 8.4 %copy-start.1 = (bf16[64,32]{0,1:T(8,128)(2,1)S(1)}, bf16[64,32]{0,1:T(8,128)(2,1)}, u32[]{:S(2)}) copy-start(bf16[64,32]{0,1:T(8,128)(2,1)} %param.16) | copy-start | bytes 12292
  7.5 8.4 %copy-start.2 = (f32[64]{0:T(128)S(1)}, f32[64]{0:T(128)}, u32[]{:S(2)}) copy-start(f32[64]{0:T(128)} %param.17) | copy-start | bytes 772
  7.5 3.7 %collective-permute-start.1 = (bf16[32,128]{1,0:T(8,128)(2,1)S(1)}, bf16[32,128]{1,0:T(8,128)(2,1)S(1)}, u32[]{:S(2)}, u32[]{:S(2)}) collective-permute-start(bf16[32,128]{1,0:T(8,128)(2,1)S(1)} %get-tuple-element.21.refs_7_), channel_id=1, source_target_pairs={{0,1},{1,0},{2,3},{3,2},{4,5},{5,4},{6,7},{7,6},{8,9},{9,8},{10,11... | collective-permute-start | bytes 24584 | tf_op jit(solution)/shard_map/ppermute | solution.py:475
  11.3 7.1 %collective-permute-start.4 = (bf16[2,32,512]{2,1,0:T(8,128)(2,1)S(1)}, bf16[2,32,512]{2,1,0:T(8,128)(2,1)S(1)}, u32[]{:S(2)}, u32[]{:S(2)}) collective-permute-start(bf16[2,32,512]{2,1,0:T(8,128)(2,1)S(1)} %get-tuple-element.32), channel_id=1, source_target_pairs={{0,1},{1,0},{2,3},{3,2},{4,5},{5,4},{6,7},{7,6},{8,9},{9,8},{10,11... | collective-permute-start | bytes 196616 | tf_op jit(solution)/shard_map/ppermute | solution.py:506
  11.4 7.0 %collective-permute-start.5 = (bf16[2,32,512]{2,1,0:T(8,128)(2,1)S(1)}, bf16[2,32,512]{2,1,0:T(8,128)(2,1)S(1)}, u32[]{:S(2)}, u32[]{:S(2)}) collective-permute-start(bf16[2,32,512]{2,1,0:T(8,128)(2,1)S(1)} %get-tuple-element.25.core_ref), channel_id=1, source_target_pairs={{0,7},{1,2},{2,1},{3,4},{4,3},{5,6},{6,5},{7,0},{8,15},{9,10},{10,... | collective-permute-start | bytes 196616 | tf_op jit(solution)/shard_map/ppermute | solution.py:505
  14.3 3.4 %collective-permute-start.2 = (bf16[32,384]{1,0:T(8,128)(2,1)S(1)}, bf16[32,384]{1,0:T(8,128)(2,1)S(1)}, u32[]{:S(2)}, u32[]{:S(2)}) collective-permute-start(bf16[32,384]{1,0:T(8,128)(2,1)S(1)} %get-tuple-element.29), channel_id=1, source_target_pairs={{0,24},{8,16},{16,8},{24,0},{1,25},{9,17},{17,9},{25,1},{2,26},{10... | collective-permute-start | bytes 73736 | tf_op jit(solution)/shard_map/ppermute | solution.py:508
  14.3 3.4 %collective-permute-start.3 = (bf16[32,384]{1,0:T(8,128)(2,1)S(1)}, bf16[32,384]{1,0:T(8,128)(2,1)S(1)}, u32[]{:S(2)}, u32[]{:S(2)}) collective-permute-start(bf16[32,384]{1,0:T(8,128)(2,1)S(1)} %get-tuple-element.30), channel_id=1, source_target_pairs={{0,8},{8,0},{16,24},{24,16},{1,9},{9,1},{17,25},{25,17},{2,10},{10... | collective-permute-start | bytes 73736 | tf_op jit(solution)/shard_map/ppermute | solution.py:507

commit v17 on v16

--- a/solution.py
+++ b/solution.py
@@ -14,7 +14,7 @@
 EDGE = 2 * REACH
 GROUP = 8
 STEP = 4
-OUT_COPIES = 4
+OUT_COPIES = 2
 IN_COPIES = 1
 F32 = jnp.float32
 BF16 = jnp.bfloat16

time: 20.1 us -> 20.1 us (level)
  no operation moved by 1% of the time
where the time goes in v17:
time: 20.1 us; the launch traced here: 20 us
  starting transfers between devices  10.5 us (52%)
  Pallas kernels  6.99 us (35%)
  waiting for transfers between devices  2.38 us (12%)
    ppermute x1, starting transfers between devices, on_device(): got_b = lax.ppermute(pay_b, 'lon', lon_second)  6.04 us
    ppermute x1, starting transfers between devices, on_device(): core_b = lax.ppermute(core_b, 'lon', lon_second)  2.76 us
    ppermute x1, waiting for transfers between devices, on_device(): got_a = lax.ppermute(pay_a, 'lon', lon_first)  2.02 us
    ppermute x1, starting transfers between devices, on_device(): row_a = lax.ppermute(row_a, 'lat', lat_first)  1.63 us
    pallas_call x1, Pallas kernels, on_device(): pl.pallas_call(functools.partial(inner_kernel, lat_len), out_shape=(jax.S...  1.6 us
    pallas_call x1, Pallas kernels, on_device(): pl.pallas_call(mix_kernel, out_shape=jax.ShapeDtypeStruct(out_shape, BF16...  1.54 us
    pallas_call x1, Pallas kernels, on_device(): pl.pallas_call(functools.partial(prepare_kernel, lon_count, lat_len), out...  1.5 us
    pallas_call x1, Pallas kernels, on_device(): pl.pallas_call(functools.partial(edge_kernel, lon_count, held), out_shape...  1.45 us
  transfers between devices with their start and end apart: 6, of which 3 were waited for; matrix products, arithmetic and copies ran while one was open for 0% of the time, Pallas kernels for 19%

profile of v17, /device:TPU:0, one launch (start us, length us, event | category | flops | bytes accessed | tf_op | source)
XLA Modules:
  0.0 20.0 jit_solution(14391909894093591273)
XLA Ops:
  0.0 1.4 %shard_map.91 = (bf16[32,128]{1,0:T(8,128)(2,1)S(1)}, bf16[32,128]{1,0:T(8,128)(2,1)S(1)}) custom-call(s32[1,1,6]{2,1,0:T(1,128)} %refs_0_.3, s32[7,128]{1,0:T(8,128)} %bitcast.5, bf16[64,16,128]{2,1,0:T(8,128)(2,1)} %refs_2_.3, bf16[32,64]{1,0:T(8,128)(2,1)} %refs_3_.3), custom_call_target="tpu_custom_call" | custom-call | flops 2000000000 | bytes 4000000 | tf_op jit(solution)/shard_map/pallas_call | solution.py:459
  1.5 0.0 copy-start
  1.5 6.0 %collective-permute-start = (bf16[32,128]{1,0:T(8,128)(2,1)S(1)}, bf16[32,128]{1,0:T(8,128)(2,1)S(1)}, u32[]{:S(2)}, u32[]{:S(2)}) collective-permute-start(bf16[32,128]{1,0:T(8,128)(2,1)S(1)} %get-tuple-element.23), channel_id=1, source_target_pairs={{0,7},{1,2},{2,1},{3,4},{4,3},{5,6},{6,5},{7,0},{8,15},{9,10},{10,... | collective-permute-start | bytes 24584 | tf_op jit(solution)/shard_map/ppermute | solution.py:474
  7.5 0.0 copy-start.1
  7.5 0.0 copy-start.2
  7.5 0.0 collective-permute-start.1
  7.5 1.5 %shard_map.92 = (bf16[32,2048]{1,0:T(8,128)(2,1)S(1)}, s32[1,128]{1,0:T(1,128)S(1)}, s32[16,128]{1,0:T(8,128)S(1)}, bf16[256,400]{1,0:T(8,128)(2,1)S(1)}) custom-call(s32[1,1,6]{2,1,0:T(1,128)} %refs_0_.3, s32[896]{0:T(1024)} %refs_1_.1, bf16[64,16,128]{2,1,0:T(8,128)(2,1)} %refs_2_.3, bf16[32,64]{1,0:T(8,128)(2,1)} %refs_3_.3, ...), custom_call_target="tpu_custom_call" | custom-call | flops 100000 | bytes 100000 | tf_op jit(solution)/shard_map/pallas_call | solution.py:476
  9.0 0.1 collective-permute-done.got_b_ref
  9.1 2.0 %collective-permute-done.1.got_a_ref = bf16[32,128]{1,0:T(8,128)(2,1)S(1)} collective-permute-done((bf16[32,128]{1,0:T(8,128)(2,1)S(1)}, bf16[32,128]{1,0:T(8,128)(2,1)S(1)}, u32[]{:S(2)}, u32[]{:S(2)}) %collective-permute-start.1) | collective-permute-done | bytes 8224 | tf_op jit(solution)/shard_map/ppermute | solution.py:475
  11.2 0.0 copy-done
  11.2 0.1 shard_map.93
  11.3 0.1 collective-permute-start.4
  11.4 2.8 %collective-permute-start.5 = (bf16[2,32,512]{2,1,0:T(8,128)(2,1)S(1)}, bf16[2,32,512]{2,1,0:T(8,128)(2,1)S(1)}, u32[]{:S(2)}, u32[]{:S(2)}) collective-permute-start(bf16[2,32,512]{2,1,0:T(8,128)(2,1)S(1)} %get-tuple-element.25.core_ref), channel_id=1, source_target_pairs={{0,7},{1,2},{2,1},{3,4},{4,3},{5,6},{6,5},{7,0},{8,15},{9,10},{10,... | collective-permute-start | bytes 196616 | tf_op jit(solution)/shard_map/ppermute | solution.py:505
  14.1 0.1 shard_map.94
  14.3 0.0 collective-permute-start.2
  14.3 1.6 %collective-permute-start.3 = (bf16[32,384]{1,0:T(8,128)(2,1)S(1)}, bf16[32,384]{1,0:T(8,128)(2,1)S(1)}, u32[]{:S(2)}, u32[]{:S(2)}) collective-permute-start(bf16[32,384]{1,0:T(8,128)(2,1)S(1)} %get-tuple-element.30), channel_id=1, source_target_pairs={{0,8},{8,0},{16,24},{24,16},{1,9},{9,1},{17,25},{25,17},{2,10},{10... | collective-permute-start | bytes 73736 | tf_op jit(solution)/shard_map/ppermute | solution.py:507
  15.9 0.0 copy-done.1
  15.9 0.0 copy-done.2
  15.9 1.6 %shard_map.95 = (bf16[512,1536]{1,0:T(8,128)(2,1)S(1)}, bf16[2,400,512]{2,1,0:T(8,128)(2,1)S(1)}, bf16[512,256]{1,0:T(8,128)(2,1)S(1)}, f32[512,128]{1,0:T(8,128)S(1)}, bf16[2,32,512]{2,1,0:T(8,128)(2,1)S(1)}) custom-call(bf16[32,2048]{1,0:T(8,128)(2,1)S(1)} %get-tuple-element.22.red_ref, bf16[32,128]{1,0:T(8,128)(2,1)S(1)} %get-tuple-element.26.edge_ref, ...), custom_call_target="tpu_custom_call" | custom-call | tf_op jit(solution)/shard_map/pallas_call | solution.py:512
  17.5 0.2 %collective-permute-done.2.row_b_ref = bf16[32,384]{1,0:T(8,128)(2,1)S(1)} collective-permute-done((bf16[32,384]{1,0:T(8,128)(2,1)S(1)}, bf16[32,384]{1,0:T(8,128)(2,1)S(1)}, u32[]{:S(2)}, u32[]{:S(2)}) %collective-permute-start.2) | collective-permute-done | bytes 24608 | tf_op jit(solution)/shard_map/ppermute | solution.py:508
  17.7 0.0 collective-permute-done.3.row_a_ref
  17.7 0.6 %shard_map.96.border_ref = bf16[512,512]{1,0:T(8,128)(2,1)S(1)} custom-call(bf16[32,384]{1,0:T(8,128)(2,1)S(1)} %collective-permute-done.2.row_b_ref, bf16[32,384]{1,0:T(8,128)(2,1)S(1)} %collective-permute-done.3.row_a_ref, bf16[256,400]{1,0:T(8,128)(2,1)S(1)} %get-tuple-element.27.weights_ref, bf16[2,400,512]{2,1,0:T(8,128)(2,1)S(1)} %get-tuple-element.31.own_stack_ref), custom_call_target="tpu_custom_call" | custom-call | tf_op jit(solution)/shard_map/pallas_call | solution.py:526
  18.4 0.0 collective-permute-done.4.core_a_ref
  18.4 0.0 collective-permute-done.5.core_b_ref
  18.4 1.5 %shard_map.97 = bf16[64,16,128]{2,1,0:T(8,128)(2,1)} custom-call(bf16[512,1536]{1,0:T(8,128)(2,1)S(1)} %get-tuple-element.28.inner_ref, bf16[512,512]{1,0:T(8,128)(2,1)S(1)} %shard_map.96.border_ref, bf16[2,32,512]{2,1,0:T(8,128)(2,1)S(1)} %collective-permute-done.4.core_a_ref, bf16[2,32,512]{2,1,0:T(8,128)(2,1)S(1)} %collective-permute-done.5.core_b_ref, ...), custom_call_target="tpu_custom_call" | custom-call | tf_op jit(solution)/shard_map/pallas_call | solution.py:535
Async XLA Ops:
  1.5 9.7 %copy-start = (bf16[112,32,512]{2,1,0:T(8,128)(2,1)S(1)}, bf16[112,32,512]{2,1,0:T(8,128)(2,1)}, u32[]{:S(2)}) copy-start(bf16[112,32,512]{2,1,0:T(8,128)(2,1)} %bank_ref.3) | copy-start | bytes 11010052
  1.5 7.7 %collective-permute-start = (bf16[32,128]{1,0:T(8,128)(2,1)S(1)}, bf16[32,128]{1,0:T(8,128)(2,1)S(1)}, u32[]{:S(2)}, u32[]{:S(2)}) collective-permute-start(bf16[32,128]{1,0:T(8,128)(2,1)S(1)} %get-tuple-element.23), channel_id=1, source_target_pairs={{0,7},{1,2},{2,1},{3,4},{4,3},{5,6},{6,5},{7,0},{8,15},{9,10},{10,... | collective-permute-start | bytes 24584 | tf_op jit(solution)/shard_map/ppermute | solution.py:474
  7.5 8.4 %copy-start.1 = (bf16[64,32]{0,1:T(8,128)(2,1)S(1)}, bf16[64,32]{0,1:T(8,128)(2,1)}, u32[]{:S(2)}) copy-start(bf16[64,32]{0,1:T(8,128)(2,1)} %param.16) | copy-start | bytes 12292
  7.5 8.4 %copy-start.2 = (f32[64]{0:T(128)S(1)}, f32[64]{0:T(128)}, u32[]{:S(2)}) copy-start(f32[64]{0:T(128)} %param.17) | copy-start | bytes 772
  7.5 3.7 %collective-permute-start.1 = (bf16[32,128]{1,0:T(8,128)(2,1)S(1)}, bf16[32,128]{1,0:T(8,128)(2,1)S(1)}, u32[]{:S(2)}, u32[]{:S(2)}) collective-permute-start(bf16[32,128]{1,0:T(8,128)(2,1)S(1)} %get-tuple-element.21.refs_7_), channel_id=1, source_target_pairs={{0,1},{1,0},{2,3},{3,2},{4,5},{5,4},{6,7},{7,6},{8,9},{9,8},{10,11... | collective-permute-start | bytes 24584 | tf_op jit(solution)/shard_map/ppermute | solution.py:475
  11.3 7.1 %collective-permute-start.4 = (bf16[2,32,512]{2,1,0:T(8,128)(2,1)S(1)}, bf16[2,32,512]{2,1,0:T(8,128)(2,1)S(1)}, u32[]{:S(2)}, u32[]{:S(2)}) collective-permute-start(bf16[2,32,512]{2,1,0:T(8,128)(2,1)S(1)} %get-tuple-element.32), channel_id=1, source_target_pairs={{0,1},{1,0},{2,3},{3,2},{4,5},{5,4},{6,7},{7,6},{8,9},{9,8},{10,11... | collective-permute-start | bytes 196616 | tf_op jit(solution)/shard_map/ppermute | solution.py:506
  11.4 7.0 %collective-permute-start.5 = (bf16[2,32,512]{2,1,0:T(8,128)(2,1)S(1)}, bf16[2,32,512]{2,1,0:T(8,128)(2,1)S(1)}, u32[]{:S(2)}, u32[]{:S(2)}) collective-permute-start(bf16[2,32,512]{2,1,0:T(8,128)(2,1)S(1)} %get-tuple-element.25.core_ref), channel_id=1, source_target_pairs={{0,7},{1,2},{2,1},{3,4},{4,3},{5,6},{6,5},{7,0},{8,15},{9,10},{10,... | collective-permute-start | bytes 196616 | tf_op jit(solution)/shard_map/ppermute | solution.py:505
  14.3 3.4 %collective-permute-start.2 = (bf16[32,384]{1,0:T(8,128)(2,1)S(1)}, bf16[32,384]{1,0:T(8,128)(2,1)S(1)}, u32[]{:S(2)}, u32[]{:S(2)}) collective-permute-start(bf16[32,384]{1,0:T(8,128)(2,1)S(1)} %get-tuple-element.29), channel_id=1, source_target_pairs={{0,24},{8,16},{16,8},{24,0},{1,25},{9,17},{17,9},{25,1},{2,26},{10... | collective-permute-start | bytes 73736 | tf_op jit(solution)/shard_map/ppermute | solution.py:508
  14.3 3.4 %collective-permute-start.3 = (bf16[32,384]{1,0:T(8,128)(2,1)S(1)}, bf16[32,384]{1,0:T(8,128)(2,1)S(1)}, u32[]{:S(2)}, u32[]{:S(2)}) collective-permute-start(bf16[32,384]{1,0:T(8,128)(2,1)S(1)} %get-tuple-element.30), channel_id=1, source_target_pairs={{0,8},{8,0},{16,24},{24,16},{1,9},{9,1},{17,25},{25,17},{2,10},{10... | collective-permute-start | bytes 73736 | tf_op jit(solution)/shard_map/ppermute | solution.py:507
